TPU v7x, 128 devices: a whole 4x4x4 slice. The times are simulated.
128 devices in a mesh: fsdp: 32 (over x, y, core), grp: 4 (over z).
Axes of the slice: x: 4, y: 4, z: 4, core: 2. Of those that a mesh axis runs over, the one named last changes fastest.
Arguments:
- q_values: bfloat16 [2048, 65536], P('fsdp', 'grp'), may hold values from -6 to 6
- scales: bfloat16 [2048, 512], P('fsdp', 'grp'), may hold values from 0.5 to 18
- block_slots: int32 [4, 32], P('grp'), may hold values from 0 to 31, each once within a row
- left_root: float32 [4, 32, 1024, 1024], P('grp', 'fsdp'), may hold values from -1 to 3
- right_root: float32 [4, 32, 1024, 1024], P('grp', 'fsdp'), may hold values from -1 to 3
- second_moment: float32 [4, 32, 1024, 1024], P('grp', 'fsdp'), may hold values from 0.02 to 0.5
Outputs:
- update: bfloat16 [2048, 65536], P('fsdp', 'grp')
- new_moment: float32 [4, 32, 1024, 1024], P('grp', 'fsdp')
All inputs are finite; a program needn't handle non-finite values.
Results may differ from a plain program's by a relative error of at most 0.0004.
Values may be sent and summed in bfloat16 or wider, within the bound.
No kernel may reach another device: no remote copies, remote signals or barrier semaphores. Data moves between devices by JAX's collectives and lax.ppermute only.
A program may use at most 128 MiB of HBM per device.

v0:
```python
import jax
import jax.numpy as jnp
from jax import lax
from jax.sharding import PartitionSpec as P


def precondition(held, left, right, moment):
    precond = jnp.matmul(
        jnp.matmul(left, held, precision=lax.Precision.HIGHEST),
        right,
        precision=lax.Precision.HIGHEST,
    )
    fresh = 0.9 * moment + 0.1 * held * held
    adam = held / (jnp.sqrt(fresh) + 1e-08)
    ratio = jnp.sqrt(jnp.sum(adam * adam)) / jnp.sqrt(jnp.sum(precond * precond) + 1e-12)
    return ((precond * ratio).astype(jnp.bfloat16), fresh)


def to_pieces(field, columns, wanted):
    rowdev = field.shape[0]
    tiles = field.reshape(rowdev, columns, field.shape[1] // columns).transpose(1, 0, 2)
    return jnp.take(tiles, wanted, axis=0)


def on_device(q_values, scales, block_slots, left_root, right_root, second_moment):
    count_fsdp = lax.axis_size("fsdp")
    index_fsdp = lax.axis_index("fsdp")
    rowdev = q_values.shape[0]
    width = left_root.shape[-1]
    owned = left_root.shape[1]
    columns = q_values.shape[1] // width
    group = width // (scales.shape[1] // columns)
    band_devs = width // rowdev
    my_band = index_fsdp // band_devs
    slots = block_slots[0]
    by_owner = slots.reshape(count_fsdp, owned)
    wanted = by_owner % columns
    mine = lax.dynamic_index_in_dim(by_owner, index_fsdp, 0, keepdims=False)
    mine_band = mine // columns
    dequant = q_values.astype(jnp.float32) * jnp.repeat(scales.astype(jnp.float32), group, axis=1)
    arrived = lax.all_to_all(
        to_pieces(dequant, columns, wanted), "fsdp", split_axis=0, concat_axis=0, tiled=True
    )
    starts = mine_band * band_devs
    gathered = jax.vmap(lambda part, start: lax.dynamic_slice_in_dim(part, start, band_devs, 0))(
        arrived.transpose(1, 0, 2, 3), starts
    )
    held_raw = gathered.reshape(owned, width, width)
    total = lax.psum(jnp.sum(held_raw * held_raw), ("fsdp", "grp"))
    total_rows = rowdev * count_fsdp
    total_cols = q_values.shape[1] * lax.axis_size("grp")
    clip = jnp.minimum(1.0, 0.5 * jnp.sqrt(jnp.float32(total_rows * total_cols)) / jnp.sqrt(total))
    held = held_raw * clip
    grafted, fresh = jax.vmap(precondition)(held, left_root[0], right_root[0], second_moment[0])
    inverse = jnp.argsort(slots)
    outgoing = grafted.reshape(owned, band_devs, rowdev, width).transpose(1, 0, 2, 3)
    outgoing = jnp.tile(outgoing, (count_fsdp // band_devs, 1, 1, 1))
    returned = lax.all_to_all(outgoing, "fsdp", split_axis=0, concat_axis=0, tiled=True)
    picks = lax.dynamic_slice_in_dim(inverse, my_band * columns, columns)
    placed = jnp.take(returned.reshape(count_fsdp * owned, rowdev, width), picks, axis=0)
    update = placed.transpose(1, 0, 2).reshape(rowdev, columns * width)
    return (update, fresh[None])


def solution(mesh):
    in_specs = (
        P("fsdp", "grp"),
        P("fsdp", "grp"),
        P("grp", None),
        P("grp", "fsdp", None, None),
        P("grp", "fsdp", None, None),
        P("grp", "fsdp", None, None),
    )
    out_specs = (P("fsdp", "grp"), P("grp", "fsdp", None, None))
    return jax.shard_map(
        on_device, mesh=mesh, in_specs=in_specs, out_specs=out_specs, check_vma=False
    )
```

profile of v0, /device:TPU:1, one launch (start us, length us, event | category | flops | bytes accessed | tf_op | source)
XLA Modules:
  0.0 350.4 jit_solution(14025820953970829547)
XLA Ops:
  0.6 0.8 fusion.8
  1.5 0.7 compare_and_fusion
  2.1 1.9 broadcast_in_dim.32
  4.0 2.6 bitcast_multiply_fusion
  6.6 2.5 copy.18
  9.2 6.5 %gather_fusion = f32[32,64,1024]{2,1,0:T(8,128)} fusion(f32[16,64,1024]{2,1,0:T(8,128)} %bitcast.43, s32[1024]{0:T(1024)S(1)} %pad_clamp_fusion.1), kind=kCustom, calls=%fused_computation | custom fusion | bytes 16777344 | tf_op jit(solution)/shard_map/jit(_take)/gather | solution.py:22
  15.7 8.7 %fusion = f32[32,1,64,1024]{3,2,1,0:T(8,128)} fusion(f32[32,64,1024]{2,1,0:T(8,128)} %gather_fusion, pred[32]{0:T(512)(128)(4,1)S(1)} %compare_and_fusion), kind=kLoop, calls=%fused_computation.3 | loop fusion | flops 2097152 | bytes 16777248 | tf_op jit(solution)/shard_map/jit(_take)/select_n | solution.py:22
  24.3 8.8 %all-to-all-start = ((f32[32,1,64,1024]{3,2,1,0:T(8,128)}), f32[32,1,64,1024]{3,2,1,0:T(8,128)}, u32[]{:S(2)}, u32[]{:S(2)}) async-start(f32[32,1,64,1024]{3,2,1,0:T(8,128)} %fusion), calls=%async_computation | async-start | bytes 16777216 | tf_op jit(solution)/shard_map/all_to_all | solution.py:41
  33.1 0.6 constant_dynamic-slice_fusion
  36.3 105.3 %all-to-all-done = f32[32,1,64,1024]{3,2,1,0:T(8,128)} async-done(((f32[32,1,64,1024]{3,2,1,0:T(8,128)}), f32[32,1,64,1024]{3,2,1,0:T(8,128)}, u32[]{:S(2)}, u32[]{:S(2)}) %all-to-all-start) | async-done | bytes 8388640 | tf_op jit(solution)/shard_map/all_to_all | solution.py:41
  141.6 3.9 %multiply_reduce_fusion = f32[]{:T(128)} fusion(f32[32,1,64,1024]{3,2,1,0:T(8,128)} %all-to-all-done, s32[]{:T(128)} %bitcast.7), kind=kLoop, calls=%fused_computation.12 | loop fusion | flops 2097151 | bytes 4194312 | tf_op jit(solution)/shard_map/reduce_sum | solution.py:49
  145.5 80.3 %psum.7 = f32[]{:T(128)} all-reduce(f32[]{:T(128)} %multiply_reduce_fusion), channel_id=1, replica_groups=mesh['fsdp'=32,'grp'=4] {'fsdp','grp'}, use_global_device_ids=true, to_apply=%region_2.3 | all-reduce | flops 1 | bytes 8 | tf_op jit(solution)/shard_map/psum | solution.py:49
  226.5 2.8 dynamic-slice_multiply_fusion
  229.3 0.6 copy-done.1
  229.9 4.8 %multiply_reduce_fusion.2 = (f32[]{:T(128)}, f32[1,1,1024,1024]{3,2,1,0:T(8,128)}) fusion(f32[1,1,1024,1024]{3,2,1,0:T(8,128)S(1)} %bitcast.45, f32[1,1,1024,1024]{3,2,1,0:T(8,128)S(1)} %copy-done.1), kind=kLoop, calls=%fused_computation.15 | loop fusion | flops 8388607 | bytes 12582916 | tf_op jit(solution)/shard_map/vmap()/reduce_sum | solution.py:15
  235.4 30.3 %fusion.4 = f32[1024,1024]{1,0:T(8,128)S(1)} fusion(f32[1024,1024]{1,0:T(8,128)} %bitcast.46, f32[1,1,1024,1024]{3,2,1,0:T(8,128)} %param.9), kind=kOutput, calls=%fused_computation.10 | convolution fusion | flops 12884901888 | bytes 12582912 | tf_op jit(solution)/shard_map/vmap()/dot_general | solution.py:9
  265.7 15.7 %multiply_reduce_fusion.1 = (f32[]{:T(128)}, f32[1024,1024]{1,0:T(8,128)}) fusion(f32[1024,1024]{1,0:T(8,128)S(1)} %fusion.4, f32[1,1,1024,1024]{3,2,1,0:T(8,128)S(1)} %copy-done.3), kind=kOutput, calls=%fused_computation.14 | convolution fusion | flops 12886999040 | bytes 12582916 | tf_op jit(solution)/shard_map/vmap()/dot_general | solution.py:8
  282.1 2.8 multiply_convert_fusion
  284.8 2.5 tile.11
  287.3 6.2 %all-to-all-start.1 = ((bf16[32,1,64,1024]{3,2,1,0:T(8,128)(2,1)}), bf16[32,1,64,1024]{3,2,1,0:T(8,128)(2,1)}, u32[]{:S(2)}, u32[]{:S(2)}) async-start(bf16[32,1,64,1024]{3,2,1,0:T(8,128)(2,1)} %bitcast.44), calls=%async_computation.1 | async-start | bytes 8388608 | tf_op jit(solution)/shard_map/all_to_all | solution.py:58
  293.6 1.6 sort.17
  295.3 50.5 %all-to-all-done.1 = bf16[32,1,64,1024]{3,2,1,0:T(8,128)(2,1)} async-done(((bf16[32,1,64,1024]{3,2,1,0:T(8,128)(2,1)}), bf16[32,1,64,1024]{3,2,1,0:T(8,128)(2,1)}, u32[]{:S(2)}, u32[]{:S(2)}) %all-to-all-start.1) | async-done | bytes 4194336 | tf_op jit(solution)/shard_map/all_to_all | solution.py:58
  345.8 2.9 gather_fusion.1
  348.9 1.5 copy.14
  (14 shorter events, 0.4 us)
Async XLA Ops:
  0.6 3.4 copy-start.2
  24.3 8.8 %copy-start.4 = (s32[1,32]{1,0:T(1,128)S(1)}, s32[1,32]{1,0:T(1,128)}, u32[]{:S(2)}) copy-start(s32[1,32]{1,0:T(1,128)} %param.8) | copy-start | bytes 388
  24.3 117.3 %all-to-all-start = ((f32[32,1,64,1024]{3,2,1,0:T(8,128)}), f32[32,1,64,1024]{3,2,1,0:T(8,128)}, u32[]{:S(2)}, u32[]{:S(2)}) async-start(f32[32,1,64,1024]{3,2,1,0:T(8,128)} %fusion), calls=%async_computation | async-start | bytes 16777216 | tf_op jit(solution)/shard_map/all_to_all | solution.py:41
  226.5 3.5 copy-start.1
  229.3 5.4 %copy-start = (f32[16,1,64,1024]{3,2,1,0:T(8,128)}, f32[16,1,64,1024]{3,2,1,0:T(8,128)S(1)}, u32[]{:S(2)}) copy-start(f32[16,1,64,1024]{3,2,1,0:T(8,128)S(1)} %dynamic-slice_multiply_fusion) | copy-start | bytes 12582916
  235.4 30.3 %copy-start.3 = (f32[1,1,1024,1024]{3,2,1,0:T(8,128)S(1)}, f32[1,1,1024,1024]{3,2,1,0:T(8,128)}, u32[]{:S(2)}) copy-start(f32[1,1,1024,1024]{3,2,1,0:T(8,128)} %param.10) | copy-start | bytes 12582916
  287.3 58.5 %all-to-all-start.1 = ((bf16[32,1,64,1024]{3,2,1,0:T(8,128)(2,1)}), bf16[32,1,64,1024]{3,2,1,0:T(8,128)(2,1)}, u32[]{:S(2)}, u32[]{:S(2)}) async-start(bf16[32,1,64,1024]{3,2,1,0:T(8,128)(2,1)} %bitcast.44), calls=%async_computation.1 | async-start | bytes 8388608 | tf_op jit(solution)/shard_map/all_to_all | solution.py:58
where the time goes:
time: 352 us; the launch traced here: 350 us
  waiting for transfers between devices  156 us (44%)
  blocking collectives  80.3 us (23%)
  matrix products  45.9 us (13%)
  other arithmetic  28.9 us (8%)
  local copies, waits for them, and re-layouts  19 us (5%)
  starting transfers between devices  15 us (4%)
  between operations  5.49 us (2%)
    all_to_all x1, waiting for transfers between devices, on_device(): lax.all_to_all(to_pieces(dequant, columns, wanted), 'fsdp', split_axis=0,...  105 us
    psum x1, blocking collectives, on_device(): total = lax.psum(jnp.sum(held_raw * held_raw), ('fsdp', 'grp'))  80.3 us
    all_to_all x1, waiting for transfers between devices, on_device(): lax.all_to_all(outgoing, 'fsdp', split_axis=0, concat_axis=0, tiled=True)  50.5 us
    dot_general x1, matrix products, precondition(): jnp.matmul(left, held, precision=lax.Precision.HIGHEST)  30.3 us
    dot_general x1, matrix products, precondition(): jnp.matmul(jnp.matmul(left, held, precision=lax.Precision.HIGHEST), right...  15.7 us
    select_n x2, other arithmetic, to_pieces(): return jnp.take(tiles, wanted, axis=0)  9.47 us
    all_to_all x1, starting transfers between devices, on_device(): lax.all_to_all(to_pieces(dequant, columns, wanted), 'fsdp', split_axis=0,...  8.78 us
  transfers between devices with their start and end apart: 2, of which 2 were waited for; matrix products, arithmetic and copies ran while one was open for 1% of the time, Pallas kernels for 0%

commit v1 on v0

v1 whole, which is shorter than its diff:
```python
import jax
import jax.numpy as jnp
from jax import lax
from jax.experimental import pallas as pl
from jax.experimental.pallas import tpu as pltpu
from jax.sharding import PartitionSpec as P

LANES = 128
EXTRA = 16
STEPS = 4
PARTS = 8
F32 = jnp.float32
BF16 = jnp.bfloat16
HBM = pl.BlockSpec(memory_space=pltpu.HBM)
SMEM = pl.BlockSpec(memory_space=pltpu.SMEM)
PARAMS = pltpu.CompilerParams(vmem_limit_bytes=60 * 1024 * 1024)


def cost(flops, nbytes):
    return pl.CostEstimate(flops=flops, bytes_accessed=nbytes, transcendentals=0)


def pack(slots, q_values, scales, width, start, part, with_scales):
    owners = slots.shape[1]
    rows, cols = q_values.shape
    columns = cols // width
    groups = width // LANES
    here = part // LANES
    tall = here * rows + (EXTRA if with_scales else 0)
    per = owners // PARTS
    piece = cols // PARTS

    def body(slots_hbm, q_hbm, s_hbm, out_hbm, slots_ref, q_ref, s_ref, turned, out_ref, ins, outs):
        reads = [
            pltpu.make_async_copy(slots_hbm, slots_ref, ins.at[PARTS]),
            pltpu.make_async_copy(s_hbm, s_ref, ins.at[PARTS + 1]),
        ]
        for k in range(PARTS):
            at = slice(k * piece, (k + 1) * piece)
            reads.append(pltpu.make_async_copy(q_hbm.at[:, at], q_ref.at[:, at], ins.at[k]))
        for read in reads:
            read.start()
        for read in reads[:2]:
            read.wait()
        if with_scales:
            padded = jnp.concatenate([s_ref[...].astype(F32), jnp.zeros((LANES - rows, LANES), F32)], axis=0)
            turned[...] = padded.T
            pad = jnp.zeros((EXTRA - groups, LANES), F32)
            for o in range(owners):
                column = lax.rem(slots_ref[0, o], columns)
                scale = turned[pl.ds(pl.multiple_of(column * groups, groups), groups), :]
                out_ref[o, here * rows :, :] = jnp.concatenate([scale, pad], axis=0).astype(BF16)
        for read in reads[2:]:
            read.wait()
        writes = []
        for k in range(PARTS):
            for o in range(k * per, (k + 1) * per):
                column = lax.rem(slots_ref[0, o], columns)
                for j in range(here):
                    at = pl.multiple_of(column * width + start + j * LANES, LANES)
                    out_ref[o, j * rows : (j + 1) * rows, :] = q_ref[:, pl.ds(at, LANES)]
            at = slice(k * per, (k + 1) * per)
            write = pltpu.make_async_copy(out_ref.at[at], out_hbm.at[at], outs.at[k])
            write.start()
            writes.append(write)
        for write in writes:
            write.wait()

    return pl.pallas_call(
        body,
        out_shape=jax.ShapeDtypeStruct((owners, tall, LANES), BF16),
        in_specs=[HBM] * 3,
        out_specs=HBM,
        scratch_shapes=[
            pltpu.SMEM(slots.shape, jnp.int32),
            pltpu.VMEM((rows, cols), BF16),
            pltpu.VMEM(scales.shape, BF16),
            pltpu.VMEM((scales.shape[1], LANES), F32),
            pltpu.VMEM((owners, tall, LANES), BF16),
            pltpu.SemaphoreType.DMA((PARTS + 2,)),
            pltpu.SemaphoreType.DMA((PARTS,)),
        ],
        compiler_params=PARAMS,
        cost_estimate=cost(0, 2 * rows * cols + 2 * owners * tall * LANES),
        name=f"pack_{start}",
    )(slots, q_values, scales)


def square_sum(q_values, scales):
    rows, cols = q_values.shape
    groups = scales.shape[1]
    group = cols // groups

    def body(q_hbm, s_hbm, out_ref, q_ref, s_ref, sems):
        reads = [pltpu.make_async_copy(q_hbm, q_ref, sems.at[0]), pltpu.make_async_copy(s_hbm, s_ref, sems.at[1])]
        for read in reads:
            read.start()
        for read in reads:
            read.wait()
        total = jnp.zeros((rows, group), F32)
        for j in range(groups):
            grad = q_ref[:, j * group : (j + 1) * group].astype(F32) * s_ref[:, j : j + 1].astype(F32)
            total = total + grad * grad
        out_ref[...] = jnp.full((8, LANES), jnp.sum(total))

    return pl.pallas_call(
        body,
        out_shape=jax.ShapeDtypeStruct((8, LANES), F32),
        in_specs=[HBM] * 2,
        scratch_shapes=[
            pltpu.VMEM((rows, cols), BF16),
            pltpu.VMEM(scales.shape, BF16),
            pltpu.SemaphoreType.DMA((2,)),
        ],
        compiler_params=PARAMS,
        cost_estimate=cost(3 * rows * cols, 2 * rows * cols),
        name="square_sum",
    )(q_values, scales)


def split_roots(left, right):
    size = left.shape[0]
    rows = size // STEPS

    def body(l_hbm, r_hbm, l1_hbm, l2_hbm, r1_hbm, r2_hbm, full, top, low, ins, outs):
        jobs = []
        for src, high_hbm, low_hbm in ((l_hbm, l1_hbm, l2_hbm), (r_hbm, r1_hbm, r2_hbm)):
            for n in range(STEPS):
                at = pl.ds(n * rows, rows)
                jobs.append((src.at[at], high_hbm.at[at], low_hbm.at[at]))
        reads = [pltpu.make_async_copy(job[0], full.at[k], ins.at[k]) for k, job in enumerate(jobs)]
        for read in reads:
            read.start()
        writes = []
        for k, (_, high_to, low_to) in enumerate(jobs):
            reads[k].wait()
            top[k], low[k] = two(full[k])
            for h, (src, to) in enumerate(((top.at[k], high_to), (low.at[k], low_to))):
                write = pltpu.make_async_copy(src, to, outs.at[2 * k + h])
                write.start()
                writes.append(write)
        for write in writes:
            write.wait()

    jobs = 2 * STEPS
    return pl.pallas_call(
        body,
        out_shape=[jax.ShapeDtypeStruct((size, size), BF16)] * 4,
        in_specs=[HBM] * 2,
        out_specs=[HBM] * 4,
        scratch_shapes=[
            pltpu.VMEM((jobs, rows, size), F32),
            pltpu.VMEM((jobs, rows, size), BF16),
            pltpu.VMEM((jobs, rows, size), BF16),
            pltpu.SemaphoreType.DMA((jobs,)),
            pltpu.SemaphoreType.DMA((2 * jobs,)),
        ],
        compiler_params=PARAMS,
        cost_estimate=cost(4 * size * size, 16 * size * size),
        name="split_roots",
    )(left, right)


def dot(a, b):
    return jnp.dot(a, b, preferred_element_type=F32)


def two(value):
    top = value.astype(BF16)
    return top, (value - top.astype(F32)).astype(BF16)


def fold(value):
    rows, cols = value.shape
    total = value[:, :LANES]
    for j in range(1, cols // LANES):
        total = total + value[:, j * LANES : (j + 1) * LANES]
    return total.reshape(rows // 8, 8, LANES).sum(axis=0)


def everywhere(value):
    return jnp.sum(value, axis=(0, 1), keepdims=True)


def dequant(a_ref, turned, first, rows, h1, h2, at_lane):
    pieces, tall, _ = a_ref.shape
    for piece in range(pieces):
        at = slice(piece * rows, (piece + 1) * rows)
        for j in range(tall // rows):
            group = piece * EXTRA + first + j
            grad = a_ref[piece, j * rows : (j + 1) * rows, :].astype(F32) * turned[:rows, group : group + 1]
            lanes = slice(at_lane + j * LANES, at_lane + (j + 1) * LANES)
            h1[at, lanes], h2[at, lanes] = two(grad)


def products(band, arrived, l1, l2, r1, r2, rows):
    size = l1.shape[0]
    _, tall, _ = arrived.shape
    pieces = size // rows
    part = tall // rows * LANES
    block = size // STEPS

    def body(
        band_ref, a_hbm, l1_hbm, l2_hbm, r1_hbm, r2_hbm, p_hbm, h1_hbm, h2_hbm, turned,
        a_ref, l1_ref, l2_ref, r1_ref, r2_ref, h1, h2, t1, t2, p_ref, ins, outs,
    ):
        deep = pl.ds(0, part)
        sources = [a_hbm.at[pl.ds(band_ref[0] * pieces, pieces)], l1_hbm, l2_hbm, r1_hbm.at[deep], r2_hbm.at[deep]]
        targets = [a_ref, l1_ref, l2_ref, r1_ref, r2_ref]
        reads = [pltpu.make_async_copy(s, t, ins.at[k]) for k, (s, t) in enumerate(zip(sources, targets))]
        for read in reads:
            read.start()
        reads[0].wait()
        scale = a_ref[:, part // LANES * rows :, :].astype(F32).reshape(pieces * EXTRA, LANES)
        turned[...] = scale.T
        dequant(a_ref, turned, 0, rows, h1, h2, 0)
        keeps = [pltpu.make_async_copy(h1, h1_hbm, outs.at[STEPS]), pltpu.make_async_copy(h2, h2_hbm, outs.at[STEPS + 1])]
        for keep in keeps:
            keep.start()
        for read in reads[1:3]:
            read.wait()

        @pl.loop(0, part // block)
        def _(n):
            at = pl.ds(pl.multiple_of(n * block, block), block)
            half = dot(l1_ref[...], h1[:, at]) + (dot(l1_ref[...], h2[:, at]) + dot(l2_ref[...], h1[:, at]))
            t1[:, at], t2[:, at] = two(half)

        for read in reads[3:]:
            read.wait()

        def p_copy(n):
            at = pl.ds(pl.multiple_of(n * block, block), block)
            return pltpu.make_async_copy(p_ref.at[:, at], p_hbm.at[:, at], outs.at[n])

        @pl.loop(0, STEPS)
        def _(n):
            at = pl.ds(pl.multiple_of(n * block, block), block)
            p_ref[:, at] = dot(t1[...], r1_ref[:, at]) + (dot(t1[...], r2_ref[:, at]) + dot(t2[...], r1_ref[:, at]))
            p_copy(n).start()

        for n in range(STEPS):
            p_copy(n).wait()
        for keep in keeps:
            keep.wait()

    square = (size, size)
    narrow = (size, part)
    return pl.pallas_call(
        body,
        out_shape=[
            jax.ShapeDtypeStruct(square, F32),
            jax.ShapeDtypeStruct(narrow, BF16),
            jax.ShapeDtypeStruct(narrow, BF16),
            jax.ShapeDtypeStruct((LANES, pieces * EXTRA), F32),
        ],
        in_specs=[SMEM] + [HBM] * 5,
        out_specs=[HBM] * 3 + [pl.BlockSpec(memory_space=pltpu.VMEM)],
        scratch_shapes=[
            pltpu.VMEM((pieces, tall, LANES), BF16),
            pltpu.VMEM(square, BF16),
            pltpu.VMEM(square, BF16),
            pltpu.VMEM((part, size), BF16),
            pltpu.VMEM((part, size), BF16),
            pltpu.VMEM(narrow, BF16),
            pltpu.VMEM(narrow, BF16),
            pltpu.VMEM(narrow, BF16),
            pltpu.VMEM(narrow, BF16),
            pltpu.VMEM(square, F32),
            pltpu.SemaphoreType.DMA((5,)),
            pltpu.SemaphoreType.DMA((STEPS + 2,)),
        ],
        compiler_params=PARAMS,
        cost_estimate=cost(12 * size * size * part, 20 * size * size),
        name="products",
    )(band, arrived, l1, l2, r1, r2)


def graft(band, clip, arrived, turned, l1, l2, r1, r2, earlier, k1, k2, moment, owners, rows):
    size = moment.shape[0]
    pieces = size // rows
    block = size // STEPS
    done = k1.shape[1]
    part = size - done
    _, tall, _ = arrived.shape

    def body(
        band_ref, clip_ref, a_hbm, turned_ref, l1_hbm, l2_hbm, r1_hbm, r2_hbm, p_hbm, h1_hbm, h2_hbm, m_hbm,
        out_hbm, fresh_hbm,
        a_ref, l1_ref, l2_ref, r1_ref, r2_ref, p_ref, h1, h2, m_ref, out_ref, asum, psum, ins, outs,
    ):
        def cut(n):
            return pl.ds(pl.multiple_of(n * block, block), block)

        deep = pl.ds(done, part)
        old = pl.ds(0, done)
        whole = [
            (a_hbm.at[pl.ds(band_ref[0] * pieces, pieces)], a_ref),
            (r1_hbm.at[deep], r1_ref),
            (r2_hbm.at[deep], r2_ref),
        ]
        whole = [pltpu.make_async_copy(s, t, ins.at[6, k]) for k, (s, t) in enumerate(whole)]

        def reads(n):
            at = cut(n)
            pairs = (
                (l1_hbm.at[at], l1_ref.at[at]),
                (l2_hbm.at[at], l2_ref.at[at]),
                (h1_hbm.at[at], h1.at[at, old]),
                (h2_hbm.at[at], h2.at[at, old]),
                (m_hbm.at[at], m_ref.at[at]),
                (p_hbm.at[at], p_ref.at[at]),
            )
            return [pltpu.make_async_copy(s, t, ins.at[k, n]) for k, (s, t) in enumerate(pairs)]

        for read in whole:
            read.start()
        for n in range(STEPS):
            for read in reads(n):
                read.start()
        clip_now = clip_ref[0, 0]
        asum[...] = jnp.zeros_like(asum)
        psum[...] = jnp.zeros_like(psum)
        whole[0].wait()
        dequant(a_ref, turned_ref, done // LANES, rows, h1, h2, done)
        for read in whole[1:]:
            read.wait()

        def fresh_copy(n):
            return pltpu.make_async_copy(m_ref.at[cut(n)], fresh_hbm.at[cut(n)], outs.at[0, n])

        def out_copy(n):
            to = pl.ds(pl.multiple_of(band_ref[0] * size + n * block, block), block)
            return pltpu.make_async_copy(out_ref.at[cut(n)], out_hbm.at[to], outs.at[1, n])

        @pl.loop(0, STEPS)
        def _(n):
            for read in reads(n):
                read.wait()
            at = cut(n)
            new = slice(done, size)
            half = dot(l1_ref[at, :], h1[:, new]) + (dot(l1_ref[at, :], h2[:, new]) + dot(l2_ref[at, :], h1[:, new]))
            high, low = two(half)
            product = dot(high, r1_ref[...]) + (dot(high, r2_ref[...]) + dot(low, r1_ref[...]))
            product = p_ref[at, :] + product
            p_ref[at, :] = product
            psum[...] += fold(product * product)
            held = (h1[at, :].astype(F32) + h2[at, :].astype(F32)) * clip_now
            fresh = 0.9 * m_ref[at, :] + 0.1 * held * held
            m_ref[at, :] = fresh
            adam = held / (jnp.sqrt(fresh) + 1e-08)
            asum[...] += fold(adam * adam)
            fresh_copy(n).start()

        clips = jnp.full((1, 1), clip_now)
        norm = jnp.sqrt(everywhere(psum[...]) * (clips * clips) + 1e-12)
        ratio = clips * (jnp.sqrt(everywhere(asum[...])) / norm)

        @pl.loop(0, STEPS)
        def _(n):
            at = cut(n)
            out_ref[at, :] = (p_ref[at, :] * ratio).astype(BF16)
            out_copy(n).start()

        for n in range(STEPS):
            fresh_copy(n).wait()
            out_copy(n).wait()

    square = (size, size)
    return pl.pallas_call(
        body,
        out_shape=[
            jax.ShapeDtypeStruct((owners * rows, size), BF16),
            jax.ShapeDtypeStruct(square, F32),
        ],
        in_specs=[SMEM, SMEM, HBM, pl.BlockSpec(memory_space=pltpu.VMEM)] + [HBM] * 8,
        out_specs=[HBM, HBM],
        scratch_shapes=[
            pltpu.VMEM((pieces, tall, LANES), BF16),
            pltpu.VMEM(square, BF16),
            pltpu.VMEM(square, BF16),
            pltpu.VMEM((part, size), BF16),
            pltpu.VMEM((part, size), BF16),
            pltpu.VMEM(square, F32),
            pltpu.VMEM(square, BF16),
            pltpu.VMEM(square, BF16),
            pltpu.VMEM(square, F32),
            pltpu.VMEM(square, BF16),
            pltpu.VMEM((8, LANES), F32),
            pltpu.VMEM((8, LANES), F32),
            pltpu.SemaphoreType.DMA((7, STEPS)),
            pltpu.SemaphoreType.DMA((2, STEPS)),
        ],
        compiler_params=PARAMS,
        cost_estimate=cost(12 * size * size * part, 24 * size * size),
        name="graft",
    )(band, clip, arrived, turned, l1, l2, r1, r2, earlier, k1, k2, moment)


def place(slots, band, returned, cols):
    owners, rows, width = returned.shape
    columns = cols // width

    def body(slots_ref, band_ref, r_hbm, out_hbm, out_ref, ins, outs):
        def each(act):
            for owner in range(owners):
                here = slots_ref[0, owner]

                @pl.when(lax.div(here, columns) == band_ref[0])
                def _():
                    act(owner, pl.ds(pl.multiple_of(lax.rem(here, columns) * width, width), width))

        def read(owner, at):
            return pltpu.make_async_copy(r_hbm.at[owner], out_ref.at[:, at], ins.at[owner])

        def write(owner, at):
            return pltpu.make_async_copy(out_ref.at[:, at], out_hbm.at[:, at], outs.at[owner])

        def pass_on(owner, at):
            read(owner, at).wait()
            write(owner, at).start()

        each(lambda owner, at: read(owner, at).start())
        each(pass_on)
        each(lambda owner, at: write(owner, at).wait())

    return pl.pallas_call(
        body,
        out_shape=jax.ShapeDtypeStruct((rows, cols), BF16),
        in_specs=[SMEM, SMEM, HBM],
        out_specs=HBM,
        scratch_shapes=[
            pltpu.VMEM((rows, cols), BF16),
            pltpu.SemaphoreType.DMA((owners,)),
            pltpu.SemaphoreType.DMA((owners,)),
        ],
        compiler_params=PARAMS,
        cost_estimate=cost(0, 4 * rows * cols),
        name="place",
    )(slots, band, returned)


def add_over(value, axis, stride, size):
    whole = lax.axis_size(axis)

    def turn(i, k):
        digit = i // stride % size
        return i + ((digit + k) % size - digit) * stride

    sent = [lax.ppermute(value, axis, [(i, turn(i, k)) for i in range(whole)]) for k in range(1, size)]
    return sum(sent, value)


def on_device(q_values, scales, block_slots, left_root, right_root, second_moment):
    count = lax.axis_size("fsdp")
    index = lax.axis_index("fsdp")
    rows, cols = q_values.shape
    width = left_root.shape[-1]
    columns = cols // width
    band_devs = width // rows
    my_band = (index // band_devs).astype(jnp.int32).reshape(1)
    slots = block_slots[0]
    mine = lax.dynamic_index_in_dim(slots, index, 0, keepdims=False)
    mine_band = (mine // columns).reshape(1)

    first = width * 3 // 4

    def exchange(value):
        return lax.all_to_all(value, "fsdp", split_axis=0, concat_axis=0, tiled=True)

    arrived = exchange(pack(block_slots, q_values, scales, width, 0, first, True))
    later = exchange(pack(block_slots, q_values, scales, width, first, width - first, False))

    total = square_sum(q_values, scales)
    for axis, stride, size in (("grp", 1, 2), ("grp", 2, 2), ("fsdp", 1, 2)):
        total = add_over(total, axis, stride, size)
    roots = split_roots(left_root[0, 0], right_root[0, 0])
    total, *roots = lax.optimization_barrier((total, *roots))
    total = add_over(total, "fsdp", 2, 4)
    product, h1, h2, turned = products(mine_band, arrived, *roots, rows)
    total, product = lax.optimization_barrier((total, product))
    total = add_over(total, "fsdp", 8, 4)[:1, :1]
    count_all = rows * count * cols * lax.axis_size("grp")
    clip = jnp.minimum(1.0, 0.5 * jnp.sqrt(F32(count_all)) / jnp.sqrt(total))

    outgoing, fresh = graft(
        mine_band, clip, later, turned, *roots, product, h1, h2, second_moment[0, 0], count, rows
    )
    outgoing = outgoing.reshape(count, rows, width)
    update = place(block_slots, my_band, exchange(outgoing), cols)
    return (update, fresh[None, None])


def solution(mesh):
    in_specs = (
        P("fsdp", "grp"),
        P("fsdp", "grp"),
        P("grp", None),
        P("grp", "fsdp", None, None),
        P("grp", "fsdp", None, None),
        P("grp", "fsdp", None, None),
    )
    out_specs = (P("fsdp", "grp"), P("grp", "fsdp", None, None))
    return jax.shard_map(
        on_device, mesh=mesh, in_specs=in_specs, out_specs=out_specs, check_vma=False
    )
```

time: 352 us -> 167 us (0.47)
  waiting for transfers between devices: 156 us -> 69.2 us
  blocking collectives: 80.3 us -> 0 us
  Pallas kernels: 0 us -> 51.3 us
  matrix products: 45.9 us -> 0 us
  other arithmetic: 28.9 us -> 0.71 us
  starting transfers between devices: 15 us -> 36.4 us
  local copies, waits for them, and re-layouts: 19 us -> 3.84 us
    all_to_all x2 -> x3, waiting for transfers between devices: 156 us -> 55.1 us  [exchange(): lax.all_to_all(value, 'fsdp', split_axis=0, concat_axis=0, tiled=True)]
    psum x1 -> x0, blocking collectives: 80.3 us -> none  [on_device(): total = lax.psum(jnp.sum(held_raw * held_raw), ('fsdp', 'grp'))]
    pallas_call x0 -> x7, Pallas kernels: none -> 51.3 us  [the longest x1 16.3 us: graft(): pl.pallas_call(body, out_shape=[jax.ShapeDtypeStruct((owners * rows, size...]
    dot_general x2 -> x0, matrix products: 45.9 us -> none  [the longest x1 30.3 us: precondition(): jnp.matmul(left, held, precision=lax.Precision.HIGHEST)]
    ppermute x0 -> x9, starting transfers between devices: none -> 14.6 us  [add_over(): lax.ppermute(value, axis, [(i, turn(i, k)) for i in range(whole)])]
    ppermute x0 -> x9, waiting for transfers between devices: none -> 14.1 us  [add_over(): lax.ppermute(value, axis, [(i, turn(i, k)) for i in range(whole)])]
    select_n x2 -> x0, other arithmetic: 9.47 us -> none  [to_pieces(): return jnp.take(tiles, wanted, axis=0)]
    gather x2 -> x0, local copies, waits for them, and re-layouts: 9.35 us -> none  [the longest x1 6.48 us: to_pieces(): return jnp.take(tiles, wanted, axis=0)]
  transfers between devices with their start and end apart: 2 -> 12, of which waited for: 2 -> 7; matrix products, arithmetic and copies ran while one was open for 1% -> 1% of each run, Pallas kernels for 0% -> 17%
where the time goes in v1:
time: 167 us; the launch traced here: 166 us
  waiting for transfers between devices  69.2 us (41%)
  Pallas kernels  51.3 us (31%)
  starting transfers between devices  36.4 us (22%)
  between operations  4.18 us (3%)
  local copies, waits for them, and re-layouts  3.84 us (2%)
    all_to_all x3, waiting for transfers between devices, exchange(): lax.all_to_all(value, 'fsdp', split_axis=0, concat_axis=0, tiled=True)  55.1 us
    all_to_all x3, starting transfers between devices, exchange(): lax.all_to_all(value, 'fsdp', split_axis=0, concat_axis=0, tiled=True)  21.8 us
    pallas_call x1, Pallas kernels, graft(): pl.pallas_call(body, out_shape=[jax.ShapeDtypeStruct((owners * rows, size...  16.3 us
    pallas_call x1, Pallas kernels, products(): pl.pallas_call(body, out_shape=[jax.ShapeDtypeStruct(square, F32), jax.Sh...  15.5 us
    ppermute x9, starting transfers between devices, add_over(): lax.ppermute(value, axis, [(i, turn(i, k)) for i in range(whole)])  14.6 us
    ppermute x9, waiting for transfers between devices, add_over(): lax.ppermute(value, axis, [(i, turn(i, k)) for i in range(whole)])  14.1 us
    pallas_call x1, Pallas kernels, split_roots(): pl.pallas_call(body, out_shape=[jax.ShapeDtypeStruct((size, size), BF16)]...  6.64 us
    pallas_call x2, Pallas kernels, pack(): pl.pallas_call(body, out_shape=jax.ShapeDtypeStruct((owners, tall, LANES)...  6.19 us
  transfers between devices with their start and end apart: 12, of which 7 were waited for; matrix products, arithmetic and copies ran while one was open for 1% of the time, Pallas kernels for 17%

profile of v1, /device:TPU:1, one launch (start us, length us, event | category | flops | bytes accessed | tf_op | source)
XLA Modules:
  0.0 165.6 jit_solution(1210946767336814578)
XLA Ops:
  0.6 3.5 %pack_0.1 = bf16[32,400,128]{2,1,0:T(8,128)(2,1)} custom-call(s32[1,32]{1,0:T(1,128)} %slots_ref.1, bf16[64,16384]{1,0:T(8,128)(2,1)} %q_hbm.5, bf16[64,128]{1,0:T(8,128)(2,1)} %s_hbm.5), custom_call_target="tpu_custom_call" | custom-call | bytes 5373952 | tf_op jit(solution)/shard_map/pack_0/pallas_call | solution.py:69
  4.1 8.6 %all-to-all-start = ((bf16[32,400,128]{2,1,0:T(8,128)(2,1)}), bf16[32,400,128]{2,1,0:T(8,128)(2,1)S(1)}, u32[]{:S(2)}, u32[]{:S(2)}) async-start(bf16[32,400,128]{2,1,0:T(8,128)(2,1)} %pack_0.1), calls=%async_computation | async-start | bytes 6553600 | tf_op jit(solution)/shard_map/all_to_all | solution.py:469
  12.7 3.1 %square_sum.1 = f32[8,128]{1,0:T(8,128)} custom-call(bf16[64,16384]{1,0:T(8,128)(2,1)} %q_hbm.5, bf16[64,128]{1,0:T(8,128)(2,1)} %s_hbm.5), custom_call_target="tpu_custom_call" | custom-call | flops 3145728 | bytes 2097152 | tf_op jit(solution)/shard_map/square_sum/pallas_call | solution.py:106
  15.9 1.7 %collective-permute-start = (f32[8,128]{1,0:T(8,128)}, f32[8,128]{1,0:T(8,128)S(1)}, u32[]{:S(2)}, u32[]{:S(2)}) collective-permute-start(f32[8,128]{1,0:T(8,128)} %square_sum.1), channel_id=1, source_target_pairs={{0,1},{1,0},{2,3},{3,2},{4,5},{5,4},{6,7},{7,6},{8,9},{9,8},{10,11... | collective-permute-start | bytes 12296 | tf_op jit(solution)/shard_map/ppermute | solution.py:450
  17.6 1.5 collective-permute-done
  19.1 0.7 add.34
  19.8 3.4 %collective-permute-start.1 = (f32[8,128]{1,0:T(8,128)S(1)}, f32[8,128]{1,0:T(8,128)S(1)}, u32[]{:S(2)}, u32[]{:S(2)}) collective-permute-start(f32[8,128]{1,0:T(8,128)S(1)} %add.34), channel_id=1, source_target_pairs={{0,2},{1,3},{2,0},{3,1},{4,6},{5,7},{6,4},{7,5},{8,10},{9,11},{10,... | collective-permute-start | bytes 12296 | tf_op jit(solution)/shard_map/ppermute | solution.py:450
  23.2 1.3 collective-permute-done.1
  24.5 1.7 %collective-permute-start.2 = (f32[8,128]{1,0:T(8,128)S(1)}, f32[8,128]{1,0:T(8,128)S(1)}, u32[]{:S(2)}, u32[]{:S(2)}) collective-permute-start(f32[8,128]{1,0:T(8,128)S(1)} %add.35), channel_id=1, source_target_pairs={{0,4},{4,0},{8,12},{12,8},{16,20},{20,16},{24,28},{28,24},{32,36},... | collective-permute-start | bytes 12296 | tf_op jit(solution)/shard_map/ppermute | solution.py:450
  26.2 6.6 %split_roots.1 = (bf16[1024,1024]{1,0:T(8,128)(2,1)}, bf16[1024,1024]{1,0:T(8,128)(2,1)}, bf16[1024,1024]{1,0:T(8,128)(2,1)}, bf16[1024,1024]{1,0:T(8,128)(2,1)}) custom-call(f32[1024,1024]{1,0:T(8,128)} %bitcast.8, f32[1024,1024]{1,0:T(8,128)} %bitcast.9), custom_call_target="tpu_custom_call" | custom-call | flops 4194304 | bytes 16777216 | tf_op jit(solution)/shard_map/split_roots/pallas_call | solution.py:146
  32.8 2.8 %collective-permute-start.5 = (f32[8,128]{1,0:T(8,128)S(1)}, f32[8,128]{1,0:T(8,128)S(1)}, u32[]{:S(2)}, u32[]{:S(2)}) collective-permute-start(f32[8,128]{1,0:T(8,128)S(1)} %add.36), channel_id=1, source_target_pairs={{0,24},{4,28},{8,0},{12,4},{16,8},{20,12},{24,16},{28,20},{32,56},... | collective-permute-start | bytes 12296 | tf_op jit(solution)/shard_map/ppermute | solution.py:450
  39.3 2.7 %pack_768.1 = bf16[32,128,128]{2,1,0:T(8,128)(2,1)} custom-call(s32[1,32]{1,0:T(1,128)} %slots_ref.1, bf16[64,16384]{1,0:T(8,128)(2,1)} %q_hbm.5, bf16[64,128]{1,0:T(8,128)(2,1)} %s_hbm.5), custom_call_target="tpu_custom_call" | custom-call | bytes 3145728 | tf_op jit(solution)/shard_map/pack_768/pallas_call | solution.py:69
  42.7 8.2 %collective-permute-done.5 = f32[8,128]{1,0:T(8,128)S(1)} collective-permute-done((f32[8,128]{1,0:T(8,128)S(1)}, f32[8,128]{1,0:T(8,128)S(1)}, u32[]{:S(2)}, u32[]{:S(2)}) %collective-permute-start.5) | collective-permute-done | bytes 4128 | tf_op jit(solution)/shard_map/ppermute | solution.py:450
  50.9 2.9 %all-to-all-done.a_hbm = bf16[32,400,128]{2,1,0:T(8,128)(2,1)S(1)} async-done(((bf16[32,400,128]{2,1,0:T(8,128)(2,1)}), bf16[32,400,128]{2,1,0:T(8,128)(2,1)S(1)}, u32[]{:S(2)}, u32[]{:S(2)}) %all-to-all-start) | async-done | bytes 3276832 | tf_op jit(solution)/shard_map/all_to_all | solution.py:469
  53.8 1.7 %copy-done.1 = bf16[32,400,128]{2,1,0:T(8,128)(2,1)} copy-done((bf16[32,400,128]{2,1,0:T(8,128)(2,1)}, bf16[32,400,128]{2,1,0:T(8,128)(2,1)S(1)}, u32[]{:S(2)}) %copy-start.1) | copy-done | bytes 3276824
  55.5 5.7 %all-to-all-start.1 = ((bf16[32,128,128]{2,1,0:T(8,128)(2,1)}), bf16[32,128,128]{2,1,0:T(8,128)(2,1)S(1)}, u32[]{:S(2)}, u32[]{:S(2)}) async-start(bf16[32,128,128]{2,1,0:T(8,128)(2,1)} %pack_768.1), calls=%async_computation.1 | async-start | bytes 2097152 | tf_op jit(solution)/shard_map/all_to_all | solution.py:469
  61.2 15.5 %products.1 = (f32[1024,1024]{1,0:T(8,128)}, bf16[1024,768]{1,0:T(8,128)(2,1)}, bf16[1024,768]{1,0:T(8,128)(2,1)}, f32[128,256]{1,0:T(8,128)}) custom-call(s32[1]{0:T(128)} %bitcast.2.band_ref, bf16[32,400,128]{2,1,0:T(8,128)(2,1)} %copy-done.1, bf16[1024,1024]{1,0:T(8,128)(2,1)} %get-tuple-element.24.l1_hbm, bf16[1024,1024]{1,0:T(8,128)(2,1)} %get-tuple-element.25.l2_hbm, ...), custom_call_target="tpu_custom_call" | custom-call | flops 9663676416 | bytes 20971520 | tf_op jit(solution)/shard_map/products/pallas_call | solution.py:249
  76.7 2.7 %collective-permute-start.8 = (f32[8,128]{1,0:T(8,128)S(1)}, f32[8,128]{1,0:T(8,128)S(1)}, u32[]{:S(2)}, u32[]{:S(2)}) collective-permute-start(f32[8,128]{1,0:T(8,128)S(1)} %add_add_fusion.1), channel_id=1, source_target_pairs={{0,96},{4,100},{8,104},{12,108},{16,112},{20,116},{24,120},{28,124... | collective-permute-start | bytes 12296 | tf_op jit(solution)/shard_map/ppermute | solution.py:450
  80.6 2.8 %collective-permute-done.7 = f32[8,128]{1,0:T(8,128)S(1)} collective-permute-done((f32[8,128]{1,0:T(8,128)S(1)}, f32[8,128]{1,0:T(8,128)S(1)}, u32[]{:S(2)}, u32[]{:S(2)}) %collective-permute-start.7) | collective-permute-done | bytes 4128 | tf_op jit(solution)/shard_map/ppermute | solution.py:450
  84.9 1.0 copy-done
  85.9 16.3 %graft.1 = (bf16[2048,1024]{1,0:T(8,128)(2,1)}, f32[1024,1024]{1,0:T(8,128)}) custom-call(s32[1]{0:T(128)} %bitcast.2.band_ref, f32[1,1]{1,0:T(1,128)S(6)} %min.3.clip_ref, bf16[32,128,128]{2,1,0:T(8,128)(2,1)} %copy-done, f32[128,256]{1,0:T(8,128)} %get-tuple-element.30.turned_ref, bf16[1024,1024]{1,0:T(8,128)(2,1)} %get-tuple-element.24.l1_hbm, ...), custom_call_target="tpu_custom_call" | custom-call | flops 3221225472 | bytes 25165824 | tf_op jit(solution)/shard_map/graft/pallas_call | solution.py:370
  102.1 7.5 %all-to-all-start.2 = ((bf16[32,64,1024]{2,1,0:T(8,128)(2,1)}), bf16[32,64,1024]{2,1,0:T(8,128)(2,1)}, u32[]{:S(2)}, u32[]{:S(2)}) async-start(bf16[32,64,1024]{2,1,0:T(8,128)(2,1)} %bitcast.10), calls=%async_computation.2 | async-start | bytes 8388608 | tf_op jit(solution)/shard_map/all_to_all | solution.py:469
  109.7 52.2 %all-to-all-done.2.r_hbm = bf16[32,64,1024]{2,1,0:T(8,128)(2,1)} async-done(((bf16[32,64,1024]{2,1,0:T(8,128)(2,1)}), bf16[32,64,1024]{2,1,0:T(8,128)(2,1)}, u32[]{:S(2)}, u32[]{:S(2)}) %all-to-all-start.2) | async-done | bytes 4194336 | tf_op jit(solution)/shard_map/all_to_all | solution.py:469
  161.9 3.5 %place.1 = bf16[64,16384]{1,0:T(8,128)(2,1)} custom-call(s32[1,32]{1,0:T(1,128)} %slots_ref.1, s32[1]{0:T(128)} %bitcast.band_ref, bf16[32,64,1024]{2,1,0:T(8,128)(2,1)} %all-to-all-done.2.r_hbm), custom_call_target="tpu_custom_call" | custom-call | bytes 4194304 | tf_op jit(solution)/shard_map/place/pallas_call | solution.py:427
  (20 shorter events, 3.7 us)
Async XLA Ops:
  4.1 49.7 %all-to-all-start = ((bf16[32,400,128]{2,1,0:T(8,128)(2,1)}), bf16[32,400,128]{2,1,0:T(8,128)(2,1)S(1)}, u32[]{:S(2)}, u32[]{:S(2)}) async-start(bf16[32,400,128]{2,1,0:T(8,128)(2,1)} %pack_0.1), calls=%async_computation | async-start | bytes 6553600 | tf_op jit(solution)/shard_map/all_to_all | solution.py:469
  15.9 3.2 %collective-permute-start = (f32[8,128]{1,0:T(8,128)}, f32[8,128]{1,0:T(8,128)S(1)}, u32[]{:S(2)}, u32[]{:S(2)}) collective-permute-start(f32[8,128]{1,0:T(8,128)} %square_sum.1), channel_id=1, source_target_pairs={{0,1},{1,0},{2,3},{3,2},{4,5},{5,4},{6,7},{7,6},{8,9},{9,8},{10,11... | collective-permute-start | bytes 12296 | tf_op jit(solution)/shard_map/ppermute | solution.py:450
  19.8 4.7 %collective-permute-start.1 = (f32[8,128]{1,0:T(8,128)S(1)}, f32[8,128]{1,0:T(8,128)S(1)}, u32[]{:S(2)}, u32[]{:S(2)}) collective-permute-start(f32[8,128]{1,0:T(8,128)S(1)} %add.34), channel_id=1, source_target_pairs={{0,2},{1,3},{2,0},{3,1},{4,6},{5,7},{6,4},{7,5},{8,10},{9,11},{10,... | collective-permute-start | bytes 12296 | tf_op jit(solution)/shard_map/ppermute | solution.py:450
  24.5 8.3 %collective-permute-start.2 = (f32[8,128]{1,0:T(8,128)S(1)}, f32[8,128]{1,0:T(8,128)S(1)}, u32[]{:S(2)}, u32[]{:S(2)}) collective-permute-start(f32[8,128]{1,0:T(8,128)S(1)} %add.35), channel_id=1, source_target_pairs={{0,4},{4,0},{8,12},{12,8},{16,20},{20,16},{24,28},{28,24},{32,36},... | collective-permute-start | bytes 12296 | tf_op jit(solution)/shard_map/ppermute | solution.py:450
  26.2 10.6 %copy-start.2 = (s32[1,32]{1,0:T(1,128)S(1)}, s32[1,32]{1,0:T(1,128)}, u32[]{:S(2)}) copy-start(s32[1,32]{1,0:T(1,128)} %slots_ref.1) | copy-start | bytes 388
  32.8 18.1 %collective-permute-start.5 = (f32[8,128]{1,0:T(8,128)S(1)}, f32[8,128]{1,0:T(8,128)S(1)}, u32[]{:S(2)}, u32[]{:S(2)}) collective-permute-start(f32[8,128]{1,0:T(8,128)S(1)} %add.36), channel_id=1, source_target_pairs={{0,24},{4,28},{8,0},{12,4},{16,8},{20,12},{24,16},{28,20},{32,56},... | collective-permute-start | bytes 12296 | tf_op jit(solution)/shard_map/ppermute | solution.py:450
  35.6 15.3 %collective-permute-start.4 = (f32[8,128]{1,0:T(8,128)S(1)}, f32[8,128]{1,0:T(8,128)S(1)}, u32[]{:S(2)}, u32[]{:S(2)}) collective-permute-start(f32[8,128]{1,0:T(8,128)S(1)} %add.36), channel_id=1, source_target_pairs={{0,16},{4,20},{8,24},{12,28},{16,0},{20,4},{24,8},{28,12},{32,48},... | collective-permute-start | bytes 12296 | tf_op jit(solution)/shard_map/ppermute | solution.py:450
  36.2 14.7 %collective-permute-start.3 = (f32[8,128]{1,0:T(8,128)S(1)}, f32[8,128]{1,0:T(8,128)S(1)}, u32[]{:S(2)}, u32[]{:S(2)}) collective-permute-start(f32[8,128]{1,0:T(8,128)S(1)} %add.36), channel_id=1, source_target_pairs={{0,8},{4,12},{8,16},{12,20},{16,24},{20,28},{24,0},{28,4},{32,40},... | collective-permute-start | bytes 12296 | tf_op jit(solution)/shard_map/ppermute | solution.py:450
  53.8 1.7 %copy-start.1 = (bf16[32,400,128]{2,1,0:T(8,128)(2,1)}, bf16[32,400,128]{2,1,0:T(8,128)(2,1)S(1)}, u32[]{:S(2)}) copy-start(bf16[32,400,128]{2,1,0:T(8,128)(2,1)S(1)} %all-to-all-done.a_hbm) | copy-start | bytes 9830404
  55.5 29.3 %all-to-all-start.1 = ((bf16[32,128,128]{2,1,0:T(8,128)(2,1)}), bf16[32,128,128]{2,1,0:T(8,128)(2,1)S(1)}, u32[]{:S(2)}, u32[]{:S(2)}) async-start(bf16[32,128,128]{2,1,0:T(8,128)(2,1)} %pack_768.1), calls=%async_computation.1 | async-start | bytes 2097152 | tf_op jit(solution)/shard_map/all_to_all | solution.py:469
  76.7 3.8 %collective-permute-start.8 = (f32[8,128]{1,0:T(8,128)S(1)}, f32[8,128]{1,0:T(8,128)S(1)}, u32[]{:S(2)}, u32[]{:S(2)}) collective-permute-start(f32[8,128]{1,0:T(8,128)S(1)} %add_add_fusion.1), channel_id=1, source_target_pairs={{0,96},{4,100},{8,104},{12,108},{16,112},{20,116},{24,120},{28,124... | collective-permute-start | bytes 12296 | tf_op jit(solution)/shard_map/ppermute | solution.py:450
  79.4 4.0 %collective-permute-start.7 = (f32[8,128]{1,0:T(8,128)S(1)}, f32[8,128]{1,0:T(8,128)S(1)}, u32[]{:S(2)}, u32[]{:S(2)}) collective-permute-start(f32[8,128]{1,0:T(8,128)S(1)} %add_add_fusion.1), channel_id=1, source_target_pairs={{0,64},{4,68},{8,72},{12,76},{16,80},{20,84},{24,88},{28,92},{32,9... | collective-permute-start | bytes 12296 | tf_op jit(solution)/shard_map/ppermute | solution.py:450
  80.0 3.7 %collective-permute-start.6 = (f32[8,128]{1,0:T(8,128)S(1)}, f32[8,128]{1,0:T(8,128)S(1)}, u32[]{:S(2)}, u32[]{:S(2)}) collective-permute-start(f32[8,128]{1,0:T(8,128)S(1)} %add_add_fusion.1), channel_id=1, source_target_pairs={{0,32},{4,36},{8,40},{12,44},{16,48},{20,52},{24,56},{28,60},{32,6... | collective-permute-start | bytes 12296 | tf_op jit(solution)/shard_map/ppermute | solution.py:450
  84.9 1.0 copy-start
  102.1 59.8 %all-to-all-start.2 = ((bf16[32,64,1024]{2,1,0:T(8,128)(2,1)}), bf16[32,64,1024]{2,1,0:T(8,128)(2,1)}, u32[]{:S(2)}, u32[]{:S(2)}) async-start(bf16[32,64,1024]{2,1,0:T(8,128)(2,1)} %bitcast.10), calls=%async_computation.2 | async-start | bytes 8388608 | tf_op jit(solution)/shard_map/all_to_all | solution.py:469

commit v2 on v0

v2 whole, which is shorter than its diff:
```python
import jax
import jax.numpy as jnp
from jax import lax
from jax.experimental import pallas as pl
from jax.experimental.pallas import tpu as pltpu
from jax.sharding import PartitionSpec as P

LANES = 128
EXTRA = 16
STEPS = 4
FINE = 32
F32 = jnp.float32
BF16 = jnp.bfloat16
HBM = pl.BlockSpec(memory_space=pltpu.HBM)
SMEM = pl.BlockSpec(memory_space=pltpu.SMEM)
VMEM = pl.BlockSpec(memory_space=pltpu.VMEM)
DMA = pltpu.SemaphoreType.DMA


def grant(mib):
    return pltpu.CompilerParams(vmem_limit_bytes=mib * 1024 * 1024)


def cost(flops, nbytes):
    return pl.CostEstimate(flops=flops, bytes_accessed=nbytes, transcendentals=0)


def dot(a, b):
    return jnp.dot(a, b, preferred_element_type=F32)


def two(value):
    top = value.astype(BF16)
    return top, (value - top.astype(F32)).astype(BF16)


def fold(value):
    rows, cols = value.shape
    total = value[:, :LANES]
    for j in range(1, cols // LANES):
        total = total + value[:, j * LANES : (j + 1) * LANES]
    return total.reshape(rows // 8, 8, LANES).sum(axis=0)


def everywhere(value):
    return jnp.sum(value, axis=(0, 1), keepdims=True)


def invert(slots_ref, inverse_ref):
    for owner in range(slots_ref.shape[1]):
        inverse_ref[slots_ref[0, owner]] = owner


def own_band(slots_ref, columns):
    return lax.div(slots_ref[0, lax.axis_index("fsdp")], columns)


def pack(slots, q_values, scales, sums_of, width, start, part):
    owners = slots.shape[1]
    rows, cols = q_values.shape
    columns = cols // width
    groups = width // LANES
    here = part // LANES
    tall = here * rows + EXTRA
    sums = EXTRA - groups

    def body(slots_hbm, q_hbm, s_hbm, *rest):
        e_hbm = rest[: len(sums_of)]
        out_hbm, slots_ref, inverse, q_ref, s_ref, e_ref, turned, out_ref, ins, outs = rest[-10:]

        def q_read(k):
            at = pl.ds(pl.multiple_of(k * width + start, LANES), part)
            return pltpu.make_async_copy(q_hbm.at[:, at], q_ref.at[k], ins.at[k])

        def write(k, band):
            at = band * columns + k
            return pltpu.make_async_copy(out_ref.at[k], out_hbm.at[inverse[at]], outs.at[at])

        reads = [
            pltpu.make_async_copy(slots_hbm, slots_ref, ins.at[columns]),
            pltpu.make_async_copy(s_hbm, s_ref, ins.at[columns + 1]),
        ]
        for k, src in enumerate(e_hbm):
            reads.append(pltpu.make_async_copy(src, e_ref.at[k], ins.at[columns + 2 + k]))
        for read in reads:
            read.start()

        @pl.loop(0, columns)
        def _(k):
            q_read(k).start()

        for read in reads:
            read.wait()
        invert(slots_ref, inverse)
        padded = jnp.concatenate([s_ref[...].astype(F32), jnp.zeros((LANES - rows, LANES), F32)], axis=0)
        turned[...] = padded.T
        head = jnp.zeros((sums, LANES), F32)
        if e_hbm:
            value = e_ref[0]
            for k in range(1, len(e_hbm)):
                value = value + e_ref[k]
            high = value.astype(BF16)
            mid, low = two(value - high.astype(F32))
            row = lax.broadcasted_iota(jnp.int32, head.shape, 0)
            for k, term in enumerate((high, mid, low)):
                head = jnp.where(row == k, jnp.broadcast_to(term[:1].astype(F32), head.shape), head)

        @pl.loop(0, columns)
        def _(k):
            scale = turned[pl.ds(pl.multiple_of(k * groups, groups), groups), :]
            out_ref[k, here * rows :, :] = jnp.concatenate([head, scale], axis=0).astype(BF16)
            q_read(k).wait()
            for j in range(here):
                out_ref[k, j * rows : (j + 1) * rows, :] = q_ref[k, :, j * LANES : (j + 1) * LANES]
            for band in range(owners // columns):
                write(k, band).start()

        @pl.loop(0, columns)
        def _(k):
            for band in range(owners // columns):
                write(k, band).wait()

    operands = [slots, q_values, scales, *sums_of]
    return pl.pallas_call(
        body,
        out_shape=jax.ShapeDtypeStruct((owners, tall, LANES), BF16),
        in_specs=[HBM] * len(operands),
        out_specs=HBM,
        scratch_shapes=[
            pltpu.SMEM(slots.shape, jnp.int32),
            pltpu.SMEM((owners,), jnp.int32),
            pltpu.VMEM((columns, rows, part), BF16),
            pltpu.VMEM(scales.shape, BF16),
            pltpu.VMEM((max(len(sums_of), 1), 8, LANES), F32),
            pltpu.VMEM((LANES, LANES), F32),
            pltpu.VMEM((columns, tall, LANES), BF16),
            DMA((columns + 2 + len(sums_of),)),
            DMA((owners,)),
        ],
        compiler_params=grant(16 if sums_of else 60),
        cost_estimate=cost(0, 2 * rows * cols + 2 * owners * tall * LANES),
        name=f"pack_{start}",
    )(*operands)


def square_sum(q_values, scales):
    rows, cols = q_values.shape
    groups = scales.shape[1]
    group = cols // groups

    def body(q_hbm, s_hbm, out_ref, q_ref, s_ref, sems):
        reads = [pltpu.make_async_copy(q_hbm, q_ref, sems.at[0]), pltpu.make_async_copy(s_hbm, s_ref, sems.at[1])]
        for read in reads:
            read.start()
        for read in reads:
            read.wait()
        total = jnp.zeros((rows, group), F32)
        for j in range(groups):
            grad = q_ref[:, j * group : (j + 1) * group].astype(F32) * s_ref[:, j : j + 1].astype(F32)
            total = total + grad * grad
        out_ref[...] = jnp.full((8, LANES), jnp.sum(total))

    return pl.pallas_call(
        body,
        out_shape=jax.ShapeDtypeStruct((8, LANES), F32),
        in_specs=[HBM] * 2,
        scratch_shapes=[pltpu.VMEM((rows, cols), BF16), pltpu.VMEM(scales.shape, BF16), DMA((2,))],
        compiler_params=grant(60),
        cost_estimate=cost(3 * rows * cols, 2 * rows * cols),
        name="square_sum",
    )(q_values, scales)


def split_roots(left, right):
    size = left.shape[0]

    def body(l_ref, r_ref, l1_ref, l2_ref, r1_ref, r2_ref):
        @pl.loop(0, size // FINE)
        def _(k):
            at = pl.ds(pl.multiple_of(k * FINE, FINE), FINE)
            l1_ref[at, :], l2_ref[at, :] = two(l_ref[at, :])
            r1_ref[at, :], r2_ref[at, :] = two(r_ref[at, :])

    return pl.pallas_call(
        body,
        out_shape=[jax.ShapeDtypeStruct((size, size), BF16)] * 4,
        in_specs=[VMEM] * 2,
        out_specs=[VMEM] * 4,
        compiler_params=grant(20),
        cost_estimate=cost(4 * size * size, 16 * size * size),
        name="split_roots",
    )(left, right)


def dequant(a_ref, band, pieces, rows, group, grad_ref, h1, h2):
    tall = a_ref.shape[1]
    here = (tall - EXTRA) // rows

    @pl.loop(0, pieces)
    def _(piece):
        source = band * pieces + piece
        scales = a_ref[source, here * rows :, :].astype(F32).T
        at = pl.ds(pl.multiple_of(piece * rows, rows), rows)
        for j in range(here):
            column = EXTRA - 8 + group + j
            grad = a_ref[source, j * rows : (j + 1) * rows, :].astype(F32) * scales[:rows, column : column + 1]
            lanes = slice(j * LANES, (j + 1) * LANES)
            grad_ref[at, lanes] = grad
            h1[at, lanes], h2[at, lanes] = two(grad)


def products(slots, arrived, l1, l2, r1, r2, rows, columns):
    size = l1.shape[0]
    _, tall, _ = arrived.shape
    pieces = size // rows
    part = tall // rows * LANES
    block = size // STEPS

    def body(slots_ref, a_ref, l1_ref, l2_ref, r1_ref, r2_ref, p_ref, grad_ref, h1, h2, t1, t2):
        dequant(a_ref, own_band(slots_ref, columns), pieces, rows, 0, grad_ref, h1, h2)

        @pl.loop(0, part // block)
        def _(n):
            at = pl.ds(pl.multiple_of(n * block, block), block)
            half = dot(l1_ref[...], h1[:, at]) + (dot(l1_ref[...], h2[:, at]) + dot(l2_ref[...], h1[:, at]))
            t1[:, at], t2[:, at] = two(half)

        @pl.loop(0, STEPS)
        def _(n):
            at = pl.ds(pl.multiple_of(n * block, block), block)
            r1_at, r2_at = r1_ref[:part, at], r2_ref[:part, at]
            p_ref[:, at] = dot(t1[...], r1_at) + (dot(t1[...], r2_at) + dot(t2[...], r1_at))

    square = (size, size)
    narrow = (size, part)
    return pl.pallas_call(
        body,
        out_shape=[jax.ShapeDtypeStruct(square, F32), jax.ShapeDtypeStruct(narrow, F32)],
        in_specs=[SMEM] + [VMEM] * 5,
        out_specs=[VMEM] * 2,
        scratch_shapes=[pltpu.VMEM(narrow, BF16)] * 4,
        compiler_params=grant(26),
        cost_estimate=cost(12 * size * size * part, 20 * size * size),
        name="products",
    )(slots, arrived, l1, l2, r1, r2)


def graft(slots, arrived, l1, l2, r1, r2, earlier, grad, moment, rows, columns, entries):
    size = moment.shape[0]
    owners, tall, _ = arrived.shape
    pieces = size // rows
    block = size // STEPS
    done = grad.shape[1]
    part = size - done
    thin = size // FINE

    def body(
        slots_ref, a_ref, l1_ref, l2_ref, r1_ref, r2_ref, p_ref, old_ref, m_hbm, out_hbm, fresh_hbm,
        new_ref, h1, h2, t1, t2, all_ref, m_ref, out_ref, asum, psum, outs,
    ):
        band = own_band(slots_ref, columns)

        def cut(n):
            return pl.ds(pl.multiple_of(n * block, block), block)

        m_read = pltpu.make_async_copy(m_hbm, m_ref, outs.at[2, 0])
        m_read.start()
        dequant(a_ref, band, pieces, rows, done // LANES, new_ref, h1, h2)
        heads = jnp.sum(a_ref[:, tall - EXTRA :, :].astype(F32), axis=0)[: EXTRA - 8]
        total = jnp.sum(heads, axis=0, keepdims=True)[:, :1]
        bound = 0.5 * jnp.sqrt(jnp.full((1, 1), entries, F32)) / jnp.sqrt(jnp.where(total > 0, total, 1.0))
        clip = jnp.where(total > 0, jnp.minimum(bound, 1.0), 1.0)
        asum[...] = jnp.zeros_like(asum)
        psum[...] = jnp.zeros_like(psum)
        half = dot(l1_ref[...], h1[...]) + (dot(l1_ref[...], h2[...]) + dot(l2_ref[...], h1[...]))
        t1[...], t2[...] = two(half)

        m_read.wait()

        def fresh_copy(n):
            return pltpu.make_async_copy(m_ref.at[cut(n)], fresh_hbm.at[cut(n)], outs.at[0, n])

        def out_copy(n):
            to = pl.ds(pl.multiple_of(band * size + n * block, block), block)
            return pltpu.make_async_copy(out_ref.at[cut(n)], out_hbm.at[to], outs.at[1, n])

        def adam(line, lanes, grads):
            held = grads * clip
            square = held * held
            fresh = 0.9 * m_ref[line, lanes] + 0.1 * square
            m_ref[line, lanes] = fresh
            root = fresh * lax.rsqrt(fresh) + 1e-08
            asum[...] += fold(square / (root * root))

        @pl.loop(0, STEPS)
        def _(n):
            at = cut(n)
            r1_at, r2_at = r1_ref[done:, at], r2_ref[done:, at]
            more = dot(t1[...], r1_at) + (dot(t1[...], r2_at) + dot(t2[...], r1_at))
            product = p_ref[:, at] + more
            all_ref[:, at] = product
            psum[...] += fold(product * product)

            @pl.loop(0, block // thin)
            def _(k):
                line = pl.ds(pl.multiple_of(n * block + k * thin, thin), thin)
                adam(line, slice(0, done), old_ref[line, :])
                adam(line, slice(done, size), new_ref[line, :])

            fresh_copy(n).start()

        norm = jnp.sqrt(everywhere(psum[...]) * (clip * clip) + 1e-12)
        ratio = clip * (jnp.sqrt(everywhere(asum[...])) / norm)

        @pl.loop(0, STEPS)
        def _(n):
            out_ref[cut(n), :] = (all_ref[cut(n), :] * ratio).astype(BF16)
            out_copy(n).start()

        for n in range(STEPS):
            fresh_copy(n).wait()
            out_copy(n).wait()

    square = (size, size)
    return pl.pallas_call(
        body,
        out_shape=[
            jax.ShapeDtypeStruct((owners * rows, size), BF16),
            jax.ShapeDtypeStruct(square, F32),
        ],
        in_specs=[SMEM] + [VMEM] * 7 + [HBM],
        out_specs=[HBM, HBM],
        scratch_shapes=[pltpu.VMEM((size, part), F32)]
        + [pltpu.VMEM((size, part), BF16)] * 4
        + [
            pltpu.VMEM(square, F32),
            pltpu.VMEM(square, F32),
            pltpu.VMEM(square, BF16),
            pltpu.VMEM((8, LANES), F32),
            pltpu.VMEM((8, LANES), F32),
            DMA((3, STEPS)),
        ],
        compiler_params=grant(24),
        cost_estimate=cost(12 * size * size * part, 24 * size * size),
        name="graft",
    )(slots, arrived, l1, l2, r1, r2, earlier, grad, moment)


def place(slots, returned, cols):
    owners, rows, width = returned.shape
    columns = cols // width

    def body(slots_ref, r_hbm, out_hbm, inverse, out_ref, ins, outs):
        first = lax.div(lax.axis_index("fsdp") * rows, width) * columns
        invert(slots_ref, inverse)

        def here(k):
            return pl.ds(pl.multiple_of(k * width, width), width)

        def read(k):
            return pltpu.make_async_copy(r_hbm.at[inverse[first + k]], out_ref.at[:, here(k)], ins.at[k])

        def write(k):
            return pltpu.make_async_copy(out_ref.at[:, here(k)], out_hbm.at[:, here(k)], outs.at[k])

        @pl.loop(0, columns)
        def _(k):
            read(k).start()

        @pl.loop(0, columns)
        def _(k):
            read(k).wait()
            write(k).start()

        @pl.loop(0, columns)
        def _(k):
            write(k).wait()

    return pl.pallas_call(
        body,
        out_shape=jax.ShapeDtypeStruct((rows, cols), BF16),
        in_specs=[SMEM, HBM],
        out_specs=HBM,
        scratch_shapes=[
            pltpu.SMEM((owners,), jnp.int32),
            pltpu.VMEM((rows, cols), BF16),
            DMA((columns,)),
            DMA((columns,)),
        ],
        compiler_params=grant(60),
        cost_estimate=cost(0, 4 * rows * cols),
        name="place",
    )(slots, returned)


def on_device(q_values, scales, block_slots, left_root, right_root, second_moment):
    count = lax.axis_size("fsdp")
    planes = lax.axis_size("grp")
    rows, cols = q_values.shape
    width = left_root.shape[-1]
    columns = cols // width
    first = width * 3 // 4

    def exchange(value):
        return lax.all_to_all(value, "fsdp", split_axis=0, concat_axis=0, tiled=True)

    arrived = exchange(pack(block_slots, q_values, scales, [], width, 0, first))
    own = square_sum(q_values, scales)
    sums = [own]
    for k in range(1, planes):
        sums.append(lax.ppermute(own, "grp", [(i, (i + k) % planes) for i in range(planes)]))
    *sums, l1, l2, r1, r2 = lax.optimization_barrier((*sums, *split_roots(left_root[0, 0], right_root[0, 0])))
    roots = (l1, l2, r1, r2)
    later = exchange(pack(block_slots, q_values, scales, sums, width, first, width - first))

    product, grad = products(block_slots, arrived, *roots, rows, columns)
    outgoing, fresh = graft(
        block_slots, later, *roots, product, grad, second_moment[0, 0], rows, columns, rows * count * cols * planes
    )
    update = place(block_slots, exchange(outgoing.reshape(count, rows, width)), cols)
    return (update, fresh[None, None])


def solution(mesh):
    in_specs = (
        P("fsdp", "grp"),
        P("fsdp", "grp"),
        P("grp", None),
        P("grp", "fsdp", None, None),
        P("grp", "fsdp", None, None),
        P("grp", "fsdp", None, None),
    )
    out_specs = (P("fsdp", "grp"), P("grp", "fsdp", None, None))
    return jax.shard_map(
        on_device, mesh=mesh, in_specs=in_specs, out_specs=out_specs, check_vma=False
    )
```

time: 352 us -> 174 us (0.49)
  waiting for transfers between devices: 156 us -> 20.2 us
  matrix products: 45.9 us -> 0 us
  Pallas kernels: 0 us -> 40.6 us
  other arithmetic: 28.9 us -> 0 us
  blocking collectives: 80.3 us -> 57.9 us
  local copies, waits for them, and re-layouts: 19 us -> 34.5 us
  between operations: 5.49 us -> 0.78 us
  starting transfers between devices: 15 us -> 18.8 us
    all_to_all x2, waiting for transfers between devices: 156 us -> 20.2 us  [exchange(): lax.all_to_all(value, 'fsdp', split_axis=0, concat_axis=0, tiled=True)]
    psum x1 -> x0, blocking collectives: 80.3 us -> none  [on_device(): total = lax.psum(jnp.sum(held_raw * held_raw), ('fsdp', 'grp'))]
    all_to_all x0 -> x1, blocking collectives: none -> 57.9 us  [exchange(): lax.all_to_all(value, 'fsdp', split_axis=0, concat_axis=0, tiled=True)]
    dot_general x2 -> x0, matrix products: 45.9 us -> none  [the longest x1 30.3 us: precondition(): jnp.matmul(left, held, precision=lax.Precision.HIGHEST)]
    pallas_call x0 -> x7, Pallas kernels: none -> 40.6 us  [the longest x1 14.8 us: products(): pl.pallas_call(body, out_shape=[jax.ShapeDtypeStruct(square, F32), jax.Sh...]
    unnamed x10 -> x50, local copies, waits for them, and re-layouts: 0.66 us -> 34.5 us
    select_n x2 -> x0, other arithmetic: 9.47 us -> none  [to_pieces(): return jnp.take(tiles, wanted, axis=0)]
    gather x2 -> x0, local copies, waits for them, and re-layouts: 9.35 us -> none  [the longest x1 6.48 us: to_pieces(): return jnp.take(tiles, wanted, axis=0)]
  transfers between devices with their start and end apart: 2 -> 5, of which waited for: 2 -> 1; matrix products, arithmetic and copies ran while one was open for 1% -> 0% of each run, Pallas kernels for 0% -> 12%
where the time goes in v2:
time: 174 us; the launch traced here: 173 us
  blocking collectives  57.9 us (33%)
  Pallas kernels  40.6 us (23%)
  local copies, waits for them, and re-layouts  34.5 us (20%)
  waiting for transfers between devices  20.2 us (12%)
  starting transfers between devices  18.8 us (11%)
    all_to_all x1, blocking collectives, exchange(): lax.all_to_all(value, 'fsdp', split_axis=0, concat_axis=0, tiled=True)  57.9 us
    unnamed x50, local copies, waits for them, and re-layouts  34.5 us
    all_to_all x2, waiting for transfers between devices, exchange(): lax.all_to_all(value, 'fsdp', split_axis=0, concat_axis=0, tiled=True)  20.2 us
    pallas_call x1, Pallas kernels, products(): pl.pallas_call(body, out_shape=[jax.ShapeDtypeStruct(square, F32), jax.Sh...  14.8 us
    all_to_all x2, starting transfers between devices, exchange(): lax.all_to_all(value, 'fsdp', split_axis=0, concat_axis=0, tiled=True)  14.3 us
    pallas_call x1, Pallas kernels, graft(): pl.pallas_call(body, out_shape=[jax.ShapeDtypeStruct((owners * rows, size...  12.9 us
    pallas_call x2, Pallas kernels, pack(): pl.pallas_call(body, out_shape=jax.ShapeDtypeStruct((owners, tall, LANES)...  5.28 us
    ppermute x3, starting transfers between devices, on_device(): lax.ppermute(own, 'grp', [(i, (i + k) % planes) for i in range(planes)])  4.53 us
  transfers between devices with their start and end apart: 5, of which 1 were waited for; matrix products, arithmetic and copies ran while one was open for 0% of the time, Pallas kernels for 12%

profile of v2, /device:TPU:1, one launch (start us, length us, event | category | flops | bytes accessed | tf_op | source)
XLA Modules:
  0.0 172.7 jit_solution(8982443689483918791)
XLA Ops:
  0.6 3.1 %pack_0.1 = bf16[32,400,128]{2,1,0:T(8,128)(2,1)} custom-call(s32[1,32]{1,0:T(1,128)} %slots_ref.5, bf16[64,16384]{1,0:T(8,128)(2,1)} %q_hbm.5, bf16[64,128]{1,0:T(8,128)(2,1)} %s_hbm.5), custom_call_target="tpu_custom_call" | custom-call | bytes 5373952 | tf_op jit(solution)/shard_map/pack_0/pallas_call | solution.py:124
  3.7 8.6 %all-to-all-start.1 = ((bf16[32,400,128]{2,1,0:T(8,128)(2,1)}), bf16[32,400,128]{2,1,0:T(8,128)(2,1)S(1)}, u32[]{:S(2)}, u32[]{:S(2)}) async-start(bf16[32,400,128]{2,1,0:T(8,128)(2,1)} %pack_0.1), calls=%async_computation.1 | async-start | bytes 6553600 | tf_op jit(solution)/shard_map/all_to_all | solution.py:405
  12.3 3.1 %square_sum.1.rest_0_ = f32[8,128]{1,0:T(8,128)} custom-call(bf16[64,16384]{1,0:T(8,128)(2,1)} %q_hbm.5, bf16[64,128]{1,0:T(8,128)(2,1)} %s_hbm.5), custom_call_target="tpu_custom_call" | custom-call | flops 3145728 | bytes 2097152 | tf_op jit(solution)/shard_map/square_sum/pallas_call | solution.py:163
  15.5 3.8 %collective-permute-start.2 = (f32[8,128]{1,0:T(8,128)}, f32[8,128]{1,0:T(8,128)S(1)}, u32[]{:S(2)}, u32[]{:S(2)}) collective-permute-start(f32[8,128]{1,0:T(8,128)} %square_sum.1.rest_0_), channel_id=1, source_target_pairs={{0,3},{1,0},{2,1},{3,2},{4,7},{5,4},{6,5},{7,6},{8,11},{9,8},{10,9... | collective-permute-start | bytes 12296 | tf_op jit(solution)/shard_map/ppermute | solution.py:411
  20.0 2.2 %copy-done.1 = f32[1,1,1024,1024]{3,2,1,0:T(8,128)S(1)} copy-done((f32[1,1,1024,1024]{3,2,1,0:T(8,128)S(1)}, f32[1,1,1024,1024]{3,2,1,0:T(8,128)}, u32[]{:S(2)}) %copy-start.1) | copy-done | bytes 4194328
  22.2 2.2 %copy-done.2 = f32[1,1,1024,1024]{3,2,1,0:T(8,128)S(1)} copy-done((f32[1,1,1024,1024]{3,2,1,0:T(8,128)S(1)}, f32[1,1,1024,1024]{3,2,1,0:T(8,128)}, u32[]{:S(2)}) %copy-start.2) | copy-done | bytes 4194328
  31.0 2.2 %pack_768.1 = bf16[32,144,128]{2,1,0:T(8,128)(2,1)} custom-call(s32[1,32]{1,0:T(1,128)S(1)} %copy-done.24, bf16[64,16384]{1,0:T(8,128)(2,1)S(1)} %copy-done, bf16[64,128]{1,0:T(8,128)(2,1)S(1)} %copy-done.22, f32[8,128]{1,0:T(8,128)S(1)} %copy-done.23, f32[8,128]{1,0:T(8,128)S(1)} %collective-permute-done.rest_1_, ...), custom_call_target="tpu_custom_call" | custom-call | bytes 3276800 | tf_op jit(solution)/shard_map/pack_768/pallas_call | solution.py:124
  33.2 20.2 %all-to-all-done.1.a_ref = bf16[32,400,128]{2,1,0:T(8,128)(2,1)S(1)} async-done(((bf16[32,400,128]{2,1,0:T(8,128)(2,1)}), bf16[32,400,128]{2,1,0:T(8,128)(2,1)S(1)}, u32[]{:S(2)}, u32[]{:S(2)}) %all-to-all-start.1) | async-done | bytes 3276832 | tf_op jit(solution)/shard_map/all_to_all | solution.py:405
  53.4 1.7 copy-done.6
  55.1 5.7 %all-to-all-start = ((bf16[32,144,128]{2,1,0:T(8,128)(2,1)}), bf16[32,144,128]{2,1,0:T(8,128)(2,1)S(1)}, u32[]{:S(2)}, u32[]{:S(2)}) async-start(bf16[32,144,128]{2,1,0:T(8,128)(2,1)} %pack_768.1), calls=%async_computation | async-start | bytes 2359296 | tf_op jit(solution)/shard_map/all_to_all | solution.py:405
  60.8 1.9 %copy-done.7 = bf16[32,400,128]{2,1,0:T(8,128)(2,1)S(1)} copy-done((bf16[32,400,128]{2,1,0:T(8,128)(2,1)S(1)}, bf16[32,400,128]{2,1,0:T(8,128)(2,1)}, u32[]{:S(2)}) %copy-start.7) | copy-done | bytes 3276824
  62.7 1.6 copy-done.11
  69.1 14.8 %products.1 = (f32[1024,1024]{1,0:T(8,128)S(1)}, f32[1024,768]{1,0:T(8,128)S(1)}) custom-call(s32[1,32]{1,0:T(1,128)S(1)} %copy-done.24, bf16[32,400,128]{2,1,0:T(8,128)(2,1)S(1)} %copy-done.7, bf16[1024,1024]{1,0:T(8,128)(2,1)S(1)} %copy-done.11, bf16[1024,1024]{1,0:T(8,128)(2,1)S(1)} %copy-done.14, bf16[1024,1024]{1,0:T(8,128)(2,1)S(1)} %copy-done.17, ...), custom_call_target="tpu_custom_call" | custom-call | flops 9663676416 | bytes 20971520 | tf_op jit(solution)/shard_map/products/pallas_call | solution.py:236
  83.9 2.0 %copy-done.4 = f32[1024,1024]{1,0:T(8,128)} copy-done((f32[1024,1024]{1,0:T(8,128)}, f32[1024,1024]{1,0:T(8,128)S(1)}, u32[]{:S(2)}) %copy-start.4) | copy-done | bytes 4194328
  85.9 1.6 copy-done.8
  87.5 2.2 %copy-done.3 = f32[1,1,1024,1024]{3,2,1,0:T(8,128)S(1)} copy-done((f32[1,1,1024,1024]{3,2,1,0:T(8,128)S(1)}, f32[1,1,1024,1024]{3,2,1,0:T(8,128)}, u32[]{:S(2)}) %copy-start.3) | copy-done | bytes 4194328
  89.7 2.2 %copy-done.5 = f32[1024,1024]{1,0:T(8,128)S(1)} copy-done((f32[1024,1024]{1,0:T(8,128)S(1)}, f32[1024,1024]{1,0:T(8,128)}, u32[]{:S(2)}) %copy-start.5) | copy-done | bytes 4194328
  91.9 1.9 %copy-done.9 = f32[1024,768]{1,0:T(8,128)S(1)} copy-done((f32[1024,768]{1,0:T(8,128)S(1)}, f32[1024,768]{1,0:T(8,128)}, u32[]{:S(2)}) %copy-start.9) | copy-done | bytes 3145752
  93.8 1.6 copy-done.15
  95.4 1.6 copy-done.18
  97.0 1.6 copy-done.21
  98.6 12.9 %graft.1 = (bf16[2048,1024]{1,0:T(8,128)(2,1)S(1)}, f32[1024,1024]{1,0:T(8,128)}) custom-call(s32[1,32]{1,0:T(1,128)S(1)} %copy-done.24, bf16[32,144,128]{2,1,0:T(8,128)(2,1)S(1)} %all-to-all-done.a_ref, bf16[1024,1024]{1,0:T(8,128)(2,1)S(1)} %copy-done.12, bf16[1024,1024]{1,0:T(8,128)(2,1)S(1)} %copy-done.15, bf16[1024,1024]{1,0:T(8,128)(2,1)S(1)} %copy-done.18, ...), custom_call_target="tpu_custom_call" | custom-call | flops 3221225472 | bytes 25165824 | tf_op jit(solution)/shard_map/graft/pallas_call | solution.py:325
  111.5 57.9 %all_to_all.15.r_hbm = bf16[32,64,1024]{2,1,0:T(8,128)(2,1)} all-to-all(bf16[32,64,1024]{2,1,0:T(8,128)(2,1)S(1)} %bitcast.7), channel_id=1, replica_groups=mesh['fsdp'=32,'grp'=4] {'fsdp'}, dimensions={0} | all-to-all | bytes 8388608 | tf_op jit(solution)/shard_map/all_to_all | solution.py:405
  169.4 3.3 %place.1 = bf16[64,16384]{1,0:T(8,128)(2,1)} custom-call(s32[1,32]{1,0:T(1,128)} %slots_ref.5, bf16[32,64,1024]{2,1,0:T(8,128)(2,1)} %all_to_all.15.r_hbm), custom_call_target="tpu_custom_call" | custom-call | bytes 4194304 | tf_op jit(solution)/shard_map/place/pallas_call | solution.py:379
  (44 shorter events, 12.1 us)
Async XLA Ops:
  3.7 49.7 %all-to-all-start.1 = ((bf16[32,400,128]{2,1,0:T(8,128)(2,1)}), bf16[32,400,128]{2,1,0:T(8,128)(2,1)S(1)}, u32[]{:S(2)}, u32[]{:S(2)}) async-start(bf16[32,400,128]{2,1,0:T(8,128)(2,1)} %pack_0.1), calls=%async_computation.1 | async-start | bytes 6553600 | tf_op jit(solution)/shard_map/all_to_all | solution.py:405
  15.5 15.5 %collective-permute-start.2 = (f32[8,128]{1,0:T(8,128)}, f32[8,128]{1,0:T(8,128)S(1)}, u32[]{:S(2)}, u32[]{:S(2)}) collective-permute-start(f32[8,128]{1,0:T(8,128)} %square_sum.1.rest_0_), channel_id=1, source_target_pairs={{0,3},{1,0},{2,1},{3,2},{4,7},{5,4},{6,5},{7,6},{8,11},{9,8},{10,9... | collective-permute-start | bytes 12296 | tf_op jit(solution)/shard_map/ppermute | solution.py:411
  19.3 11.7 %collective-permute-start.1 = (f32[8,128]{1,0:T(8,128)}, f32[8,128]{1,0:T(8,128)S(1)}, u32[]{:S(2)}, u32[]{:S(2)}) collective-permute-start(f32[8,128]{1,0:T(8,128)} %square_sum.1.rest_0_), channel_id=1, source_target_pairs={{0,2},{1,3},{2,0},{3,1},{4,6},{5,7},{6,4},{7,5},{8,10},{9,11},{10,... | collective-permute-start | bytes 12296 | tf_op jit(solution)/shard_map/ppermute | solution.py:411
  19.3 11.7 %collective-permute-start = (f32[8,128]{1,0:T(8,128)}, f32[8,128]{1,0:T(8,128)S(1)}, u32[]{:S(2)}, u32[]{:S(2)}) collective-permute-start(f32[8,128]{1,0:T(8,128)} %square_sum.1.rest_0_), channel_id=1, source_target_pairs={{0,1},{1,2},{2,3},{3,0},{4,5},{5,6},{6,7},{7,4},{8,9},{9,10},{10,1... | collective-permute-start | bytes 12296 | tf_op jit(solution)/shard_map/ppermute | solution.py:411
  20.0 2.2 %copy-start.1 = (f32[1,1,1024,1024]{3,2,1,0:T(8,128)S(1)}, f32[1,1,1024,1024]{3,2,1,0:T(8,128)}, u32[]{:S(2)}) copy-start(f32[1,1,1024,1024]{3,2,1,0:T(8,128)} %param.9) | copy-start | bytes 12582916
  22.2 2.2 %copy-start.2 = (f32[1,1,1024,1024]{3,2,1,0:T(8,128)S(1)}, f32[1,1,1024,1024]{3,2,1,0:T(8,128)}, u32[]{:S(2)}) copy-start(f32[1,1,1024,1024]{3,2,1,0:T(8,128)} %param.10) | copy-start | bytes 12582916
  24.4 6.6 %copy-start = (bf16[64,16384]{1,0:T(8,128)(2,1)S(1)}, bf16[64,16384]{1,0:T(8,128)(2,1)}, u32[]{:S(2)}) copy-start(bf16[64,16384]{1,0:T(8,128)(2,1)} %q_hbm.5) | copy-start | bytes 6291460
  24.4 6.6 %copy-start.22 = (bf16[64,128]{1,0:T(8,128)(2,1)S(1)}, bf16[64,128]{1,0:T(8,128)(2,1)}, u32[]{:S(2)}) copy-start(bf16[64,128]{1,0:T(8,128)(2,1)} %s_hbm.5) | copy-start | bytes 49156
  24.4 6.6 %copy-start.23 = (f32[8,128]{1,0:T(8,128)S(1)}, f32[8,128]{1,0:T(8,128)}, u32[]{:S(2)}) copy-start(f32[8,128]{1,0:T(8,128)} %square_sum.1.rest_0_) | copy-start | bytes 12292
  24.4 6.6 %copy-start.24 = (s32[1,32]{1,0:T(1,128)S(1)}, s32[1,32]{1,0:T(1,128)}, u32[]{:S(2)}) copy-start(s32[1,32]{1,0:T(1,128)} %slots_ref.5) | copy-start | bytes 388
  53.4 1.7 copy-start.6
  55.1 32.4 %all-to-all-start = ((bf16[32,144,128]{2,1,0:T(8,128)(2,1)}), bf16[32,144,128]{2,1,0:T(8,128)(2,1)S(1)}, u32[]{:S(2)}, u32[]{:S(2)}) async-start(bf16[32,144,128]{2,1,0:T(8,128)(2,1)} %pack_768.1), calls=%async_computation | async-start | bytes 2359296 | tf_op jit(solution)/shard_map/all_to_all | solution.py:405
  60.8 1.9 %copy-start.7 = (bf16[32,400,128]{2,1,0:T(8,128)(2,1)S(1)}, bf16[32,400,128]{2,1,0:T(8,128)(2,1)}, u32[]{:S(2)}) copy-start(bf16[32,400,128]{2,1,0:T(8,128)(2,1)} %copy-done.6) | copy-start | bytes 9830404
  62.7 1.6 copy-start.11
  64.3 1.6 copy-start.14
  65.9 1.6 copy-start.17
  67.5 1.6 copy-start.20
  69.1 18.4 %copy-start.12 = (bf16[1024,1024]{1,0:T(8,128)(2,1)S(1)}, bf16[1024,1024]{1,0:T(8,128)(2,1)}, u32[]{:S(2)}) copy-start(bf16[1024,1024]{1,0:T(8,128)(2,1)} %copy-done.10) | copy-start | bytes 6291460
  83.9 2.0 %copy-start.4 = (f32[1024,1024]{1,0:T(8,128)}, f32[1024,1024]{1,0:T(8,128)S(1)}, u32[]{:S(2)}) copy-start(f32[1024,1024]{1,0:T(8,128)S(1)} %get-tuple-element.30.p_ref) | copy-start | bytes 12582916
  85.9 1.6 copy-start.8
  87.5 2.2 %copy-start.3 = (f32[1,1,1024,1024]{3,2,1,0:T(8,128)S(1)}, f32[1,1,1024,1024]{3,2,1,0:T(8,128)}, u32[]{:S(2)}) copy-start(f32[1,1,1024,1024]{3,2,1,0:T(8,128)} %param.11) | copy-start | bytes 12582916
  89.7 2.2 %copy-start.5 = (f32[1024,1024]{1,0:T(8,128)S(1)}, f32[1024,1024]{1,0:T(8,128)}, u32[]{:S(2)}) copy-start(f32[1024,1024]{1,0:T(8,128)} %copy-done.4) | copy-start | bytes 12582916
  91.9 1.9 %copy-start.9 = (f32[1024,768]{1,0:T(8,128)S(1)}, f32[1024,768]{1,0:T(8,128)}, u32[]{:S(2)}) copy-start(f32[1024,768]{1,0:T(8,128)} %copy-done.8) | copy-start | bytes 9437188
  93.8 1.6 copy-start.15
  (6 other events, 8.6 us)

commit v3 on v2

--- a/solution.py
+++ b/solution.py
@@ -8,17 +8,13 @@
 LANES = 128
 EXTRA = 16
 STEPS = 4
-FINE = 32
+FINE = 8
 F32 = jnp.float32
 BF16 = jnp.bfloat16
 HBM = pl.BlockSpec(memory_space=pltpu.HBM)
 SMEM = pl.BlockSpec(memory_space=pltpu.SMEM)
-VMEM = pl.BlockSpec(memory_space=pltpu.VMEM)
+PARAMS = pltpu.CompilerParams(vmem_limit_bytes=63 * 1024 * 1024)
 DMA = pltpu.SemaphoreType.DMA
-
-
-def grant(mib):
-    return pltpu.CompilerParams(vmem_limit_bytes=mib * 1024 * 1024)
 
 
 def cost(flops, nbytes):
@@ -137,7 +133,7 @@
             DMA((columns + 2 + len(sums_of),)),
             DMA((owners,)),
         ],
-        compiler_params=grant(16 if sums_of else 60),
+        compiler_params=PARAMS,
         cost_estimate=cost(0, 2 * rows * cols + 2 * owners * tall * LANES),
         name=f"pack_{start}",
     )(*operands)
@@ -165,7 +161,7 @@
         out_shape=jax.ShapeDtypeStruct((8, LANES), F32),
         in_specs=[HBM] * 2,
         scratch_shapes=[pltpu.VMEM((rows, cols), BF16), pltpu.VMEM(scales.shape, BF16), DMA((2,))],
-        compiler_params=grant(60),
+        compiler_params=PARAMS,
         cost_estimate=cost(3 * rows * cols, 2 * rows * cols),
         name="square_sum",
     )(q_values, scales)
@@ -173,39 +169,59 @@
 
 def split_roots(left, right):
     size = left.shape[0]
-
-    def body(l_ref, r_ref, l1_ref, l2_ref, r1_ref, r2_ref):
-        @pl.loop(0, size // FINE)
-        def _(k):
-            at = pl.ds(pl.multiple_of(k * FINE, FINE), FINE)
-            l1_ref[at, :], l2_ref[at, :] = two(l_ref[at, :])
-            r1_ref[at, :], r2_ref[at, :] = two(r_ref[at, :])
-
+    rows = size // STEPS
+
+    def body(l_hbm, r_hbm, l1_hbm, l2_hbm, r1_hbm, r2_hbm, full, top, low, ins, outs):
+        jobs = []
+        for src, high_hbm, low_hbm in ((l_hbm, l1_hbm, l2_hbm), (r_hbm, r1_hbm, r2_hbm)):
+            for n in range(STEPS):
+                at = pl.ds(n * rows, rows)
+                jobs.append((src.at[at], high_hbm.at[at], low_hbm.at[at]))
+        reads = [pltpu.make_async_copy(job[0], full.at[k], ins.at[k]) for k, job in enumerate(jobs)]
+        for read in reads:
+            read.start()
+        writes = []
+        for k, (_, high_to, low_to) in enumerate(jobs):
+            reads[k].wait()
+            top[k], low[k] = two(full[k])
+            for h, (src, to) in enumerate(((top.at[k], high_to), (low.at[k], low_to))):
+                write = pltpu.make_async_copy(src, to, outs.at[2 * k + h])
+                write.start()
+                writes.append(write)
+        for write in writes:
+            write.wait()
+
+    jobs = 2 * STEPS
     return pl.pallas_call(
         body,
         out_shape=[jax.ShapeDtypeStruct((size, size), BF16)] * 4,
-        in_specs=[VMEM] * 2,
-        out_specs=[VMEM] * 4,
-        compiler_params=grant(20),
+        in_specs=[HBM] * 2,
+        out_specs=[HBM] * 4,
+        scratch_shapes=[
+            pltpu.VMEM((jobs, rows, size), F32),
+            pltpu.VMEM((jobs, rows, size), BF16),
+            pltpu.VMEM((jobs, rows, size), BF16),
+            DMA((jobs,)),
+            DMA((2 * jobs,)),
+        ],
+        compiler_params=PARAMS,
         cost_estimate=cost(4 * size * size, 16 * size * size),
         name="split_roots",
     )(left, right)
 
 
-def dequant(a_ref, band, pieces, rows, group, grad_ref, h1, h2):
-    tall = a_ref.shape[1]
+def dequant(a_ref, turned, rows, group, at_lane, grad_ref, h1, h2):
+    pieces, tall, _ = a_ref.shape
     here = (tall - EXTRA) // rows
-
-    @pl.loop(0, pieces)
-    def _(piece):
-        source = band * pieces + piece
-        scales = a_ref[source, here * rows :, :].astype(F32).T
-        at = pl.ds(pl.multiple_of(piece * rows, rows), rows)
+    scales = a_ref[:, here * rows :, :].astype(F32).reshape(pieces * EXTRA, LANES)
+    turned[...] = scales.T
+    for piece in range(pieces):
+        at = slice(piece * rows, (piece + 1) * rows)
         for j in range(here):
-            column = EXTRA - 8 + group + j
-            grad = a_ref[source, j * rows : (j + 1) * rows, :].astype(F32) * scales[:rows, column : column + 1]
+            column = piece * EXTRA + EXTRA - 8 + group + j
+            grad = a_ref[piece, j * rows : (j + 1) * rows, :].astype(F32) * turned[:rows, column : column + 1]
+            grad_ref[at, at_lane + j * LANES : at_lane + (j + 1) * LANES] = grad
             lanes = slice(j * LANES, (j + 1) * LANES)
-            grad_ref[at, lanes] = grad
             h1[at, lanes], h2[at, lanes] = two(grad)
 
 
@@ -216,8 +232,28 @@
     part = tall // rows * LANES
     block = size // STEPS
 
-    def body(slots_ref, a_ref, l1_ref, l2_ref, r1_ref, r2_ref, p_ref, grad_ref, h1, h2, t1, t2):
-        dequant(a_ref, own_band(slots_ref, columns), pieces, rows, 0, grad_ref, h1, h2)
+    def body(
+        slots_ref, a_hbm, l1_hbm, l2_hbm, r1_hbm, r2_hbm, p_hbm, grad_hbm,
+        a_ref, l1_ref, l2_ref, r1_ref, r2_ref, grad_ref, h1, h2, t1, t2, p_ref, turned, ins, outs,
+    ):
+        band = own_band(slots_ref, columns)
+        deep = pl.ds(0, part)
+        pairs = (
+            (a_hbm.at[pl.ds(band * pieces, pieces)], a_ref),
+            (l1_hbm, l1_ref),
+            (l2_hbm, l2_ref),
+            (r1_hbm.at[deep], r1_ref),
+            (r2_hbm.at[deep], r2_ref),
+        )
+        reads = [pltpu.make_async_copy(s, t, ins.at[k]) for k, (s, t) in enumerate(pairs)]
+        for read in reads:
+            read.start()
+        reads[0].wait()
+        dequant(a_ref, turned, rows, 0, 0, grad_ref, h1, h2)
+        for read in reads[1:3]:
+            read.wait()
+        keep = pltpu.make_async_copy(grad_ref, grad_hbm, outs.at[STEPS])
+        keep.start()
 
         @pl.loop(0, part // block)
         def _(n):
@@ -225,21 +261,37 @@
             half = dot(l1_ref[...], h1[:, at]) + (dot(l1_ref[...], h2[:, at]) + dot(l2_ref[...], h1[:, at]))
             t1[:, at], t2[:, at] = two(half)
 
+        for read in reads[3:]:
+            read.wait()
+
+        def p_copy(n):
+            at = pl.ds(pl.multiple_of(n * block, block), block)
+            return pltpu.make_async_copy(p_ref.at[:, at], p_hbm.at[:, at], outs.at[n])
+
         @pl.loop(0, STEPS)
         def _(n):
             at = pl.ds(pl.multiple_of(n * block, block), block)
-            r1_at, r2_at = r1_ref[:part, at], r2_ref[:part, at]
-            p_ref[:, at] = dot(t1[...], r1_at) + (dot(t1[...], r2_at) + dot(t2[...], r1_at))
+            p_ref[:, at] = dot(t1[...], r1_ref[:, at]) + (dot(t1[...], r2_ref[:, at]) + dot(t2[...], r1_ref[:, at]))
+            p_copy(n).start()
+
+        for n in range(STEPS):
+            p_copy(n).wait()
+        keep.wait()
 
     square = (size, size)
     narrow = (size, part)
     return pl.pallas_call(
         body,
         out_shape=[jax.ShapeDtypeStruct(square, F32), jax.ShapeDtypeStruct(narrow, F32)],
-        in_specs=[SMEM] + [VMEM] * 5,
-        out_specs=[VMEM] * 2,
-        scratch_shapes=[pltpu.VMEM(narrow, BF16)] * 4,
-        compiler_params=grant(26),
+        in_specs=[SMEM] + [HBM] * 5,
+        out_specs=[HBM] * 2,
+        scratch_shapes=[pltpu.VMEM((pieces, tall, LANES), BF16)]
+        + [pltpu.VMEM(square, BF16)] * 2
+        + [pltpu.VMEM((part, size), BF16)] * 2
+        + [pltpu.VMEM(narrow, F32)]
+        + [pltpu.VMEM(narrow, BF16)] * 4
+        + [pltpu.VMEM(square, F32), pltpu.VMEM((LANES, pieces * EXTRA), F32), DMA((5,)), DMA((STEPS + 1,))],
+        compiler_params=PARAMS,
         cost_estimate=cost(12 * size * size * part, 20 * size * size),
         name="products",
     )(slots, arrived, l1, l2, r1, r2)
@@ -255,27 +307,58 @@
     thin = size // FINE
 
     def body(
-        slots_ref, a_ref, l1_ref, l2_ref, r1_ref, r2_ref, p_ref, old_ref, m_hbm, out_hbm, fresh_hbm,
-        new_ref, h1, h2, t1, t2, all_ref, m_ref, out_ref, asum, psum, outs,
+        slots_ref, a_hbm, l1_hbm, l2_hbm, r1_hbm, r2_hbm, p_hbm, grad_hbm, m_hbm, out_hbm, fresh_hbm,
+        sums_ref, a_ref, l1_ref, l2_ref, r1_ref, r2_ref, p_ref, grad_ref, h1, h2, t1, t2, m_ref, out_ref,
+        turned, asum, psum, ins, outs,
     ):
         band = own_band(slots_ref, columns)
+        deep = pl.ds(done, part)
 
         def cut(n):
             return pl.ds(pl.multiple_of(n * block, block), block)
 
-        m_read = pltpu.make_async_copy(m_hbm, m_ref, outs.at[2, 0])
-        m_read.start()
-        dequant(a_ref, band, pieces, rows, done // LANES, new_ref, h1, h2)
-        heads = jnp.sum(a_ref[:, tall - EXTRA :, :].astype(F32), axis=0)[: EXTRA - 8]
+        pairs = (
+            (a_hbm.at[pl.ds(band * pieces, pieces)], a_ref),
+            (a_hbm.at[:, pl.ds(tall - EXTRA, EXTRA)], sums_ref),
+            (l1_hbm, l1_ref),
+            (l2_hbm, l2_ref),
+            (r1_hbm.at[deep], r1_ref),
+            (r2_hbm.at[deep], r2_ref),
+        )
+        reads = [pltpu.make_async_copy(s, t, ins.at[3, k]) for k, (s, t) in enumerate(pairs)]
+
+        def step_reads(n):
+            at = cut(n)
+            pairs = (
+                (p_hbm.at[:, at], p_ref.at[:, at]),
+                (grad_hbm.at[at], grad_ref.at[at, pl.ds(0, done)]),
+                (m_hbm.at[at], m_ref.at[at]),
+            )
+            return [pltpu.make_async_copy(s, t, ins.at[k, n]) for k, (s, t) in enumerate(pairs)]
+
+        for read in reads:
+            read.start()
+
+        @pl.loop(0, STEPS)
+        def _(n):
+            for read in step_reads(n):
+                read.start()
+
+        for read in reads[:2]:
+            read.wait()
+        dequant(a_ref, turned, rows, done // LANES, done, grad_ref, h1, h2)
+        heads = jnp.sum(sums_ref[...].astype(F32), axis=0)[: EXTRA - 8]
         total = jnp.sum(heads, axis=0, keepdims=True)[:, :1]
         bound = 0.5 * jnp.sqrt(jnp.full((1, 1), entries, F32)) / jnp.sqrt(jnp.where(total > 0, total, 1.0))
         clip = jnp.where(total > 0, jnp.minimum(bound, 1.0), 1.0)
         asum[...] = jnp.zeros_like(asum)
         psum[...] = jnp.zeros_like(psum)
+        for read in reads[2:4]:
+            read.wait()
         half = dot(l1_ref[...], h1[...]) + (dot(l1_ref[...], h2[...]) + dot(l2_ref[...], h1[...]))
         t1[...], t2[...] = two(half)
-
-        m_read.wait()
+        for read in reads[4:]:
+            read.wait()
 
         def fresh_copy(n):
             return pltpu.make_async_copy(m_ref.at[cut(n)], fresh_hbm.at[cut(n)], outs.at[0, n])
@@ -284,28 +367,27 @@
             to = pl.ds(pl.multiple_of(band * size + n * block, block), block)
             return pltpu.make_async_copy(out_ref.at[cut(n)], out_hbm.at[to], outs.at[1, n])
 
-        def adam(line, lanes, grads):
-            held = grads * clip
-            square = held * held
-            fresh = 0.9 * m_ref[line, lanes] + 0.1 * square
-            m_ref[line, lanes] = fresh
-            root = fresh * lax.rsqrt(fresh) + 1e-08
-            asum[...] += fold(square / (root * root))
-
         @pl.loop(0, STEPS)
         def _(n):
+            for read in step_reads(n):
+                read.wait()
             at = cut(n)
-            r1_at, r2_at = r1_ref[done:, at], r2_ref[done:, at]
-            more = dot(t1[...], r1_at) + (dot(t1[...], r2_at) + dot(t2[...], r1_at))
+            more = dot(t1[...], r1_ref[:, at]) + (dot(t1[...], r2_ref[:, at]) + dot(t2[...], r1_ref[:, at]))
             product = p_ref[:, at] + more
-            all_ref[:, at] = product
+            p_ref[:, at] = product
             psum[...] += fold(product * product)
 
             @pl.loop(0, block // thin)
             def _(k):
                 line = pl.ds(pl.multiple_of(n * block + k * thin, thin), thin)
-                adam(line, slice(0, done), old_ref[line, :])
-                adam(line, slice(done, size), new_ref[line, :])
+                held = grad_ref[line, :] * clip
+                square = held * held
+                fresh = 0.9 * m_ref[line, :] + 0.1 * square
+                m_ref[line, :] = fresh
+                root = fresh * lax.rsqrt(fresh) + 1e-08
+                inverse = pl.reciprocal(root, approx=True)
+                adam = held * (inverse * (2.0 - root * inverse))
+                asum[...] += fold(adam * adam)
 
             fresh_copy(n).start()
 
@@ -314,7 +396,7 @@
 
         @pl.loop(0, STEPS)
         def _(n):
-            out_ref[cut(n), :] = (all_ref[cut(n), :] * ratio).astype(BF16)
+            out_ref[cut(n), :] = (p_ref[cut(n), :] * ratio).astype(BF16)
             out_copy(n).start()
 
         for n in range(STEPS):
@@ -328,19 +410,23 @@
             jax.ShapeDtypeStruct((owners * rows, size), BF16),
             jax.ShapeDtypeStruct(square, F32),
         ],
-        in_specs=[SMEM] + [VMEM] * 7 + [HBM],
+        in_specs=[SMEM] + [HBM] * 8,
         out_specs=[HBM, HBM],
-        scratch_shapes=[pltpu.VMEM((size, part), F32)]
+        scratch_shapes=[pltpu.VMEM((owners, EXTRA, LANES), BF16), pltpu.VMEM((pieces, tall, LANES), BF16)]
+        + [pltpu.VMEM(square, BF16)] * 2
+        + [pltpu.VMEM((part, size), BF16)] * 2
+        + [pltpu.VMEM(square, F32)] * 2
         + [pltpu.VMEM((size, part), BF16)] * 4
         + [
             pltpu.VMEM(square, F32),
-            pltpu.VMEM(square, F32),
             pltpu.VMEM(square, BF16),
+            pltpu.VMEM((LANES, pieces * EXTRA), F32),
             pltpu.VMEM((8, LANES), F32),
             pltpu.VMEM((8, LANES), F32),
-            DMA((3, STEPS)),
+            DMA((4, 6)),
+            DMA((2, STEPS)),
         ],
-        compiler_params=grant(24),
+        compiler_params=PARAMS,
         cost_estimate=cost(12 * size * size * part, 24 * size * size),
         name="graft",
     )(slots, arrived, l1, l2, r1, r2, earlier, grad, moment)
@@ -387,7 +473,7 @@
             DMA((columns,)),
             DMA((columns,)),
         ],
-        compiler_params=grant(60),
+        compiler_params=PARAMS,
         cost_estimate=cost(0, 4 * rows * cols),
         name="place",
     )(slots, returned)

time: 174 us -> 150 us (0.86)
  local copies, waits for them, and re-layouts: 34.5 us -> 0.59 us
  waiting for transfers between devices: 20.2 us -> 26.7 us
  Pallas kernels: 40.6 us -> 47 us
  blocking collectives: 57.9 us -> 55.4 us
    unnamed x50 -> x6, local copies, waits for them, and re-layouts: 34.5 us -> 0.59 us
    all_to_all x2, waiting for transfers between devices: 20.2 us -> 26.7 us  [exchange(): lax.all_to_all(value, 'fsdp', split_axis=0, concat_axis=0, tiled=True)]
    pallas_call x1, Pallas kernels: 1.15 us -> 6.6 us  [split_roots(): pl.pallas_call(body, out_shape=[jax.ShapeDtypeStruct((size, size), BF16)]...]
    all_to_all x1, blocking collectives: 57.9 us -> 55.4 us  [exchange(): lax.all_to_all(value, 'fsdp', split_axis=0, concat_axis=0, tiled=True)]
  transfers between devices with their start and end apart: 5 -> 5, of which waited for: 1 -> 2; matrix products, arithmetic and copies ran while one was open for 0% -> 0% of each run, Pallas kernels for 12% -> 19%
where the time goes in v3:
time: 150 us; the launch traced here: 149 us
  blocking collectives  55.4 us (37%)
  Pallas kernels  47 us (31%)
  waiting for transfers between devices  26.7 us (18%)
  starting transfers between devices  18.9 us (13%)
    all_to_all x1, blocking collectives, exchange(): lax.all_to_all(value, 'fsdp', split_axis=0, concat_axis=0, tiled=True)  55.4 us
    all_to_all x2, waiting for transfers between devices, exchange(): lax.all_to_all(value, 'fsdp', split_axis=0, concat_axis=0, tiled=True)  26.7 us
    pallas_call x1, Pallas kernels, products(): pl.pallas_call(body, out_shape=[jax.ShapeDtypeStruct(square, F32), jax.Sh...  15.6 us
    all_to_all x2, starting transfers between devices, exchange(): lax.all_to_all(value, 'fsdp', split_axis=0, concat_axis=0, tiled=True)  14.4 us
    pallas_call x1, Pallas kernels, graft(): pl.pallas_call(body, out_shape=[jax.ShapeDtypeStruct((owners * rows, size...  13 us
    pallas_call x1, Pallas kernels, split_roots(): pl.pallas_call(body, out_shape=[jax.ShapeDtypeStruct((size, size), BF16)]...  6.6 us
    pallas_call x2, Pallas kernels, pack(): pl.pallas_call(body, out_shape=jax.ShapeDtypeStruct((owners, tall, LANES)...  5.42 us
    ppermute x3, starting transfers between devices, on_device(): lax.ppermute(own, 'grp', [(i, (i + k) % planes) for i in range(planes)])  4.53 us
  transfers between devices with their start and end apart: 5, of which 2 were waited for; matrix products, arithmetic and copies ran while one was open for 0% of the time, Pallas kernels for 19%

profile of v3, /device:TPU:1, one launch (start us, length us, event | category | flops | bytes accessed | tf_op | source)
XLA Modules:
  0.0 149.3 jit_solution(14371458119753889330)
XLA Ops:
  0.6 3.1 %pack_0.1 = bf16[32,400,128]{2,1,0:T(8,128)(2,1)} custom-call(s32[1,32]{1,0:T(1,128)} %slots_ref.5, bf16[64,16384]{1,0:T(8,128)(2,1)} %q_hbm.5, bf16[64,128]{1,0:T(8,128)(2,1)} %s_hbm.5), custom_call_target="tpu_custom_call" | custom-call | bytes 5373952 | tf_op jit(solution)/shard_map/pack_0/pallas_call | solution.py:120
  3.7 8.6 %all-to-all-start.1 = ((bf16[32,400,128]{2,1,0:T(8,128)(2,1)}), bf16[32,400,128]{2,1,0:T(8,128)(2,1)}, u32[]{:S(2)}, u32[]{:S(2)}) async-start(bf16[32,400,128]{2,1,0:T(8,128)(2,1)} %pack_0.1), calls=%async_computation.1 | async-start | bytes 6553600 | tf_op jit(solution)/shard_map/all_to_all | solution.py:491
  12.4 3.1 %square_sum.1.rest_0_ = f32[8,128]{1,0:T(8,128)} custom-call(bf16[64,16384]{1,0:T(8,128)(2,1)} %q_hbm.5, bf16[64,128]{1,0:T(8,128)(2,1)} %s_hbm.5), custom_call_target="tpu_custom_call" | custom-call | flops 3145728 | bytes 2097152 | tf_op jit(solution)/shard_map/square_sum/pallas_call | solution.py:159
  15.5 3.8 %collective-permute-start.2 = (f32[8,128]{1,0:T(8,128)}, f32[8,128]{1,0:T(8,128)S(1)}, u32[]{:S(2)}, u32[]{:S(2)}) collective-permute-start(f32[8,128]{1,0:T(8,128)} %square_sum.1.rest_0_), channel_id=1, source_target_pairs={{0,3},{1,0},{2,1},{3,2},{4,7},{5,4},{6,5},{7,6},{8,11},{9,8},{10,9... | collective-permute-start | bytes 12296 | tf_op jit(solution)/shard_map/ppermute | solution.py:497
  19.3 0.0 collective-permute-start.1
  19.3 0.7 collective-permute-start
  20.0 6.6 %split_roots.1 = (bf16[1024,1024]{1,0:T(8,128)(2,1)}, bf16[1024,1024]{1,0:T(8,128)(2,1)}, bf16[1024,1024]{1,0:T(8,128)(2,1)}, bf16[1024,1024]{1,0:T(8,128)(2,1)}) custom-call(f32[1024,1024]{1,0:T(8,128)} %bitcast.5, f32[1024,1024]{1,0:T(8,128)} %bitcast.6), custom_call_target="tpu_custom_call" | custom-call | flops 4194304 | bytes 16777216 | tf_op jit(solution)/shard_map/split_roots/pallas_call | solution.py:195
  26.6 0.0 collective-permute-done.2.rest_3_
  26.6 0.0 copy-start
  26.7 0.0 collective-permute-done.1.rest_2_
  26.7 0.0 copy-start.1
  26.7 0.0 collective-permute-done.rest_1_
  26.7 0.0 copy-start.2
  26.7 0.5 copy-done
  27.2 0.0 copy-done.1
  27.3 0.0 copy-done.2
  27.3 2.4 %pack_768.1 = bf16[32,144,128]{2,1,0:T(8,128)(2,1)} custom-call(s32[1,32]{1,0:T(1,128)} %slots_ref.5, bf16[64,16384]{1,0:T(8,128)(2,1)} %q_hbm.5, bf16[64,128]{1,0:T(8,128)(2,1)} %s_hbm.5, f32[8,128]{1,0:T(8,128)} %square_sum.1.rest_0_, f32[8,128]{1,0:T(8,128)} %copy-done.2, f32[8,128]{1,0:T(8,128)} %copy-done.1, f32[8,128]{1,0:T(8,128)} %copy-done), custom_call_target="tpu_custom_call" | custom-call | bytes 3276800 | tf_op jit(solution)/shard_map/pack_768/pallas_call | solution.py:120
  29.6 23.9 %all-to-all-done.1.a_hbm = bf16[32,400,128]{2,1,0:T(8,128)(2,1)} async-done(((bf16[32,400,128]{2,1,0:T(8,128)(2,1)}), bf16[32,400,128]{2,1,0:T(8,128)(2,1)}, u32[]{:S(2)}, u32[]{:S(2)}) %all-to-all-start.1) | async-done | bytes 3276832 | tf_op jit(solution)/shard_map/all_to_all | solution.py:491
  53.5 5.7 %all-to-all-start = ((bf16[32,144,128]{2,1,0:T(8,128)(2,1)}), bf16[32,144,128]{2,1,0:T(8,128)(2,1)}, u32[]{:S(2)}, u32[]{:S(2)}) async-start(bf16[32,144,128]{2,1,0:T(8,128)(2,1)} %pack_768.1), calls=%async_computation | async-start | bytes 2359296 | tf_op jit(solution)/shard_map/all_to_all | solution.py:491
  59.2 15.6 %products.1 = (f32[1024,1024]{1,0:T(8,128)}, f32[1024,768]{1,0:T(8,128)}) custom-call(s32[1,32]{1,0:T(1,128)} %slots_ref.5, bf16[32,400,128]{2,1,0:T(8,128)(2,1)} %all-to-all-done.1.a_hbm, bf16[1024,1024]{1,0:T(8,128)(2,1)} %get-tuple-element.26.l1_hbm, bf16[1024,1024]{1,0:T(8,128)(2,1)} %get-tuple-element.27.l2_hbm, ...), custom_call_target="tpu_custom_call" | custom-call | flops 9663676416 | bytes 20971520 | tf_op jit(solution)/shard_map/products/pallas_call | solution.py:283
  74.8 2.8 %all-to-all-done.a_hbm = bf16[32,144,128]{2,1,0:T(8,128)(2,1)} async-done(((bf16[32,144,128]{2,1,0:T(8,128)(2,1)}), bf16[32,144,128]{2,1,0:T(8,128)(2,1)}, u32[]{:S(2)}, u32[]{:S(2)}) %all-to-all-start) | async-done | bytes 1179680 | tf_op jit(solution)/shard_map/all_to_all | solution.py:491
  77.6 13.0 %graft.1 = (bf16[2048,1024]{1,0:T(8,128)(2,1)}, f32[1024,1024]{1,0:T(8,128)}) custom-call(s32[1,32]{1,0:T(1,128)} %slots_ref.5, bf16[32,144,128]{2,1,0:T(8,128)(2,1)} %all-to-all-done.a_hbm, bf16[1024,1024]{1,0:T(8,128)(2,1)} %get-tuple-element.26.l1_hbm, bf16[1024,1024]{1,0:T(8,128)(2,1)} %get-tuple-element.27.l2_hbm, ...), custom_call_target="tpu_custom_call" | custom-call | flops 3221225472 | bytes 25165824 | tf_op jit(solution)/shard_map/graft/pallas_call | solution.py:407
  90.6 55.4 %all_to_all.15.r_hbm = bf16[32,64,1024]{2,1,0:T(8,128)(2,1)} all-to-all(bf16[32,64,1024]{2,1,0:T(8,128)(2,1)} %bitcast.7), channel_id=1, replica_groups=mesh['fsdp'=32,'grp'=4] {'fsdp'}, dimensions={0} | all-to-all | bytes 8388608 | tf_op jit(solution)/shard_map/all_to_all | solution.py:491
  146.0 3.3 %place.1 = bf16[64,16384]{1,0:T(8,128)(2,1)} custom-call(s32[1,32]{1,0:T(1,128)} %slots_ref.5, bf16[32,64,1024]{2,1,0:T(8,128)(2,1)} %all_to_all.15.r_hbm), custom_call_target="tpu_custom_call" | custom-call | bytes 4194304 | tf_op jit(solution)/shard_map/place/pallas_call | solution.py:465
Async XLA Ops:
  3.7 49.8 %all-to-all-start.1 = ((bf16[32,400,128]{2,1,0:T(8,128)(2,1)}), bf16[32,400,128]{2,1,0:T(8,128)(2,1)}, u32[]{:S(2)}, u32[]{:S(2)}) async-start(bf16[32,400,128]{2,1,0:T(8,128)(2,1)} %pack_0.1), calls=%async_computation.1 | async-start | bytes 6553600 | tf_op jit(solution)/shard_map/all_to_all | solution.py:491
  15.5 11.1 %collective-permute-start.2 = (f32[8,128]{1,0:T(8,128)}, f32[8,128]{1,0:T(8,128)S(1)}, u32[]{:S(2)}, u32[]{:S(2)}) collective-permute-start(f32[8,128]{1,0:T(8,128)} %square_sum.1.rest_0_), channel_id=1, source_target_pairs={{0,3},{1,0},{2,1},{3,2},{4,7},{5,4},{6,5},{7,6},{8,11},{9,8},{10,9... | collective-permute-start | bytes 12296 | tf_op jit(solution)/shard_map/ppermute | solution.py:497
  19.3 7.3 %collective-permute-start.1 = (f32[8,128]{1,0:T(8,128)}, f32[8,128]{1,0:T(8,128)S(1)}, u32[]{:S(2)}, u32[]{:S(2)}) collective-permute-start(f32[8,128]{1,0:T(8,128)} %square_sum.1.rest_0_), channel_id=1, source_target_pairs={{0,2},{1,3},{2,0},{3,1},{4,6},{5,7},{6,4},{7,5},{8,10},{9,11},{10,... | collective-permute-start | bytes 12296 | tf_op jit(solution)/shard_map/ppermute | solution.py:497
  19.3 7.3 %collective-permute-start = (f32[8,128]{1,0:T(8,128)}, f32[8,128]{1,0:T(8,128)S(1)}, u32[]{:S(2)}, u32[]{:S(2)}) collective-permute-start(f32[8,128]{1,0:T(8,128)} %square_sum.1.rest_0_), channel_id=1, source_target_pairs={{0,1},{1,2},{2,3},{3,0},{4,5},{5,6},{6,7},{7,4},{8,9},{9,10},{10,1... | collective-permute-start | bytes 12296 | tf_op jit(solution)/shard_map/ppermute | solution.py:497
  26.6 0.6 copy-start
  26.7 0.6 copy-start.1
  26.7 0.6 copy-start.2
  53.5 24.1 %all-to-all-start = ((bf16[32,144,128]{2,1,0:T(8,128)(2,1)}), bf16[32,144,128]{2,1,0:T(8,128)(2,1)}, u32[]{:S(2)}, u32[]{:S(2)}) async-start(bf16[32,144,128]{2,1,0:T(8,128)(2,1)} %pack_768.1), calls=%async_computation | async-start | bytes 2359296 | tf_op jit(solution)/shard_map/all_to_all | solution.py:491

commit v4 on v3

--- a/solution.py
+++ b/solution.py
@@ -8,7 +8,7 @@
 LANES = 128
 EXTRA = 16
 STEPS = 4
-FINE = 8
+FINE = 16
 F32 = jnp.float32
 BF16 = jnp.bfloat16
 HBM = pl.BlockSpec(memory_space=pltpu.HBM)
@@ -246,9 +246,11 @@
             (r2_hbm.at[deep], r2_ref),
         )
         reads = [pltpu.make_async_copy(s, t, ins.at[k]) for k, (s, t) in enumerate(pairs)]
-        for read in reads:
+        for read in reads[:3]:
             read.start()
         reads[0].wait()
+        for read in reads[3:]:
+            read.start()
         dequant(a_ref, turned, rows, 0, 0, grad_ref, h1, h2)
         for read in reads[1:3]:
             read.wait()
@@ -336,7 +338,11 @@
             )
             return [pltpu.make_async_copy(s, t, ins.at[k, n]) for k, (s, t) in enumerate(pairs)]
 
-        for read in reads:
+        for read in reads[:4]:
+            read.start()
+        for read in reads[:2]:
+            read.wait()
+        for read in reads[4:]:
             read.start()
 
         @pl.loop(0, STEPS)
@@ -344,8 +350,6 @@
             for read in step_reads(n):
                 read.start()
 
-        for read in reads[:2]:
-            read.wait()
         dequant(a_ref, turned, rows, done // LANES, done, grad_ref, h1, h2)
         heads = jnp.sum(sums_ref[...].astype(F32), axis=0)[: EXTRA - 8]
         total = jnp.sum(heads, axis=0, keepdims=True)[:, :1]
@@ -377,8 +381,8 @@
             p_ref[:, at] = product
             psum[...] += fold(product * product)
 
-            @pl.loop(0, block // thin)
-            def _(k):
+            steps = []
+            for k in range(block // thin):
                 line = pl.ds(pl.multiple_of(n * block + k * thin, thin), thin)
                 held = grad_ref[line, :] * clip
                 square = held * held
@@ -387,8 +391,8 @@
                 root = fresh * lax.rsqrt(fresh) + 1e-08
                 inverse = pl.reciprocal(root, approx=True)
                 adam = held * (inverse * (2.0 - root * inverse))
-                asum[...] += fold(adam * adam)
-
+                steps.append(fold(adam * adam))
+            asum[...] += sum(steps)
             fresh_copy(n).start()
 
         norm = jnp.sqrt(everywhere(psum[...]) * (clip * clip) + 1e-12)
@@ -436,26 +440,16 @@
     owners, rows, width = returned.shape
     columns = cols // width
 
-    def body(slots_ref, r_hbm, out_hbm, inverse, out_ref, ins, outs):
+    def body(slots_ref, r_ref, out_hbm, inverse, outs):
         first = lax.div(lax.axis_index("fsdp") * rows, width) * columns
         invert(slots_ref, inverse)
 
-        def here(k):
-            return pl.ds(pl.multiple_of(k * width, width), width)
-
-        def read(k):
-            return pltpu.make_async_copy(r_hbm.at[inverse[first + k]], out_ref.at[:, here(k)], ins.at[k])
-
         def write(k):
-            return pltpu.make_async_copy(out_ref.at[:, here(k)], out_hbm.at[:, here(k)], outs.at[k])
+            here = pl.ds(pl.multiple_of(k * width, width), width)
+            return pltpu.make_async_copy(r_ref.at[inverse[first + k]], out_hbm.at[:, here], outs.at[k])
 
         @pl.loop(0, columns)
         def _(k):
-            read(k).start()
-
-        @pl.loop(0, columns)
-        def _(k):
-            read(k).wait()
             write(k).start()
 
         @pl.loop(0, columns)
@@ -465,15 +459,10 @@
     return pl.pallas_call(
         body,
         out_shape=jax.ShapeDtypeStruct((rows, cols), BF16),
-        in_specs=[SMEM, HBM],
+        in_specs=[SMEM, pl.BlockSpec(memory_space=pltpu.VMEM)],
         out_specs=HBM,
-        scratch_shapes=[
-            pltpu.SMEM((owners,), jnp.int32),
-            pltpu.VMEM((rows, cols), BF16),
-            DMA((columns,)),
-            DMA((columns,)),
-        ],
-        compiler_params=PARAMS,
+        scratch_shapes=[pltpu.SMEM((owners,), jnp.int32), DMA((columns,))],
+        compiler_params=pltpu.CompilerParams(vmem_limit_bytes=12 * 1024 * 1024),
         cost_estimate=cost(0, 4 * rows * cols),
         name="place",
     )(slots, returned)

time: 150 us -> 147 us (0.980)
  Pallas kernels: 47 us -> 44.6 us
where the time goes in v4:
time: 147 us
  blocking collectives  55.1 us (37%)
  Pallas kernels  44.6 us (30%)
  waiting for transfers between devices  26.8 us (18%)
  starting transfers between devices  18.9 us (13%)
    all_to_all x1, blocking collectives, exchange(): lax.all_to_all(value, 'fsdp', split_axis=0, concat_axis=0, tiled=True)  55.1 us
    all_to_all x2, waiting for transfers between devices, exchange(): lax.all_to_all(value, 'fsdp', split_axis=0, concat_axis=0, tiled=True)  26.7 us
    pallas_call x1, Pallas kernels, products(): pl.pallas_call(body, out_shape=[jax.ShapeDtypeStruct(square, F32), jax.Sh...  15.5 us
    all_to_all x2, starting transfers between devices, exchange(): lax.all_to_all(value, 'fsdp', split_axis=0, concat_axis=0, tiled=True)  14.4 us
    pallas_call x1, Pallas kernels, graft(): pl.pallas_call(body, out_shape=[jax.ShapeDtypeStruct((owners * rows, size...  11.9 us
    pallas_call x1, Pallas kernels, split_roots(): pl.pallas_call(body, out_shape=[jax.ShapeDtypeStruct((size, size), BF16)]...  6.59 us
    pallas_call x2, Pallas kernels, pack(): pl.pallas_call(body, out_shape=jax.ShapeDtypeStruct((owners, tall, LANES)...  5.41 us
    ppermute x3, starting transfers between devices, on_device(): lax.ppermute(own, 'grp', [(i, (i + k) % planes) for i in range(planes)])  4.53 us
  transfers between devices with their start and end apart: 5, of which 2 were waited for; matrix products, arithmetic and copies ran while one was open for 0% of the time, Pallas kernels for 19%

profile of v4, /device:TPU:1, one launch (start us, length us, event | category | flops | bytes accessed | tf_op | source)
XLA Modules:
  0.0 146.7 jit_solution(12687364735305115752)
XLA Ops:
  0.6 3.1 %pack_0.1 = bf16[32,400,128]{2,1,0:T(8,128)(2,1)} custom-call(s32[1,32]{1,0:T(1,128)} %slots_ref.5, bf16[64,16384]{1,0:T(8,128)(2,1)} %q_hbm.5, bf16[64,128]{1,0:T(8,128)(2,1)} %s_hbm.5), custom_call_target="tpu_custom_call" | custom-call | bytes 5373952 | tf_op jit(solution)/shard_map/pack_0/pallas_call | solution.py:120
  3.7 8.6 %all-to-all-start.1 = ((bf16[32,400,128]{2,1,0:T(8,128)(2,1)}), bf16[32,400,128]{2,1,0:T(8,128)(2,1)}, u32[]{:S(2)}, u32[]{:S(2)}) async-start(bf16[32,400,128]{2,1,0:T(8,128)(2,1)} %pack_0.1), calls=%async_computation.1 | async-start | bytes 6553600 | tf_op jit(solution)/shard_map/all_to_all | solution.py:480
  12.4 3.1 %square_sum.1.rest_0_ = f32[8,128]{1,0:T(8,128)} custom-call(bf16[64,16384]{1,0:T(8,128)(2,1)} %q_hbm.5, bf16[64,128]{1,0:T(8,128)(2,1)} %s_hbm.5), custom_call_target="tpu_custom_call" | custom-call | flops 3145728 | bytes 2097152 | tf_op jit(solution)/shard_map/square_sum/pallas_call | solution.py:159
  15.5 3.8 %collective-permute-start.2 = (f32[8,128]{1,0:T(8,128)}, f32[8,128]{1,0:T(8,128)S(1)}, u32[]{:S(2)}, u32[]{:S(2)}) collective-permute-start(f32[8,128]{1,0:T(8,128)} %square_sum.1.rest_0_), channel_id=1, source_target_pairs={{0,3},{1,0},{2,1},{3,2},{4,7},{5,4},{6,5},{7,6},{8,11},{9,8},{10,9... | collective-permute-start | bytes 12296 | tf_op jit(solution)/shard_map/ppermute | solution.py:486
  19.3 0.0 collective-permute-start.1
  19.3 0.7 collective-permute-start
  20.0 6.6 %split_roots.1 = (bf16[1024,1024]{1,0:T(8,128)(2,1)}, bf16[1024,1024]{1,0:T(8,128)(2,1)}, bf16[1024,1024]{1,0:T(8,128)(2,1)}, bf16[1024,1024]{1,0:T(8,128)(2,1)}) custom-call(f32[1024,1024]{1,0:T(8,128)} %bitcast.5, f32[1024,1024]{1,0:T(8,128)} %bitcast.6), custom_call_target="tpu_custom_call" | custom-call | flops 4194304 | bytes 16777216 | tf_op jit(solution)/shard_map/split_roots/pallas_call | solution.py:195
  26.6 0.0 collective-permute-done.2.rest_3_
  26.6 0.0 copy-start.1
  26.6 0.0 collective-permute-done.1.rest_2_
  26.7 0.0 collective-permute-done.rest_1_
  26.7 0.5 copy-done.1
  27.2 0.0 copy-done.2
  27.2 0.0 copy-done.3
  27.3 2.3 %pack_768.1 = bf16[32,144,128]{2,1,0:T(8,128)(2,1)} custom-call(s32[1,32]{1,0:T(1,128)} %slots_ref.5, bf16[64,16384]{1,0:T(8,128)(2,1)} %q_hbm.5, bf16[64,128]{1,0:T(8,128)(2,1)} %s_hbm.5, f32[8,128]{1,0:T(8,128)} %square_sum.1.rest_0_, f32[8,128]{1,0:T(8,128)} %copy-done.3, f32[8,128]{1,0:T(8,128)} %copy-done.2, f32[8,128]{1,0:T(8,128)} %copy-done.1), custom_call_target="tpu_custom_call" | custom-call | bytes 3276800 | tf_op jit(solution)/shard_map/pack_768/pallas_call | solution.py:120
  29.6 23.9 %all-to-all-done.1.a_hbm = bf16[32,400,128]{2,1,0:T(8,128)(2,1)} async-done(((bf16[32,400,128]{2,1,0:T(8,128)(2,1)}), bf16[32,400,128]{2,1,0:T(8,128)(2,1)}, u32[]{:S(2)}, u32[]{:S(2)}) %all-to-all-start.1) | async-done | bytes 3276832 | tf_op jit(solution)/shard_map/all_to_all | solution.py:480
  53.5 5.7 %all-to-all-start = ((bf16[32,144,128]{2,1,0:T(8,128)(2,1)}), bf16[32,144,128]{2,1,0:T(8,128)(2,1)}, u32[]{:S(2)}, u32[]{:S(2)}) async-start(bf16[32,144,128]{2,1,0:T(8,128)(2,1)} %pack_768.1), calls=%async_computation | async-start | bytes 2359296 | tf_op jit(solution)/shard_map/all_to_all | solution.py:480
  59.2 15.5 %products.1 = (f32[1024,1024]{1,0:T(8,128)}, f32[1024,768]{1,0:T(8,128)}) custom-call(s32[1,32]{1,0:T(1,128)} %slots_ref.5, bf16[32,400,128]{2,1,0:T(8,128)(2,1)} %all-to-all-done.1.a_hbm, bf16[1024,1024]{1,0:T(8,128)(2,1)} %get-tuple-element.26.l1_hbm, bf16[1024,1024]{1,0:T(8,128)(2,1)} %get-tuple-element.27.l2_hbm, ...), custom_call_target="tpu_custom_call" | custom-call | flops 9663676416 | bytes 20971520 | tf_op jit(solution)/shard_map/products/pallas_call | solution.py:285
  74.8 2.9 %all-to-all-done.a_hbm = bf16[32,144,128]{2,1,0:T(8,128)(2,1)} async-done(((bf16[32,144,128]{2,1,0:T(8,128)(2,1)}), bf16[32,144,128]{2,1,0:T(8,128)(2,1)}, u32[]{:S(2)}, u32[]{:S(2)}) %all-to-all-start) | async-done | bytes 1179680 | tf_op jit(solution)/shard_map/all_to_all | solution.py:480
  77.6 11.9 %graft.1 = (bf16[2048,1024]{1,0:T(8,128)(2,1)}, f32[1024,1024]{1,0:T(8,128)}) custom-call(s32[1,32]{1,0:T(1,128)} %slots_ref.5, bf16[32,144,128]{2,1,0:T(8,128)(2,1)} %all-to-all-done.a_hbm, bf16[1024,1024]{1,0:T(8,128)(2,1)} %get-tuple-element.26.l1_hbm, bf16[1024,1024]{1,0:T(8,128)(2,1)} %get-tuple-element.27.l2_hbm, ...), custom_call_target="tpu_custom_call" | custom-call | flops 3221225472 | bytes 25165824 | tf_op jit(solution)/shard_map/graft/pallas_call | solution.py:411
  89.5 0.0 copy-start
  89.6 55.1 %all_to_all.15.r_ref = bf16[32,64,1024]{2,1,0:T(8,128)(2,1)S(1)} all-to-all(bf16[32,64,1024]{2,1,0:T(8,128)(2,1)} %bitcast.7), channel_id=1, replica_groups=mesh['fsdp'=32,'grp'=4] {'fsdp'}, dimensions={0} | all-to-all | bytes 8388608 | tf_op jit(solution)/shard_map/all_to_all | solution.py:480
  144.7 0.0 copy-done
  144.7 2.0 %place.1 = bf16[64,16384]{1,0:T(8,128)(2,1)} custom-call(s32[1,32]{1,0:T(1,128)S(1)} %copy-done, bf16[32,64,1024]{2,1,0:T(8,128)(2,1)S(1)} %all_to_all.15.r_ref), custom_call_target="tpu_custom_call" | custom-call | bytes 4194304 | tf_op jit(solution)/shard_map/place/pallas_call | solution.py:459
  (2 shorter events, 0.0 us)
Async XLA Ops:
  3.7 49.8 %all-to-all-start.1 = ((bf16[32,400,128]{2,1,0:T(8,128)(2,1)}), bf16[32,400,128]{2,1,0:T(8,128)(2,1)}, u32[]{:S(2)}, u32[]{:S(2)}) async-start(bf16[32,400,128]{2,1,0:T(8,128)(2,1)} %pack_0.1), calls=%async_computation.1 | async-start | bytes 6553600 | tf_op jit(solution)/shard_map/all_to_all | solution.py:480
  15.5 11.1 %collective-permute-start.2 = (f32[8,128]{1,0:T(8,128)}, f32[8,128]{1,0:T(8,128)S(1)}, u32[]{:S(2)}, u32[]{:S(2)}) collective-permute-start(f32[8,128]{1,0:T(8,128)} %square_sum.1.rest_0_), channel_id=1, source_target_pairs={{0,3},{1,0},{2,1},{3,2},{4,7},{5,4},{6,5},{7,6},{8,11},{9,8},{10,9... | collective-permute-start | bytes 12296 | tf_op jit(solution)/shard_map/ppermute | solution.py:486
  19.3 7.3 %collective-permute-start.1 = (f32[8,128]{1,0:T(8,128)}, f32[8,128]{1,0:T(8,128)S(1)}, u32[]{:S(2)}, u32[]{:S(2)}) collective-permute-start(f32[8,128]{1,0:T(8,128)} %square_sum.1.rest_0_), channel_id=1, source_target_pairs={{0,2},{1,3},{2,0},{3,1},{4,6},{5,7},{6,4},{7,5},{8,10},{9,11},{10,... | collective-permute-start | bytes 12296 | tf_op jit(solution)/shard_map/ppermute | solution.py:486
  19.3 7.3 %collective-permute-start = (f32[8,128]{1,0:T(8,128)}, f32[8,128]{1,0:T(8,128)S(1)}, u32[]{:S(2)}, u32[]{:S(2)}) collective-permute-start(f32[8,128]{1,0:T(8,128)} %square_sum.1.rest_0_), channel_id=1, source_target_pairs={{0,1},{1,2},{2,3},{3,0},{4,5},{5,6},{6,7},{7,4},{8,9},{9,10},{10,1... | collective-permute-start | bytes 12296 | tf_op jit(solution)/shard_map/ppermute | solution.py:486
  26.6 0.6 copy-start.1
  26.7 0.6 copy-start.2
  26.7 0.6 copy-start.3
  53.5 24.1 %all-to-all-start = ((bf16[32,144,128]{2,1,0:T(8,128)(2,1)}), bf16[32,144,128]{2,1,0:T(8,128)(2,1)}, u32[]{:S(2)}, u32[]{:S(2)}) async-start(bf16[32,144,128]{2,1,0:T(8,128)(2,1)} %pack_768.1), calls=%async_computation | async-start | bytes 2359296 | tf_op jit(solution)/shard_map/all_to_all | solution.py:480
  89.5 55.1 %copy-start = (s32[1,32]{1,0:T(1,128)S(1)}, s32[1,32]{1,0:T(1,128)}, u32[]{:S(2)}) copy-start(s32[1,32]{1,0:T(1,128)} %slots_ref.5) | copy-start | bytes 388

commit v5 on v4

--- a/solution.py
+++ b/solution.py
@@ -234,7 +234,7 @@
 
     def body(
         slots_ref, a_hbm, l1_hbm, l2_hbm, r1_hbm, r2_hbm, p_hbm, grad_hbm,
-        a_ref, l1_ref, l2_ref, r1_ref, r2_ref, grad_ref, h1, h2, t1, t2, p_ref, turned, ins, outs,
+        a_ref, l1_ref, l2_ref, r_ref, grad_ref, h1, h2, t_ref, p_ref, turned, ins, outs,
     ):
         band = own_band(slots_ref, columns)
         deep = pl.ds(0, part)
@@ -242,8 +242,7 @@
             (a_hbm.at[pl.ds(band * pieces, pieces)], a_ref),
             (l1_hbm, l1_ref),
             (l2_hbm, l2_ref),
-            (r1_hbm.at[deep], r1_ref),
-            (r2_hbm.at[deep], r2_ref),
+            *((src.at[deep], r_ref.at[pl.ds(k * part, part)]) for k, src in enumerate((r1_hbm, r2_hbm, r1_hbm))),
         )
         reads = [pltpu.make_async_copy(s, t, ins.at[k]) for k, (s, t) in enumerate(pairs)]
         for read in reads[:3]:
@@ -261,7 +260,9 @@
         def _(n):
             at = pl.ds(pl.multiple_of(n * block, block), block)
             half = dot(l1_ref[...], h1[:, at]) + (dot(l1_ref[...], h2[:, at]) + dot(l2_ref[...], h1[:, at]))
-            t1[:, at], t2[:, at] = two(half)
+            high, low = two(half)
+            for k, term in enumerate((high, high, low)):
+                t_ref[:, pl.ds(pl.multiple_of(k * part + n * block, block), block)] = term
 
         for read in reads[3:]:
             read.wait()
@@ -273,7 +274,7 @@
         @pl.loop(0, STEPS)
         def _(n):
             at = pl.ds(pl.multiple_of(n * block, block), block)
-            p_ref[:, at] = dot(t1[...], r1_ref[:, at]) + (dot(t1[...], r2_ref[:, at]) + dot(t2[...], r1_ref[:, at]))
+            p_ref[:, at] = dot(t_ref[...], r_ref[:, at])
             p_copy(n).start()
 
         for n in range(STEPS):
@@ -289,10 +290,10 @@
         out_specs=[HBM] * 2,
         scratch_shapes=[pltpu.VMEM((pieces, tall, LANES), BF16)]
         + [pltpu.VMEM(square, BF16)] * 2
-        + [pltpu.VMEM((part, size), BF16)] * 2
-        + [pltpu.VMEM(narrow, F32)]
-        + [pltpu.VMEM(narrow, BF16)] * 4
-        + [pltpu.VMEM(square, F32), pltpu.VMEM((LANES, pieces * EXTRA), F32), DMA((5,)), DMA((STEPS + 1,))],
+        + [pltpu.VMEM((3 * part, size), BF16), pltpu.VMEM(narrow, F32)]
+        + [pltpu.VMEM(narrow, BF16)] * 2
+        + [pltpu.VMEM((size, 3 * part), BF16), pltpu.VMEM(square, F32)]
+        + [pltpu.VMEM((LANES, pieces * EXTRA), F32), DMA((6,)), DMA((STEPS + 1,))],
         compiler_params=PARAMS,
         cost_estimate=cost(12 * size * size * part, 20 * size * size),
         name="products",
@@ -310,7 +311,7 @@
 
     def body(
         slots_ref, a_hbm, l1_hbm, l2_hbm, r1_hbm, r2_hbm, p_hbm, grad_hbm, m_hbm, out_hbm, fresh_hbm,
-        sums_ref, a_ref, l1_ref, l2_ref, r1_ref, r2_ref, p_ref, grad_ref, h1, h2, t1, t2, m_ref, out_ref,
+        sums_ref, a_ref, l1_ref, l2_ref, r_ref, p_ref, grad_ref, h1, h2, t_ref, m_ref, out_ref,
         turned, asum, psum, ins, outs,
     ):
         band = own_band(slots_ref, columns)
@@ -324,8 +325,7 @@
             (a_hbm.at[:, pl.ds(tall - EXTRA, EXTRA)], sums_ref),
             (l1_hbm, l1_ref),
             (l2_hbm, l2_ref),
-            (r1_hbm.at[deep], r1_ref),
-            (r2_hbm.at[deep], r2_ref),
+            *((src.at[deep], r_ref.at[pl.ds(k * part, part)]) for k, src in enumerate((r1_hbm, r2_hbm, r1_hbm))),
         )
         reads = [pltpu.make_async_copy(s, t, ins.at[3, k]) for k, (s, t) in enumerate(pairs)]
 
@@ -360,7 +360,9 @@
         for read in reads[2:4]:
             read.wait()
         half = dot(l1_ref[...], h1[...]) + (dot(l1_ref[...], h2[...]) + dot(l2_ref[...], h1[...]))
-        t1[...], t2[...] = two(half)
+        high, low = two(half)
+        for k, term in enumerate((high, high, low)):
+            t_ref[:, k * part : (k + 1) * part] = term
         for read in reads[4:]:
             read.wait()
 
@@ -376,8 +378,7 @@
             for read in step_reads(n):
                 read.wait()
             at = cut(n)
-            more = dot(t1[...], r1_ref[:, at]) + (dot(t1[...], r2_ref[:, at]) + dot(t2[...], r1_ref[:, at]))
-            product = p_ref[:, at] + more
+            product = p_ref[:, at] + dot(t_ref[...], r_ref[:, at])
             p_ref[:, at] = product
             psum[...] += fold(product * product)
 
@@ -418,16 +419,17 @@
         out_specs=[HBM, HBM],
         scratch_shapes=[pltpu.VMEM((owners, EXTRA, LANES), BF16), pltpu.VMEM((pieces, tall, LANES), BF16)]
         + [pltpu.VMEM(square, BF16)] * 2
-        + [pltpu.VMEM((part, size), BF16)] * 2
+        + [pltpu.VMEM((3 * part, size), BF16)]
         + [pltpu.VMEM(square, F32)] * 2
-        + [pltpu.VMEM((size, part), BF16)] * 4
+        + [pltpu.VMEM((size, part), BF16)] * 2
+        + [pltpu.VMEM((size, 3 * part), BF16)]
         + [
             pltpu.VMEM(square, F32),
             pltpu.VMEM(square, BF16),
             pltpu.VMEM((LANES, pieces * EXTRA), F32),
             pltpu.VMEM((8, LANES), F32),
             pltpu.VMEM((8, LANES), F32),
-            DMA((4, 6)),
+            DMA((4, 7)),
             DMA((2, STEPS)),
         ],
         compiler_params=PARAMS,

time: 147 us -> 148 us (level)
  no operation moved by 1% of the time
where the time goes in v5:
time: 148 us; the launch traced here: 147 us
  blocking collectives  55.4 us (37%)
  Pallas kernels  44.9 us (30%)
  waiting for transfers between devices  26.5 us (18%)
  starting transfers between devices  18.9 us (13%)
    all_to_all x1, blocking collectives, exchange(): lax.all_to_all(value, 'fsdp', split_axis=0, concat_axis=0, tiled=True)  55.4 us
    all_to_all x2, waiting for transfers between devices, exchange(): lax.all_to_all(value, 'fsdp', split_axis=0, concat_axis=0, tiled=True)  26.5 us
    pallas_call x1, Pallas kernels, products(): pl.pallas_call(body, out_shape=[jax.ShapeDtypeStruct(square, F32), jax.Sh...  15.8 us
    all_to_all x2, starting transfers between devices, exchange(): lax.all_to_all(value, 'fsdp', split_axis=0, concat_axis=0, tiled=True)  14.4 us
    pallas_call x1, Pallas kernels, graft(): pl.pallas_call(body, out_shape=[jax.ShapeDtypeStruct((owners * rows, size...  12 us
    pallas_call x1, Pallas kernels, split_roots(): pl.pallas_call(body, out_shape=[jax.ShapeDtypeStruct((size, size), BF16)]...  6.59 us
    pallas_call x2, Pallas kernels, pack(): pl.pallas_call(body, out_shape=jax.ShapeDtypeStruct((owners, tall, LANES)...  5.4 us
    ppermute x3, starting transfers between devices, on_device(): lax.ppermute(own, 'grp', [(i, (i + k) % planes) for i in range(planes)])  4.53 us
  transfers between devices with their start and end apart: 5, of which 2 were waited for; matrix products, arithmetic and copies ran while one was open for 0% of the time, Pallas kernels for 19%

profile of v5, /device:TPU:1, one launch (start us, length us, event | category | flops | bytes accessed | tf_op | source)
XLA Modules:
  0.0 147.0 jit_solution(1684816718939552328)
XLA Ops:
  0.6 3.1 %pack_0.1 = bf16[32,400,128]{2,1,0:T(8,128)(2,1)} custom-call(s32[1,32]{1,0:T(1,128)} %slots_ref.5, bf16[64,16384]{1,0:T(8,128)(2,1)} %q_hbm.5, bf16[64,128]{1,0:T(8,128)(2,1)} %s_hbm.5), custom_call_target="tpu_custom_call" | custom-call | bytes 5373952 | tf_op jit(solution)/shard_map/pack_0/pallas_call | solution.py:120
  3.7 8.6 %all-to-all-start.1 = ((bf16[32,400,128]{2,1,0:T(8,128)(2,1)}), bf16[32,400,128]{2,1,0:T(8,128)(2,1)}, u32[]{:S(2)}, u32[]{:S(2)}) async-start(bf16[32,400,128]{2,1,0:T(8,128)(2,1)} %pack_0.1), calls=%async_computation.1 | async-start | bytes 6553600 | tf_op jit(solution)/shard_map/all_to_all | solution.py:482
  12.4 3.1 %square_sum.1.rest_0_ = f32[8,128]{1,0:T(8,128)} custom-call(bf16[64,16384]{1,0:T(8,128)(2,1)} %q_hbm.5, bf16[64,128]{1,0:T(8,128)(2,1)} %s_hbm.5), custom_call_target="tpu_custom_call" | custom-call | flops 3145728 | bytes 2097152 | tf_op jit(solution)/shard_map/square_sum/pallas_call | solution.py:159
  15.5 3.8 %collective-permute-start.2 = (f32[8,128]{1,0:T(8,128)}, f32[8,128]{1,0:T(8,128)S(1)}, u32[]{:S(2)}, u32[]{:S(2)}) collective-permute-start(f32[8,128]{1,0:T(8,128)} %square_sum.1.rest_0_), channel_id=1, source_target_pairs={{0,3},{1,0},{2,1},{3,2},{4,7},{5,4},{6,5},{7,6},{8,11},{9,8},{10,9... | collective-permute-start | bytes 12296 | tf_op jit(solution)/shard_map/ppermute | solution.py:488
  19.3 0.0 collective-permute-start.1
  19.3 0.7 collective-permute-start
  20.0 6.6 %split_roots.1 = (bf16[1024,1024]{1,0:T(8,128)(2,1)}, bf16[1024,1024]{1,0:T(8,128)(2,1)}, bf16[1024,1024]{1,0:T(8,128)(2,1)}, bf16[1024,1024]{1,0:T(8,128)(2,1)}) custom-call(f32[1024,1024]{1,0:T(8,128)} %bitcast.5, f32[1024,1024]{1,0:T(8,128)} %bitcast.6), custom_call_target="tpu_custom_call" | custom-call | flops 4194304 | bytes 16777216 | tf_op jit(solution)/shard_map/split_roots/pallas_call | solution.py:195
  26.6 0.0 collective-permute-done.2.rest_3_
  26.6 0.0 copy-start.1
  26.6 0.0 collective-permute-done.1.rest_2_
  26.7 0.0 collective-permute-done.rest_1_
  26.7 0.0 copy-start.3
  26.7 0.5 copy-done.1
  27.2 0.0 copy-done.2
  27.2 0.0 copy-done.3
  27.3 2.3 %pack_768.1 = bf16[32,144,128]{2,1,0:T(8,128)(2,1)} custom-call(s32[1,32]{1,0:T(1,128)} %slots_ref.5, bf16[64,16384]{1,0:T(8,128)(2,1)} %q_hbm.5, bf16[64,128]{1,0:T(8,128)(2,1)} %s_hbm.5, f32[8,128]{1,0:T(8,128)} %square_sum.1.rest_0_, f32[8,128]{1,0:T(8,128)} %copy-done.3, f32[8,128]{1,0:T(8,128)} %copy-done.2, f32[8,128]{1,0:T(8,128)} %copy-done.1), custom_call_target="tpu_custom_call" | custom-call | bytes 3276800 | tf_op jit(solution)/shard_map/pack_768/pallas_call | solution.py:120
  29.6 23.9 %all-to-all-done.1.a_hbm = bf16[32,400,128]{2,1,0:T(8,128)(2,1)} async-done(((bf16[32,400,128]{2,1,0:T(8,128)(2,1)}), bf16[32,400,128]{2,1,0:T(8,128)(2,1)}, u32[]{:S(2)}, u32[]{:S(2)}) %all-to-all-start.1) | async-done | bytes 3276832 | tf_op jit(solution)/shard_map/all_to_all | solution.py:482
  53.5 5.7 %all-to-all-start = ((bf16[32,144,128]{2,1,0:T(8,128)(2,1)}), bf16[32,144,128]{2,1,0:T(8,128)(2,1)}, u32[]{:S(2)}, u32[]{:S(2)}) async-start(bf16[32,144,128]{2,1,0:T(8,128)(2,1)} %pack_768.1), calls=%async_computation | async-start | bytes 2359296 | tf_op jit(solution)/shard_map/all_to_all | solution.py:482
  59.2 15.8 %products.1 = (f32[1024,1024]{1,0:T(8,128)}, f32[1024,768]{1,0:T(8,128)}) custom-call(s32[1,32]{1,0:T(1,128)} %slots_ref.5, bf16[32,400,128]{2,1,0:T(8,128)(2,1)} %all-to-all-done.1.a_hbm, bf16[1024,1024]{1,0:T(8,128)(2,1)} %get-tuple-element.26.l1_hbm, bf16[1024,1024]{1,0:T(8,128)(2,1)} %get-tuple-element.27.l2_hbm, ...), custom_call_target="tpu_custom_call" | custom-call | flops 9663676416 | bytes 20971520 | tf_op jit(solution)/shard_map/products/pallas_call | solution.py:286
  75.0 2.6 %all-to-all-done.a_hbm = bf16[32,144,128]{2,1,0:T(8,128)(2,1)} async-done(((bf16[32,144,128]{2,1,0:T(8,128)(2,1)}), bf16[32,144,128]{2,1,0:T(8,128)(2,1)}, u32[]{:S(2)}, u32[]{:S(2)}) %all-to-all-start) | async-done | bytes 1179680 | tf_op jit(solution)/shard_map/all_to_all | solution.py:482
  77.6 12.0 %graft.1 = (bf16[2048,1024]{1,0:T(8,128)(2,1)}, f32[1024,1024]{1,0:T(8,128)}) custom-call(s32[1,32]{1,0:T(1,128)} %slots_ref.5, bf16[32,144,128]{2,1,0:T(8,128)(2,1)} %all-to-all-done.a_hbm, bf16[1024,1024]{1,0:T(8,128)(2,1)} %get-tuple-element.26.l1_hbm, bf16[1024,1024]{1,0:T(8,128)(2,1)} %get-tuple-element.27.l2_hbm, ...), custom_call_target="tpu_custom_call" | custom-call | flops 3221225472 | bytes 25165824 | tf_op jit(solution)/shard_map/graft/pallas_call | solution.py:412
  89.6 0.0 copy-start
  89.6 55.4 %all_to_all.15.r_ref = bf16[32,64,1024]{2,1,0:T(8,128)(2,1)S(1)} all-to-all(bf16[32,64,1024]{2,1,0:T(8,128)(2,1)} %bitcast.7), channel_id=1, replica_groups=mesh['fsdp'=32,'grp'=4] {'fsdp'}, dimensions={0} | all-to-all | bytes 8388608 | tf_op jit(solution)/shard_map/all_to_all | solution.py:482
  145.0 2.0 %place.1 = bf16[64,16384]{1,0:T(8,128)(2,1)} custom-call(s32[1,32]{1,0:T(1,128)S(1)} %copy-done, bf16[32,64,1024]{2,1,0:T(8,128)(2,1)S(1)} %all_to_all.15.r_ref), custom_call_target="tpu_custom_call" | custom-call | bytes 4194304 | tf_op jit(solution)/shard_map/place/pallas_call | solution.py:461
  (2 shorter events, 0.0 us)
Async XLA Ops:
  3.7 49.8 %all-to-all-start.1 = ((bf16[32,400,128]{2,1,0:T(8,128)(2,1)}), bf16[32,400,128]{2,1,0:T(8,128)(2,1)}, u32[]{:S(2)}, u32[]{:S(2)}) async-start(bf16[32,400,128]{2,1,0:T(8,128)(2,1)} %pack_0.1), calls=%async_computation.1 | async-start | bytes 6553600 | tf_op jit(solution)/shard_map/all_to_all | solution.py:482
  15.5 11.1 %collective-permute-start.2 = (f32[8,128]{1,0:T(8,128)}, f32[8,128]{1,0:T(8,128)S(1)}, u32[]{:S(2)}, u32[]{:S(2)}) collective-permute-start(f32[8,128]{1,0:T(8,128)} %square_sum.1.rest_0_), channel_id=1, source_target_pairs={{0,3},{1,0},{2,1},{3,2},{4,7},{5,4},{6,5},{7,6},{8,11},{9,8},{10,9... | collective-permute-start | bytes 12296 | tf_op jit(solution)/shard_map/ppermute | solution.py:488
  19.3 7.3 %collective-permute-start.1 = (f32[8,128]{1,0:T(8,128)}, f32[8,128]{1,0:T(8,128)S(1)}, u32[]{:S(2)}, u32[]{:S(2)}) collective-permute-start(f32[8,128]{1,0:T(8,128)} %square_sum.1.rest_0_), channel_id=1, source_target_pairs={{0,2},{1,3},{2,0},{3,1},{4,6},{5,7},{6,4},{7,5},{8,10},{9,11},{10,... | collective-permute-start | bytes 12296 | tf_op jit(solution)/shard_map/ppermute | solution.py:488
  19.3 7.3 %collective-permute-start = (f32[8,128]{1,0:T(8,128)}, f32[8,128]{1,0:T(8,128)S(1)}, u32[]{:S(2)}, u32[]{:S(2)}) collective-permute-start(f32[8,128]{1,0:T(8,128)} %square_sum.1.rest_0_), channel_id=1, source_target_pairs={{0,1},{1,2},{2,3},{3,0},{4,5},{5,6},{6,7},{7,4},{8,9},{9,10},{10,1... | collective-permute-start | bytes 12296 | tf_op jit(solution)/shard_map/ppermute | solution.py:488
  26.6 0.6 copy-start.1
  26.7 0.6 copy-start.2
  26.7 0.6 copy-start.3
  53.5 24.1 %all-to-all-start = ((bf16[32,144,128]{2,1,0:T(8,128)(2,1)}), bf16[32,144,128]{2,1,0:T(8,128)(2,1)}, u32[]{:S(2)}, u32[]{:S(2)}) async-start(bf16[32,144,128]{2,1,0:T(8,128)(2,1)} %pack_768.1), calls=%async_computation | async-start | bytes 2359296 | tf_op jit(solution)/shard_map/all_to_all | solution.py:482
  89.6 55.4 %copy-start = (s32[1,32]{1,0:T(1,128)S(1)}, s32[1,32]{1,0:T(1,128)}, u32[]{:S(2)}) copy-start(s32[1,32]{1,0:T(1,128)} %slots_ref.5) | copy-start | bytes 388

commit v6 on v4

--- a/solution.py
+++ b/solution.py
@@ -210,16 +210,16 @@
     )(left, right)
 
 
-def dequant(a_ref, turned, rows, group, at_lane, grad_ref, h1, h2):
-    pieces, tall, _ = a_ref.shape
+def dequant(a_ref, base, pieces, turned, rows, group, at_lane, grad_ref, h1, h2):
+    tall = a_ref.shape[1]
     here = (tall - EXTRA) // rows
-    scales = a_ref[:, here * rows :, :].astype(F32).reshape(pieces * EXTRA, LANES)
+    scales = a_ref[pl.ds(base, pieces), here * rows :, :].astype(F32).reshape(pieces * EXTRA, LANES)
     turned[...] = scales.T
     for piece in range(pieces):
         at = slice(piece * rows, (piece + 1) * rows)
         for j in range(here):
             column = piece * EXTRA + EXTRA - 8 + group + j
-            grad = a_ref[piece, j * rows : (j + 1) * rows, :].astype(F32) * turned[:rows, column : column + 1]
+            grad = a_ref[base + piece, j * rows : (j + 1) * rows, :].astype(F32) * turned[:rows, column : column + 1]
             grad_ref[at, at_lane + j * LANES : at_lane + (j + 1) * LANES] = grad
             lanes = slice(j * LANES, (j + 1) * LANES)
             h1[at, lanes], h2[at, lanes] = two(grad)
@@ -251,7 +251,7 @@
         reads[0].wait()
         for read in reads[3:]:
             read.start()
-        dequant(a_ref, turned, rows, 0, 0, grad_ref, h1, h2)
+        dequant(a_ref, 0, pieces, turned, rows, 0, 0, grad_ref, h1, h2)
         for read in reads[1:3]:
             read.wait()
         keep = pltpu.make_async_copy(grad_ref, grad_hbm, outs.at[STEPS])
@@ -309,19 +309,18 @@
     thin = size // FINE
 
     def body(
-        slots_ref, a_hbm, l1_hbm, l2_hbm, r1_hbm, r2_hbm, p_hbm, grad_hbm, m_hbm, out_hbm, fresh_hbm,
-        sums_ref, a_ref, l1_ref, l2_ref, r1_ref, r2_ref, p_ref, grad_ref, h1, h2, t1, t2, m_ref, out_ref,
+        slots_hbm, a_hbm, l1_hbm, l2_hbm, r1_hbm, r2_hbm, p_hbm, grad_hbm, m_hbm, out_hbm, fresh_hbm,
+        slots_ref, a_ref, l1_ref, l2_ref, r1_ref, r2_ref, p_ref, grad_ref, h1, h2, t1, t2, m_ref, out_ref,
         turned, asum, psum, ins, outs,
     ):
-        band = own_band(slots_ref, columns)
         deep = pl.ds(done, part)
 
         def cut(n):
             return pl.ds(pl.multiple_of(n * block, block), block)
 
         pairs = (
-            (a_hbm.at[pl.ds(band * pieces, pieces)], a_ref),
-            (a_hbm.at[:, pl.ds(tall - EXTRA, EXTRA)], sums_ref),
+            (slots_hbm, slots_ref),
+            (a_hbm, a_ref),
             (l1_hbm, l1_ref),
             (l2_hbm, l2_ref),
             (r1_hbm.at[deep], r1_ref),
@@ -329,29 +328,33 @@
         )
         reads = [pltpu.make_async_copy(s, t, ins.at[3, k]) for k, (s, t) in enumerate(pairs)]
 
-        def step_reads(n):
+        def p_read(n):
             at = cut(n)
-            pairs = (
-                (p_hbm.at[:, at], p_ref.at[:, at]),
-                (grad_hbm.at[at], grad_ref.at[at, pl.ds(0, done)]),
-                (m_hbm.at[at], m_ref.at[at]),
-            )
-            return [pltpu.make_async_copy(s, t, ins.at[k, n]) for k, (s, t) in enumerate(pairs)]
+            return pltpu.make_async_copy(p_hbm.at[:, at], p_ref.at[:, at], ins.at[0, n])
+
+        def adam_reads(n):
+            at = cut(n)
+            pairs = ((grad_hbm.at[at], grad_ref.at[at, pl.ds(0, done)]), (m_hbm.at[at], m_ref.at[at]))
+            return [pltpu.make_async_copy(s, t, ins.at[1 + k, n]) for k, (s, t) in enumerate(pairs)]
 
         for read in reads[:4]:
             read.start()
         for read in reads[:2]:
             read.wait()
-        for read in reads[4:]:
-            read.start()
-
-        @pl.loop(0, STEPS)
+        band = own_band(slots_ref, columns)
+        base = band * pieces
+
+        for read in reads[4:] + adam_reads(0):
+            read.start()
+
+        @pl.loop(1, STEPS)
         def _(n):
-            for read in step_reads(n):
+            for read in [p_read(n), *adam_reads(n)]:
                 read.start()
 
-        dequant(a_ref, turned, rows, done // LANES, done, grad_ref, h1, h2)
-        heads = jnp.sum(sums_ref[...].astype(F32), axis=0)[: EXTRA - 8]
+        p_read(0).start()
+        dequant(a_ref, base, pieces, turned, rows, done // LANES, done, grad_ref, h1, h2)
+        heads = jnp.sum(a_ref[:, tall - EXTRA :, :].astype(F32), axis=0)[: EXTRA - 8]
         total = jnp.sum(heads, axis=0, keepdims=True)[:, :1]
         bound = 0.5 * jnp.sqrt(jnp.full((1, 1), entries, F32)) / jnp.sqrt(jnp.where(total > 0, total, 1.0))
         clip = jnp.where(total > 0, jnp.minimum(bound, 1.0), 1.0)
@@ -359,10 +362,6 @@
         psum[...] = jnp.zeros_like(psum)
         for read in reads[2:4]:
             read.wait()
-        half = dot(l1_ref[...], h1[...]) + (dot(l1_ref[...], h2[...]) + dot(l2_ref[...], h1[...]))
-        t1[...], t2[...] = two(half)
-        for read in reads[4:]:
-            read.wait()
 
         def fresh_copy(n):
             return pltpu.make_async_copy(m_ref.at[cut(n)], fresh_hbm.at[cut(n)], outs.at[0, n])
@@ -371,16 +370,9 @@
             to = pl.ds(pl.multiple_of(band * size + n * block, block), block)
             return pltpu.make_async_copy(out_ref.at[cut(n)], out_hbm.at[to], outs.at[1, n])
 
-        @pl.loop(0, STEPS)
-        def _(n):
-            for read in step_reads(n):
+        def adam(n):
+            for read in adam_reads(n):
                 read.wait()
-            at = cut(n)
-            more = dot(t1[...], r1_ref[:, at]) + (dot(t1[...], r2_ref[:, at]) + dot(t2[...], r1_ref[:, at]))
-            product = p_ref[:, at] + more
-            p_ref[:, at] = product
-            psum[...] += fold(product * product)
-
             steps = []
             for k in range(block // thin):
                 line = pl.ds(pl.multiple_of(n * block + k * thin, thin), thin)
@@ -390,11 +382,32 @@
                 m_ref[line, :] = fresh
                 root = fresh * lax.rsqrt(fresh) + 1e-08
                 inverse = pl.reciprocal(root, approx=True)
-                adam = held * (inverse * (2.0 - root * inverse))
-                steps.append(fold(adam * adam))
+                ratios = held * (inverse * (2.0 - root * inverse))
+                steps.append(fold(ratios * ratios))
             asum[...] += sum(steps)
             fresh_copy(n).start()
 
+        half = dot(l1_ref[...], h1[...])
+        adam(0)
+        half = half + (dot(l1_ref[...], h2[...]) + dot(l2_ref[...], h1[...]))
+        t1[...], t2[...] = two(half)
+        for read in reads[4:]:
+            read.wait()
+
+        def second(n):
+            p_read(n).wait()
+            at = cut(n)
+            more = dot(t1[...], r1_ref[:, at]) + (dot(t1[...], r2_ref[:, at]) + dot(t2[...], r1_ref[:, at]))
+            product = p_ref[:, at] + more
+            p_ref[:, at] = product
+            psum[...] += fold(product * product)
+
+        @pl.loop(1, STEPS)
+        def _(n):
+            second(n)
+            adam(n)
+
+        second(0)
         norm = jnp.sqrt(everywhere(psum[...]) * (clip * clip) + 1e-12)
         ratio = clip * (jnp.sqrt(everywhere(asum[...])) / norm)
 
@@ -414,9 +427,9 @@
             jax.ShapeDtypeStruct((owners * rows, size), BF16),
             jax.ShapeDtypeStruct(square, F32),
         ],
-        in_specs=[SMEM] + [HBM] * 8,
+        in_specs=[HBM] * 9,
         out_specs=[HBM, HBM],
-        scratch_shapes=[pltpu.VMEM((owners, EXTRA, LANES), BF16), pltpu.VMEM((pieces, tall, LANES), BF16)]
+        scratch_shapes=[pltpu.SMEM(slots.shape, jnp.int32), pltpu.VMEM((owners, tall, LANES), BF16)]
         + [pltpu.VMEM(square, BF16)] * 2
         + [pltpu.VMEM((part, size), BF16)] * 2
         + [pltpu.VMEM(square, F32)] * 2

time: 147 us -> 148 us (level)
  no operation moved by 1% of the time
where the time goes in v6:
time: 148 us
  blocking collectives  55.2 us (37%)
  Pallas kernels  45.4 us (31%)
  waiting for transfers between devices  26.7 us (18%)
  starting transfers between devices  18.9 us (13%)
    all_to_all x1, blocking collectives, exchange(): lax.all_to_all(value, 'fsdp', split_axis=0, concat_axis=0, tiled=True)  55.2 us
    all_to_all x2, waiting for transfers between devices, exchange(): lax.all_to_all(value, 'fsdp', split_axis=0, concat_axis=0, tiled=True)  26.7 us
    pallas_call x1, Pallas kernels, products(): pl.pallas_call(body, out_shape=[jax.ShapeDtypeStruct(square, F32), jax.Sh...  15.5 us
    all_to_all x2, starting transfers between devices, exchange(): lax.all_to_all(value, 'fsdp', split_axis=0, concat_axis=0, tiled=True)  14.4 us
    pallas_call x1, Pallas kernels, graft(): pl.pallas_call(body, out_shape=[jax.ShapeDtypeStruct((owners * rows, size...  12.7 us
    pallas_call x1, Pallas kernels, split_roots(): pl.pallas_call(body, out_shape=[jax.ShapeDtypeStruct((size, size), BF16)]...  6.59 us
    pallas_call x2, Pallas kernels, pack(): pl.pallas_call(body, out_shape=jax.ShapeDtypeStruct((owners, tall, LANES)...  5.41 us
    ppermute x3, starting transfers between devices, on_device(): lax.ppermute(own, 'grp', [(i, (i + k) % planes) for i in range(planes)])  4.53 us
  transfers between devices with their start and end apart: 5, of which 2 were waited for; matrix products, arithmetic and copies ran while one was open for 0% of the time, Pallas kernels for 19%

profile of v6, /device:TPU:1, one launch (start us, length us, event | category | flops | bytes accessed | tf_op | source)
XLA Modules:
  0.0 147.8 jit_solution(10878736582383262334)
XLA Ops:
  0.6 3.1 %pack_0.1 = bf16[32,400,128]{2,1,0:T(8,128)(2,1)} custom-call(s32[1,32]{1,0:T(1,128)} %slots_ref.3, bf16[64,16384]{1,0:T(8,128)(2,1)} %q_hbm.5, bf16[64,128]{1,0:T(8,128)(2,1)} %s_hbm.5), custom_call_target="tpu_custom_call" | custom-call | bytes 5373952 | tf_op jit(solution)/shard_map/pack_0/pallas_call | solution.py:120
  3.7 8.6 %all-to-all-start.1 = ((bf16[32,400,128]{2,1,0:T(8,128)(2,1)}), bf16[32,400,128]{2,1,0:T(8,128)(2,1)}, u32[]{:S(2)}, u32[]{:S(2)}) async-start(bf16[32,400,128]{2,1,0:T(8,128)(2,1)} %pack_0.1), calls=%async_computation.1 | async-start | bytes 6553600 | tf_op jit(solution)/shard_map/all_to_all | solution.py:493
  12.4 3.1 %square_sum.1.rest_0_ = f32[8,128]{1,0:T(8,128)} custom-call(bf16[64,16384]{1,0:T(8,128)(2,1)} %q_hbm.5, bf16[64,128]{1,0:T(8,128)(2,1)} %s_hbm.5), custom_call_target="tpu_custom_call" | custom-call | flops 3145728 | bytes 2097152 | tf_op jit(solution)/shard_map/square_sum/pallas_call | solution.py:159
  15.5 3.8 %collective-permute-start.2 = (f32[8,128]{1,0:T(8,128)}, f32[8,128]{1,0:T(8,128)S(1)}, u32[]{:S(2)}, u32[]{:S(2)}) collective-permute-start(f32[8,128]{1,0:T(8,128)} %square_sum.1.rest_0_), channel_id=1, source_target_pairs={{0,3},{1,0},{2,1},{3,2},{4,7},{5,4},{6,5},{7,6},{8,11},{9,8},{10,9... | collective-permute-start | bytes 12296 | tf_op jit(solution)/shard_map/ppermute | solution.py:499
  19.3 0.0 collective-permute-start.1
  19.3 0.7 collective-permute-start
  20.0 6.6 %split_roots.1 = (bf16[1024,1024]{1,0:T(8,128)(2,1)}, bf16[1024,1024]{1,0:T(8,128)(2,1)}, bf16[1024,1024]{1,0:T(8,128)(2,1)}, bf16[1024,1024]{1,0:T(8,128)(2,1)}) custom-call(f32[1024,1024]{1,0:T(8,128)} %bitcast.5, f32[1024,1024]{1,0:T(8,128)} %bitcast.6), custom_call_target="tpu_custom_call" | custom-call | flops 4194304 | bytes 16777216 | tf_op jit(solution)/shard_map/split_roots/pallas_call | solution.py:195
  26.6 0.0 collective-permute-done.2.rest_3_
  26.6 0.0 copy-start.1
  26.6 0.0 collective-permute-done.1.rest_2_
  26.7 0.0 collective-permute-done.rest_1_
  26.7 0.5 copy-done.1
  27.2 0.0 copy-done.2
  27.2 0.0 copy-done.3
  27.3 2.3 %pack_768.1 = bf16[32,144,128]{2,1,0:T(8,128)(2,1)} custom-call(s32[1,32]{1,0:T(1,128)} %slots_ref.3, bf16[64,16384]{1,0:T(8,128)(2,1)} %q_hbm.5, bf16[64,128]{1,0:T(8,128)(2,1)} %s_hbm.5, f32[8,128]{1,0:T(8,128)} %square_sum.1.rest_0_, f32[8,128]{1,0:T(8,128)} %copy-done.3, f32[8,128]{1,0:T(8,128)} %copy-done.2, f32[8,128]{1,0:T(8,128)} %copy-done.1), custom_call_target="tpu_custom_call" | custom-call | bytes 3276800 | tf_op jit(solution)/shard_map/pack_768/pallas_call | solution.py:120
  29.6 23.9 %all-to-all-done.1.a_hbm = bf16[32,400,128]{2,1,0:T(8,128)(2,1)} async-done(((bf16[32,400,128]{2,1,0:T(8,128)(2,1)}), bf16[32,400,128]{2,1,0:T(8,128)(2,1)}, u32[]{:S(2)}, u32[]{:S(2)}) %all-to-all-start.1) | async-done | bytes 3276832 | tf_op jit(solution)/shard_map/all_to_all | solution.py:493
  53.5 5.7 %all-to-all-start = ((bf16[32,144,128]{2,1,0:T(8,128)(2,1)}), bf16[32,144,128]{2,1,0:T(8,128)(2,1)}, u32[]{:S(2)}, u32[]{:S(2)}) async-start(bf16[32,144,128]{2,1,0:T(8,128)(2,1)} %pack_768.1), calls=%async_computation | async-start | bytes 2359296 | tf_op jit(solution)/shard_map/all_to_all | solution.py:493
  59.2 15.5 %products.1 = (f32[1024,1024]{1,0:T(8,128)}, f32[1024,768]{1,0:T(8,128)}) custom-call(s32[1,32]{1,0:T(1,128)} %slots_ref.3, bf16[32,400,128]{2,1,0:T(8,128)(2,1)} %all-to-all-done.1.a_hbm, bf16[1024,1024]{1,0:T(8,128)(2,1)} %get-tuple-element.26.l1_hbm, bf16[1024,1024]{1,0:T(8,128)(2,1)} %get-tuple-element.27.l2_hbm, ...), custom_call_target="tpu_custom_call" | custom-call | flops 9663676416 | bytes 20971520 | tf_op jit(solution)/shard_map/products/pallas_call | solution.py:285
  74.8 2.9 %all-to-all-done.a_hbm = bf16[32,144,128]{2,1,0:T(8,128)(2,1)} async-done(((bf16[32,144,128]{2,1,0:T(8,128)(2,1)}), bf16[32,144,128]{2,1,0:T(8,128)(2,1)}, u32[]{:S(2)}, u32[]{:S(2)}) %all-to-all-start) | async-done | bytes 1179680 | tf_op jit(solution)/shard_map/all_to_all | solution.py:493
  77.6 12.7 %graft.1 = (bf16[2048,1024]{1,0:T(8,128)(2,1)}, f32[1024,1024]{1,0:T(8,128)}) custom-call(s32[1,32]{1,0:T(1,128)} %slots_ref.3, bf16[32,144,128]{2,1,0:T(8,128)(2,1)} %all-to-all-done.a_hbm, bf16[1024,1024]{1,0:T(8,128)(2,1)} %get-tuple-element.26.l1_hbm, bf16[1024,1024]{1,0:T(8,128)(2,1)} %get-tuple-element.27.l2_hbm, ...), custom_call_target="tpu_custom_call" | custom-call | flops 3221225472 | bytes 25165824 | tf_op jit(solution)/shard_map/graft/pallas_call | solution.py:424
  90.4 0.0 copy-start
  90.4 55.2 %all_to_all.15.r_ref = bf16[32,64,1024]{2,1,0:T(8,128)(2,1)S(1)} all-to-all(bf16[32,64,1024]{2,1,0:T(8,128)(2,1)} %bitcast.7), channel_id=1, replica_groups=mesh['fsdp'=32,'grp'=4] {'fsdp'}, dimensions={0} | all-to-all | bytes 8388608 | tf_op jit(solution)/shard_map/all_to_all | solution.py:493
  145.6 0.0 copy-done
  145.6 2.0 %place.1 = bf16[64,16384]{1,0:T(8,128)(2,1)} custom-call(s32[1,32]{1,0:T(1,128)S(1)} %copy-done, bf16[32,64,1024]{2,1,0:T(8,128)(2,1)S(1)} %all_to_all.15.r_ref), custom_call_target="tpu_custom_call" | custom-call | bytes 4194304 | tf_op jit(solution)/shard_map/place/pallas_call | solution.py:472
  (2 shorter events, 0.0 us)
Async XLA Ops:
  3.7 49.8 %all-to-all-start.1 = ((bf16[32,400,128]{2,1,0:T(8,128)(2,1)}), bf16[32,400,128]{2,1,0:T(8,128)(2,1)}, u32[]{:S(2)}, u32[]{:S(2)}) async-start(bf16[32,400,128]{2,1,0:T(8,128)(2,1)} %pack_0.1), calls=%async_computation.1 | async-start | bytes 6553600 | tf_op jit(solution)/shard_map/all_to_all | solution.py:493
  15.5 11.1 %collective-permute-start.2 = (f32[8,128]{1,0:T(8,128)}, f32[8,128]{1,0:T(8,128)S(1)}, u32[]{:S(2)}, u32[]{:S(2)}) collective-permute-start(f32[8,128]{1,0:T(8,128)} %square_sum.1.rest_0_), channel_id=1, source_target_pairs={{0,3},{1,0},{2,1},{3,2},{4,7},{5,4},{6,5},{7,6},{8,11},{9,8},{10,9... | collective-permute-start | bytes 12296 | tf_op jit(solution)/shard_map/ppermute | solution.py:499
  19.3 7.3 %collective-permute-start.1 = (f32[8,128]{1,0:T(8,128)}, f32[8,128]{1,0:T(8,128)S(1)}, u32[]{:S(2)}, u32[]{:S(2)}) collective-permute-start(f32[8,128]{1,0:T(8,128)} %square_sum.1.rest_0_), channel_id=1, source_target_pairs={{0,2},{1,3},{2,0},{3,1},{4,6},{5,7},{6,4},{7,5},{8,10},{9,11},{10,... | collective-permute-start | bytes 12296 | tf_op jit(solution)/shard_map/ppermute | solution.py:499
  19.3 7.3 %collective-permute-start = (f32[8,128]{1,0:T(8,128)}, f32[8,128]{1,0:T(8,128)S(1)}, u32[]{:S(2)}, u32[]{:S(2)}) collective-permute-start(f32[8,128]{1,0:T(8,128)} %square_sum.1.rest_0_), channel_id=1, source_target_pairs={{0,1},{1,2},{2,3},{3,0},{4,5},{5,6},{6,7},{7,4},{8,9},{9,10},{10,1... | collective-permute-start | bytes 12296 | tf_op jit(solution)/shard_map/ppermute | solution.py:499
  26.6 0.6 copy-start.1
  26.7 0.6 copy-start.2
  26.7 0.6 copy-start.3
  53.5 24.1 %all-to-all-start = ((bf16[32,144,128]{2,1,0:T(8,128)(2,1)}), bf16[32,144,128]{2,1,0:T(8,128)(2,1)}, u32[]{:S(2)}, u32[]{:S(2)}) async-start(bf16[32,144,128]{2,1,0:T(8,128)(2,1)} %pack_768.1), calls=%async_computation | async-start | bytes 2359296 | tf_op jit(solution)/shard_map/all_to_all | solution.py:493
  90.4 55.2 %copy-start = (s32[1,32]{1,0:T(1,128)S(1)}, s32[1,32]{1,0:T(1,128)}, u32[]{:S(2)}) copy-start(s32[1,32]{1,0:T(1,128)} %slots_ref.3) | copy-start | bytes 388

commit v7 on v6

--- a/solution.py
+++ b/solution.py
@@ -344,15 +344,14 @@
         band = own_band(slots_ref, columns)
         base = band * pieces
 
-        for read in reads[4:] + adam_reads(0):
-            read.start()
-
-        @pl.loop(1, STEPS)
+        for read in reads[4:]:
+            read.start()
+
+        @pl.loop(0, STEPS)
         def _(n):
             for read in [p_read(n), *adam_reads(n)]:
                 read.start()
 
-        p_read(0).start()
         dequant(a_ref, base, pieces, turned, rows, done // LANES, done, grad_ref, h1, h2)
         heads = jnp.sum(a_ref[:, tall - EXTRA :, :].astype(F32), axis=0)[: EXTRA - 8]
         total = jnp.sum(heads, axis=0, keepdims=True)[:, :1]
@@ -387,27 +386,21 @@
             asum[...] += sum(steps)
             fresh_copy(n).start()
 
-        half = dot(l1_ref[...], h1[...])
-        adam(0)
-        half = half + (dot(l1_ref[...], h2[...]) + dot(l2_ref[...], h1[...]))
+        half = dot(l1_ref[...], h1[...]) + (dot(l1_ref[...], h2[...]) + dot(l2_ref[...], h1[...]))
         t1[...], t2[...] = two(half)
         for read in reads[4:]:
             read.wait()
 
-        def second(n):
+        @pl.loop(0, STEPS)
+        def _(n):
             p_read(n).wait()
             at = cut(n)
             more = dot(t1[...], r1_ref[:, at]) + (dot(t1[...], r2_ref[:, at]) + dot(t2[...], r1_ref[:, at]))
             product = p_ref[:, at] + more
             p_ref[:, at] = product
             psum[...] += fold(product * product)
-
-        @pl.loop(1, STEPS)
-        def _(n):
-            second(n)
             adam(n)
 
-        second(0)
         norm = jnp.sqrt(everywhere(psum[...]) * (clip * clip) + 1e-12)
         ratio = clip * (jnp.sqrt(everywhere(asum[...])) / norm)
 

time: 148 us -> 147 us (level)
  no operation moved by 1% of the time
where the time goes in v7:
time: 147 us
  blocking collectives  55.2 us (38%)
  Pallas kernels  44.5 us (30%)
  waiting for transfers between devices  26.8 us (18%)
  starting transfers between devices  18.9 us (13%)
    all_to_all x1, blocking collectives, exchange(): lax.all_to_all(value, 'fsdp', split_axis=0, concat_axis=0, tiled=True)  55.2 us
    all_to_all x2, waiting for transfers between devices, exchange(): lax.all_to_all(value, 'fsdp', split_axis=0, concat_axis=0, tiled=True)  26.7 us
    pallas_call x1, Pallas kernels, products(): pl.pallas_call(body, out_shape=[jax.ShapeDtypeStruct(square, F32), jax.Sh...  15.5 us
    all_to_all x2, starting transfers between devices, exchange(): lax.all_to_all(value, 'fsdp', split_axis=0, concat_axis=0, tiled=True)  14.4 us
    pallas_call x1, Pallas kernels, graft(): pl.pallas_call(body, out_shape=[jax.ShapeDtypeStruct((owners * rows, size...  11.8 us
    pallas_call x1, Pallas kernels, split_roots(): pl.pallas_call(body, out_shape=[jax.ShapeDtypeStruct((size, size), BF16)]...  6.59 us
    pallas_call x2, Pallas kernels, pack(): pl.pallas_call(body, out_shape=jax.ShapeDtypeStruct((owners, tall, LANES)...  5.4 us
    ppermute x3, starting transfers between devices, on_device(): lax.ppermute(own, 'grp', [(i, (i + k) % planes) for i in range(planes)])  4.53 us
  transfers between devices with their start and end apart: 5, of which 2 were waited for; matrix products, arithmetic and copies ran while one was open for 0% of the time, Pallas kernels for 19%

profile of v7, /device:TPU:1, one launch (start us, length us, event | category | flops | bytes accessed | tf_op | source)
XLA Modules:
  0.0 146.6 jit_solution(5491425758226012929)
XLA Ops:
  0.6 3.1 %pack_0.1 = bf16[32,400,128]{2,1,0:T(8,128)(2,1)} custom-call(s32[1,32]{1,0:T(1,128)} %slots_ref.3, bf16[64,16384]{1,0:T(8,128)(2,1)} %q_hbm.5, bf16[64,128]{1,0:T(8,128)(2,1)} %s_hbm.5), custom_call_target="tpu_custom_call" | custom-call | bytes 5373952 | tf_op jit(solution)/shard_map/pack_0/pallas_call | solution.py:120
  3.7 8.6 %all-to-all-start.1 = ((bf16[32,400,128]{2,1,0:T(8,128)(2,1)}), bf16[32,400,128]{2,1,0:T(8,128)(2,1)}, u32[]{:S(2)}, u32[]{:S(2)}) async-start(bf16[32,400,128]{2,1,0:T(8,128)(2,1)} %pack_0.1), calls=%async_computation.1 | async-start | bytes 6553600 | tf_op jit(solution)/shard_map/all_to_all | solution.py:486
  12.4 3.1 %square_sum.1.rest_0_ = f32[8,128]{1,0:T(8,128)} custom-call(bf16[64,16384]{1,0:T(8,128)(2,1)} %q_hbm.5, bf16[64,128]{1,0:T(8,128)(2,1)} %s_hbm.5), custom_call_target="tpu_custom_call" | custom-call | flops 3145728 | bytes 2097152 | tf_op jit(solution)/shard_map/square_sum/pallas_call | solution.py:159
  15.5 3.8 %collective-permute-start.2 = (f32[8,128]{1,0:T(8,128)}, f32[8,128]{1,0:T(8,128)S(1)}, u32[]{:S(2)}, u32[]{:S(2)}) collective-permute-start(f32[8,128]{1,0:T(8,128)} %square_sum.1.rest_0_), channel_id=1, source_target_pairs={{0,3},{1,0},{2,1},{3,2},{4,7},{5,4},{6,5},{7,6},{8,11},{9,8},{10,9... | collective-permute-start | bytes 12296 | tf_op jit(solution)/shard_map/ppermute | solution.py:492
  19.3 0.0 collective-permute-start.1
  19.3 0.7 collective-permute-start
  20.0 6.6 %split_roots.1 = (bf16[1024,1024]{1,0:T(8,128)(2,1)}, bf16[1024,1024]{1,0:T(8,128)(2,1)}, bf16[1024,1024]{1,0:T(8,128)(2,1)}, bf16[1024,1024]{1,0:T(8,128)(2,1)}) custom-call(f32[1024,1024]{1,0:T(8,128)} %bitcast.5, f32[1024,1024]{1,0:T(8,128)} %bitcast.6), custom_call_target="tpu_custom_call" | custom-call | flops 4194304 | bytes 16777216 | tf_op jit(solution)/shard_map/split_roots/pallas_call | solution.py:195
  26.6 0.0 collective-permute-done.2.rest_3_
  26.6 0.0 copy-start.1
  26.6 0.0 collective-permute-done.1.rest_2_
  26.7 0.0 copy-start.2
  26.7 0.0 collective-permute-done.rest_1_
  26.7 0.5 copy-done.1
  27.2 0.0 copy-done.2
  27.2 0.0 copy-done.3
  27.3 2.3 %pack_768.1 = bf16[32,144,128]{2,1,0:T(8,128)(2,1)} custom-call(s32[1,32]{1,0:T(1,128)} %slots_ref.3, bf16[64,16384]{1,0:T(8,128)(2,1)} %q_hbm.5, bf16[64,128]{1,0:T(8,128)(2,1)} %s_hbm.5, f32[8,128]{1,0:T(8,128)} %square_sum.1.rest_0_, f32[8,128]{1,0:T(8,128)} %copy-done.3, f32[8,128]{1,0:T(8,128)} %copy-done.2, f32[8,128]{1,0:T(8,128)} %copy-done.1), custom_call_target="tpu_custom_call" | custom-call | bytes 3276800 | tf_op jit(solution)/shard_map/pack_768/pallas_call | solution.py:120
  29.6 23.9 %all-to-all-done.1.a_hbm = bf16[32,400,128]{2,1,0:T(8,128)(2,1)} async-done(((bf16[32,400,128]{2,1,0:T(8,128)(2,1)}), bf16[32,400,128]{2,1,0:T(8,128)(2,1)}, u32[]{:S(2)}, u32[]{:S(2)}) %all-to-all-start.1) | async-done | bytes 3276832 | tf_op jit(solution)/shard_map/all_to_all | solution.py:486
  53.5 5.7 %all-to-all-start = ((bf16[32,144,128]{2,1,0:T(8,128)(2,1)}), bf16[32,144,128]{2,1,0:T(8,128)(2,1)}, u32[]{:S(2)}, u32[]{:S(2)}) async-start(bf16[32,144,128]{2,1,0:T(8,128)(2,1)} %pack_768.1), calls=%async_computation | async-start | bytes 2359296 | tf_op jit(solution)/shard_map/all_to_all | solution.py:486
  59.2 15.5 %products.1 = (f32[1024,1024]{1,0:T(8,128)}, f32[1024,768]{1,0:T(8,128)}) custom-call(s32[1,32]{1,0:T(1,128)} %slots_ref.3, bf16[32,400,128]{2,1,0:T(8,128)(2,1)} %all-to-all-done.1.a_hbm, bf16[1024,1024]{1,0:T(8,128)(2,1)} %get-tuple-element.26.l1_hbm, bf16[1024,1024]{1,0:T(8,128)(2,1)} %get-tuple-element.27.l2_hbm, ...), custom_call_target="tpu_custom_call" | custom-call | flops 9663676416 | bytes 20971520 | tf_op jit(solution)/shard_map/products/pallas_call | solution.py:285
  74.8 2.9 %all-to-all-done.a_hbm = bf16[32,144,128]{2,1,0:T(8,128)(2,1)} async-done(((bf16[32,144,128]{2,1,0:T(8,128)(2,1)}), bf16[32,144,128]{2,1,0:T(8,128)(2,1)}, u32[]{:S(2)}, u32[]{:S(2)}) %all-to-all-start) | async-done | bytes 1179680 | tf_op jit(solution)/shard_map/all_to_all | solution.py:486
  77.6 11.8 %graft.1 = (bf16[2048,1024]{1,0:T(8,128)(2,1)}, f32[1024,1024]{1,0:T(8,128)}) custom-call(s32[1,32]{1,0:T(1,128)} %slots_ref.3, bf16[32,144,128]{2,1,0:T(8,128)(2,1)} %all-to-all-done.a_hbm, bf16[1024,1024]{1,0:T(8,128)(2,1)} %get-tuple-element.26.l1_hbm, bf16[1024,1024]{1,0:T(8,128)(2,1)} %get-tuple-element.27.l2_hbm, ...), custom_call_target="tpu_custom_call" | custom-call | flops 3221225472 | bytes 25165824 | tf_op jit(solution)/shard_map/graft/pallas_call | solution.py:417
  89.4 0.0 copy-start
  89.4 55.2 %all_to_all.15.r_ref = bf16[32,64,1024]{2,1,0:T(8,128)(2,1)S(1)} all-to-all(bf16[32,64,1024]{2,1,0:T(8,128)(2,1)} %bitcast.7), channel_id=1, replica_groups=mesh['fsdp'=32,'grp'=4] {'fsdp'}, dimensions={0} | all-to-all | bytes 8388608 | tf_op jit(solution)/shard_map/all_to_all | solution.py:486
  144.6 2.0 %place.1 = bf16[64,16384]{1,0:T(8,128)(2,1)} custom-call(s32[1,32]{1,0:T(1,128)S(1)} %copy-done, bf16[32,64,1024]{2,1,0:T(8,128)(2,1)S(1)} %all_to_all.15.r_ref), custom_call_target="tpu_custom_call" | custom-call | bytes 4194304 | tf_op jit(solution)/shard_map/place/pallas_call | solution.py:465
  (2 shorter events, 0.0 us)
Async XLA Ops:
  3.7 49.8 %all-to-all-start.1 = ((bf16[32,400,128]{2,1,0:T(8,128)(2,1)}), bf16[32,400,128]{2,1,0:T(8,128)(2,1)}, u32[]{:S(2)}, u32[]{:S(2)}) async-start(bf16[32,400,128]{2,1,0:T(8,128)(2,1)} %pack_0.1), calls=%async_computation.1 | async-start | bytes 6553600 | tf_op jit(solution)/shard_map/all_to_all | solution.py:486
  15.5 11.1 %collective-permute-start.2 = (f32[8,128]{1,0:T(8,128)}, f32[8,128]{1,0:T(8,128)S(1)}, u32[]{:S(2)}, u32[]{:S(2)}) collective-permute-start(f32[8,128]{1,0:T(8,128)} %square_sum.1.rest_0_), channel_id=1, source_target_pairs={{0,3},{1,0},{2,1},{3,2},{4,7},{5,4},{6,5},{7,6},{8,11},{9,8},{10,9... | collective-permute-start | bytes 12296 | tf_op jit(solution)/shard_map/ppermute | solution.py:492
  19.3 7.3 %collective-permute-start.1 = (f32[8,128]{1,0:T(8,128)}, f32[8,128]{1,0:T(8,128)S(1)}, u32[]{:S(2)}, u32[]{:S(2)}) collective-permute-start(f32[8,128]{1,0:T(8,128)} %square_sum.1.rest_0_), channel_id=1, source_target_pairs={{0,2},{1,3},{2,0},{3,1},{4,6},{5,7},{6,4},{7,5},{8,10},{9,11},{10,... | collective-permute-start | bytes 12296 | tf_op jit(solution)/shard_map/ppermute | solution.py:492
  19.3 7.3 %collective-permute-start = (f32[8,128]{1,0:T(8,128)}, f32[8,128]{1,0:T(8,128)S(1)}, u32[]{:S(2)}, u32[]{:S(2)}) collective-permute-start(f32[8,128]{1,0:T(8,128)} %square_sum.1.rest_0_), channel_id=1, source_target_pairs={{0,1},{1,2},{2,3},{3,0},{4,5},{5,6},{6,7},{7,4},{8,9},{9,10},{10,1... | collective-permute-start | bytes 12296 | tf_op jit(solution)/shard_map/ppermute | solution.py:492
  26.6 0.6 copy-start.1
  26.7 0.6 copy-start.2
  26.7 0.6 copy-start.3
  53.5 24.1 %all-to-all-start = ((bf16[32,144,128]{2,1,0:T(8,128)(2,1)}), bf16[32,144,128]{2,1,0:T(8,128)(2,1)}, u32[]{:S(2)}, u32[]{:S(2)}) async-start(bf16[32,144,128]{2,1,0:T(8,128)(2,1)} %pack_768.1), calls=%async_computation | async-start | bytes 2359296 | tf_op jit(solution)/shard_map/all_to_all | solution.py:486
  89.4 55.2 %copy-start = (s32[1,32]{1,0:T(1,128)S(1)}, s32[1,32]{1,0:T(1,128)}, u32[]{:S(2)}) copy-start(s32[1,32]{1,0:T(1,128)} %slots_ref.3) | copy-start | bytes 388

commit v8 on v7

--- a/solution.py
+++ b/solution.py
@@ -85,6 +85,7 @@
         def _(k):
             q_read(k).start()
 
+        bands = range(owners // columns) if e_hbm else [lax.div(lax.axis_index("fsdp") * rows, width)]
         for read in reads:
             read.wait()
         invert(slots_ref, inverse)
@@ -108,12 +109,12 @@
             q_read(k).wait()
             for j in range(here):
                 out_ref[k, j * rows : (j + 1) * rows, :] = q_ref[k, :, j * LANES : (j + 1) * LANES]
-            for band in range(owners // columns):
+            for band in bands:
                 write(k, band).start()
 
         @pl.loop(0, columns)
         def _(k):
-            for band in range(owners // columns):
+            for band in bands:
                 write(k, band).wait()
 
     operands = [slots, q_values, scales, *sums_of]
@@ -386,8 +387,13 @@
             asum[...] += sum(steps)
             fresh_copy(n).start()
 
-        half = dot(l1_ref[...], h1[...]) + (dot(l1_ref[...], h2[...]) + dot(l2_ref[...], h1[...]))
-        t1[...], t2[...] = two(half)
+
+        @pl.loop(0, STEPS)
+        def _(n):
+            at = cut(n)
+            half = dot(l1_ref[at, :], h1[...]) + (dot(l1_ref[at, :], h2[...]) + dot(l2_ref[at, :], h1[...]))
+            t1[at, :], t2[at, :] = two(half)
+
         for read in reads[4:]:
             read.wait()
 

time: 147 us -> 147 us (level)
  no operation moved by 1% of the time
where the time goes in v8:
time: 147 us
  blocking collectives  55.2 us (38%)
  Pallas kernels  44.6 us (30%)
  waiting for transfers between devices  26.7 us (18%)
  starting transfers between devices  18.9 us (13%)
    all_to_all x1, blocking collectives, exchange(): lax.all_to_all(value, 'fsdp', split_axis=0, concat_axis=0, tiled=True)  55.2 us
    all_to_all x2, waiting for transfers between devices, exchange(): lax.all_to_all(value, 'fsdp', split_axis=0, concat_axis=0, tiled=True)  26.7 us
    pallas_call x1, Pallas kernels, products(): pl.pallas_call(body, out_shape=[jax.ShapeDtypeStruct(square, F32), jax.Sh...  15.5 us
    all_to_all x2, starting transfers between devices, exchange(): lax.all_to_all(value, 'fsdp', split_axis=0, concat_axis=0, tiled=True)  14.4 us
    pallas_call x1, Pallas kernels, graft(): pl.pallas_call(body, out_shape=[jax.ShapeDtypeStruct((owners * rows, size...  12.3 us
    pallas_call x1, Pallas kernels, split_roots(): pl.pallas_call(body, out_shape=[jax.ShapeDtypeStruct((size, size), BF16)]...  6.59 us
    pallas_call x2, Pallas kernels, pack(): pl.pallas_call(body, out_shape=jax.ShapeDtypeStruct((owners, tall, LANES)...  4.99 us
    ppermute x3, starting transfers between devices, on_device(): lax.ppermute(own, 'grp', [(i, (i + k) % planes) for i in range(planes)])  4.53 us
  transfers between devices with their start and end apart: 5, of which 2 were waited for; matrix products, arithmetic and copies ran while one was open for 0% of the time, Pallas kernels for 19%

profile of v8, /device:TPU:1, one launch (start us, length us, event | category | flops | bytes accessed | tf_op | source)
XLA Modules:
  0.0 146.7 jit_solution(16634498341275028719)
XLA Ops:
  0.6 2.6 %pack_0.1 = bf16[32,400,128]{2,1,0:T(8,128)(2,1)} custom-call(s32[1,32]{1,0:T(1,128)} %slots_ref.3, bf16[64,16384]{1,0:T(8,128)(2,1)} %q_hbm.5, bf16[64,128]{1,0:T(8,128)(2,1)} %s_hbm.5), custom_call_target="tpu_custom_call" | custom-call | bytes 5373952 | tf_op jit(solution)/shard_map/pack_0/pallas_call | solution.py:121
  3.3 8.6 %all-to-all-start.1 = ((bf16[32,400,128]{2,1,0:T(8,128)(2,1)}), bf16[32,400,128]{2,1,0:T(8,128)(2,1)}, u32[]{:S(2)}, u32[]{:S(2)}) async-start(bf16[32,400,128]{2,1,0:T(8,128)(2,1)} %pack_0.1), calls=%async_computation.1 | async-start | bytes 6553600 | tf_op jit(solution)/shard_map/all_to_all | solution.py:492
  11.9 3.1 %square_sum.1.rest_0_ = f32[8,128]{1,0:T(8,128)} custom-call(bf16[64,16384]{1,0:T(8,128)(2,1)} %q_hbm.5, bf16[64,128]{1,0:T(8,128)(2,1)} %s_hbm.5), custom_call_target="tpu_custom_call" | custom-call | flops 3145728 | bytes 2097152 | tf_op jit(solution)/shard_map/square_sum/pallas_call | solution.py:160
  15.1 3.8 %collective-permute-start.2 = (f32[8,128]{1,0:T(8,128)}, f32[8,128]{1,0:T(8,128)S(1)}, u32[]{:S(2)}, u32[]{:S(2)}) collective-permute-start(f32[8,128]{1,0:T(8,128)} %square_sum.1.rest_0_), channel_id=1, source_target_pairs={{0,3},{1,0},{2,1},{3,2},{4,7},{5,4},{6,5},{7,6},{8,11},{9,8},{10,9... | collective-permute-start | bytes 12296 | tf_op jit(solution)/shard_map/ppermute | solution.py:498
  18.9 0.0 collective-permute-start.1
  18.9 0.7 collective-permute-start
  19.6 6.6 %split_roots.1 = (bf16[1024,1024]{1,0:T(8,128)(2,1)}, bf16[1024,1024]{1,0:T(8,128)(2,1)}, bf16[1024,1024]{1,0:T(8,128)(2,1)}, bf16[1024,1024]{1,0:T(8,128)(2,1)}) custom-call(f32[1024,1024]{1,0:T(8,128)} %bitcast.5, f32[1024,1024]{1,0:T(8,128)} %bitcast.6), custom_call_target="tpu_custom_call" | custom-call | flops 4194304 | bytes 16777216 | tf_op jit(solution)/shard_map/split_roots/pallas_call | solution.py:196
  26.2 0.0 collective-permute-done.2.rest_3_
  26.2 0.0 copy-start.1
  26.2 0.0 collective-permute-done.1.rest_2_
  26.2 0.0 copy-start.2
  26.2 0.0 collective-permute-done.rest_1_
  26.2 0.5 copy-done.1
  26.8 0.0 copy-done.2
  26.8 0.0 copy-done.3
  26.8 2.4 %pack_768.1 = bf16[32,144,128]{2,1,0:T(8,128)(2,1)} custom-call(s32[1,32]{1,0:T(1,128)} %slots_ref.3, bf16[64,16384]{1,0:T(8,128)(2,1)} %q_hbm.5, bf16[64,128]{1,0:T(8,128)(2,1)} %s_hbm.5, f32[8,128]{1,0:T(8,128)} %square_sum.1.rest_0_, f32[8,128]{1,0:T(8,128)} %copy-done.3, f32[8,128]{1,0:T(8,128)} %copy-done.2, f32[8,128]{1,0:T(8,128)} %copy-done.1), custom_call_target="tpu_custom_call" | custom-call | bytes 3276800 | tf_op jit(solution)/shard_map/pack_768/pallas_call | solution.py:121
  29.2 23.9 %all-to-all-done.1.a_hbm = bf16[32,400,128]{2,1,0:T(8,128)(2,1)} async-done(((bf16[32,400,128]{2,1,0:T(8,128)(2,1)}), bf16[32,400,128]{2,1,0:T(8,128)(2,1)}, u32[]{:S(2)}, u32[]{:S(2)}) %all-to-all-start.1) | async-done | bytes 3276832 | tf_op jit(solution)/shard_map/all_to_all | solution.py:492
  53.1 5.7 %all-to-all-start = ((bf16[32,144,128]{2,1,0:T(8,128)(2,1)}), bf16[32,144,128]{2,1,0:T(8,128)(2,1)}, u32[]{:S(2)}, u32[]{:S(2)}) async-start(bf16[32,144,128]{2,1,0:T(8,128)(2,1)} %pack_768.1), calls=%async_computation | async-start | bytes 2359296 | tf_op jit(solution)/shard_map/all_to_all | solution.py:492
  58.8 15.5 %products.1 = (f32[1024,1024]{1,0:T(8,128)}, f32[1024,768]{1,0:T(8,128)}) custom-call(s32[1,32]{1,0:T(1,128)} %slots_ref.3, bf16[32,400,128]{2,1,0:T(8,128)(2,1)} %all-to-all-done.1.a_hbm, bf16[1024,1024]{1,0:T(8,128)(2,1)} %get-tuple-element.26.l1_hbm, bf16[1024,1024]{1,0:T(8,128)(2,1)} %get-tuple-element.27.l2_hbm, ...), custom_call_target="tpu_custom_call" | custom-call | flops 9663676416 | bytes 20971520 | tf_op jit(solution)/shard_map/products/pallas_call | solution.py:286
  74.3 2.9 %all-to-all-done.a_hbm = bf16[32,144,128]{2,1,0:T(8,128)(2,1)} async-done(((bf16[32,144,128]{2,1,0:T(8,128)(2,1)}), bf16[32,144,128]{2,1,0:T(8,128)(2,1)}, u32[]{:S(2)}, u32[]{:S(2)}) %all-to-all-start) | async-done | bytes 1179680 | tf_op jit(solution)/shard_map/all_to_all | solution.py:492
  77.2 12.3 %graft.1 = (bf16[2048,1024]{1,0:T(8,128)(2,1)}, f32[1024,1024]{1,0:T(8,128)}) custom-call(s32[1,32]{1,0:T(1,128)} %slots_ref.3, bf16[32,144,128]{2,1,0:T(8,128)(2,1)} %all-to-all-done.a_hbm, bf16[1024,1024]{1,0:T(8,128)(2,1)} %get-tuple-element.26.l1_hbm, bf16[1024,1024]{1,0:T(8,128)(2,1)} %get-tuple-element.27.l2_hbm, ...), custom_call_target="tpu_custom_call" | custom-call | flops 3221225472 | bytes 25165824 | tf_op jit(solution)/shard_map/graft/pallas_call | solution.py:423
  89.5 0.0 copy-start
  89.6 55.2 %all_to_all.15.r_ref = bf16[32,64,1024]{2,1,0:T(8,128)(2,1)S(1)} all-to-all(bf16[32,64,1024]{2,1,0:T(8,128)(2,1)} %bitcast.7), channel_id=1, replica_groups=mesh['fsdp'=32,'grp'=4] {'fsdp'}, dimensions={0} | all-to-all | bytes 8388608 | tf_op jit(solution)/shard_map/all_to_all | solution.py:492
  144.7 2.0 %place.1 = bf16[64,16384]{1,0:T(8,128)(2,1)} custom-call(s32[1,32]{1,0:T(1,128)S(1)} %copy-done, bf16[32,64,1024]{2,1,0:T(8,128)(2,1)S(1)} %all_to_all.15.r_ref), custom_call_target="tpu_custom_call" | custom-call | bytes 4194304 | tf_op jit(solution)/shard_map/place/pallas_call | solution.py:471
  (2 shorter events, 0.0 us)
Async XLA Ops:
  3.3 49.8 %all-to-all-start.1 = ((bf16[32,400,128]{2,1,0:T(8,128)(2,1)}), bf16[32,400,128]{2,1,0:T(8,128)(2,1)}, u32[]{:S(2)}, u32[]{:S(2)}) async-start(bf16[32,400,128]{2,1,0:T(8,128)(2,1)} %pack_0.1), calls=%async_computation.1 | async-start | bytes 6553600 | tf_op jit(solution)/shard_map/all_to_all | solution.py:492
  15.1 11.1 %collective-permute-start.2 = (f32[8,128]{1,0:T(8,128)}, f32[8,128]{1,0:T(8,128)S(1)}, u32[]{:S(2)}, u32[]{:S(2)}) collective-permute-start(f32[8,128]{1,0:T(8,128)} %square_sum.1.rest_0_), channel_id=1, source_target_pairs={{0,3},{1,0},{2,1},{3,2},{4,7},{5,4},{6,5},{7,6},{8,11},{9,8},{10,9... | collective-permute-start | bytes 12296 | tf_op jit(solution)/shard_map/ppermute | solution.py:498
  18.9 7.3 %collective-permute-start.1 = (f32[8,128]{1,0:T(8,128)}, f32[8,128]{1,0:T(8,128)S(1)}, u32[]{:S(2)}, u32[]{:S(2)}) collective-permute-start(f32[8,128]{1,0:T(8,128)} %square_sum.1.rest_0_), channel_id=1, source_target_pairs={{0,2},{1,3},{2,0},{3,1},{4,6},{5,7},{6,4},{7,5},{8,10},{9,11},{10,... | collective-permute-start | bytes 12296 | tf_op jit(solution)/shard_map/ppermute | solution.py:498
  18.9 7.3 %collective-permute-start = (f32[8,128]{1,0:T(8,128)}, f32[8,128]{1,0:T(8,128)S(1)}, u32[]{:S(2)}, u32[]{:S(2)}) collective-permute-start(f32[8,128]{1,0:T(8,128)} %square_sum.1.rest_0_), channel_id=1, source_target_pairs={{0,1},{1,2},{2,3},{3,0},{4,5},{5,6},{6,7},{7,4},{8,9},{9,10},{10,1... | collective-permute-start | bytes 12296 | tf_op jit(solution)/shard_map/ppermute | solution.py:498
  26.2 0.6 copy-start.1
  26.2 0.6 copy-start.2
  26.2 0.6 copy-start.3
  53.1 24.1 %all-to-all-start = ((bf16[32,144,128]{2,1,0:T(8,128)(2,1)}), bf16[32,144,128]{2,1,0:T(8,128)(2,1)}, u32[]{:S(2)}, u32[]{:S(2)}) async-start(bf16[32,144,128]{2,1,0:T(8,128)(2,1)} %pack_768.1), calls=%async_computation | async-start | bytes 2359296 | tf_op jit(solution)/shard_map/all_to_all | solution.py:492
  89.5 55.2 %copy-start = (s32[1,32]{1,0:T(1,128)S(1)}, s32[1,32]{1,0:T(1,128)}, u32[]{:S(2)}) copy-start(s32[1,32]{1,0:T(1,128)} %slots_ref.3) | copy-start | bytes 388

commit v9 on v8

--- a/solution.py
+++ b/solution.py
@@ -338,14 +338,14 @@
             pairs = ((grad_hbm.at[at], grad_ref.at[at, pl.ds(0, done)]), (m_hbm.at[at], m_ref.at[at]))
             return [pltpu.make_async_copy(s, t, ins.at[1 + k, n]) for k, (s, t) in enumerate(pairs)]
 
-        for read in reads[:4]:
+        for read in reads[:3]:
             read.start()
         for read in reads[:2]:
             read.wait()
         band = own_band(slots_ref, columns)
         base = band * pieces
 
-        for read in reads[4:]:
+        for read in reads[3:]:
             read.start()
 
         @pl.loop(0, STEPS)
@@ -360,8 +360,7 @@
         clip = jnp.where(total > 0, jnp.minimum(bound, 1.0), 1.0)
         asum[...] = jnp.zeros_like(asum)
         psum[...] = jnp.zeros_like(psum)
-        for read in reads[2:4]:
-            read.wait()
+        reads[2].wait()
 
         def fresh_copy(n):
             return pltpu.make_async_copy(m_ref.at[cut(n)], fresh_hbm.at[cut(n)], outs.at[0, n])
@@ -387,13 +386,9 @@
             asum[...] += sum(steps)
             fresh_copy(n).start()
 
-
-        @pl.loop(0, STEPS)
-        def _(n):
-            at = cut(n)
-            half = dot(l1_ref[at, :], h1[...]) + (dot(l1_ref[at, :], h2[...]) + dot(l2_ref[at, :], h1[...]))
-            t1[at, :], t2[at, :] = two(half)
-
+        half = dot(l1_ref[...], h1[...]) + dot(l1_ref[...], h2[...])
+        reads[3].wait()
+        t1[...], t2[...] = two(half + dot(l2_ref[...], h1[...]))
         for read in reads[4:]:
             read.wait()
 

time: 147 us -> 147 us (level)
  no operation moved by 1% of the time
where the time goes in v9:
time: 147 us
  blocking collectives  55.1 us (37%)
  Pallas kernels  44.6 us (30%)
  waiting for transfers between devices  26.7 us (18%)
  starting transfers between devices  18.9 us (13%)
    all_to_all x1, blocking collectives, exchange(): lax.all_to_all(value, 'fsdp', split_axis=0, concat_axis=0, tiled=True)  55.1 us
    all_to_all x2, waiting for transfers between devices, exchange(): lax.all_to_all(value, 'fsdp', split_axis=0, concat_axis=0, tiled=True)  26.7 us
    pallas_call x1, Pallas kernels, products(): pl.pallas_call(body, out_shape=[jax.ShapeDtypeStruct(square, F32), jax.Sh...  15.5 us
    all_to_all x2, starting transfers between devices, exchange(): lax.all_to_all(value, 'fsdp', split_axis=0, concat_axis=0, tiled=True)  14.4 us
    pallas_call x1, Pallas kernels, graft(): pl.pallas_call(body, out_shape=[jax.ShapeDtypeStruct((owners * rows, size...  12.4 us
    pallas_call x1, Pallas kernels, split_roots(): pl.pallas_call(body, out_shape=[jax.ShapeDtypeStruct((size, size), BF16)]...  6.59 us
    pallas_call x2, Pallas kernels, pack(): pl.pallas_call(body, out_shape=jax.ShapeDtypeStruct((owners, tall, LANES)...  4.98 us
    ppermute x3, starting transfers between devices, on_device(): lax.ppermute(own, 'grp', [(i, (i + k) % planes) for i in range(planes)])  4.53 us
  transfers between devices with their start and end apart: 5, of which 2 were waited for; matrix products, arithmetic and copies ran while one was open for 0% of the time, Pallas kernels for 19%

profile of v9, /device:TPU:1, one launch (start us, length us, event | category | flops | bytes accessed | tf_op | source)
XLA Modules:
  0.0 146.8 jit_solution(7241172300506995089)
XLA Ops:
  0.6 2.6 %pack_0.1 = bf16[32,400,128]{2,1,0:T(8,128)(2,1)} custom-call(s32[1,32]{1,0:T(1,128)} %slots_ref.3, bf16[64,16384]{1,0:T(8,128)(2,1)} %q_hbm.5, bf16[64,128]{1,0:T(8,128)(2,1)} %s_hbm.5), custom_call_target="tpu_custom_call" | custom-call | bytes 5373952 | tf_op jit(solution)/shard_map/pack_0/pallas_call | solution.py:121
  3.3 8.6 %all-to-all-start.1 = ((bf16[32,400,128]{2,1,0:T(8,128)(2,1)}), bf16[32,400,128]{2,1,0:T(8,128)(2,1)}, u32[]{:S(2)}, u32[]{:S(2)}) async-start(bf16[32,400,128]{2,1,0:T(8,128)(2,1)} %pack_0.1), calls=%async_computation.1 | async-start | bytes 6553600 | tf_op jit(solution)/shard_map/all_to_all | solution.py:487
  11.9 3.1 %square_sum.1.rest_0_ = f32[8,128]{1,0:T(8,128)} custom-call(bf16[64,16384]{1,0:T(8,128)(2,1)} %q_hbm.5, bf16[64,128]{1,0:T(8,128)(2,1)} %s_hbm.5), custom_call_target="tpu_custom_call" | custom-call | flops 3145728 | bytes 2097152 | tf_op jit(solution)/shard_map/square_sum/pallas_call | solution.py:160
  15.1 3.8 %collective-permute-start.2 = (f32[8,128]{1,0:T(8,128)}, f32[8,128]{1,0:T(8,128)S(1)}, u32[]{:S(2)}, u32[]{:S(2)}) collective-permute-start(f32[8,128]{1,0:T(8,128)} %square_sum.1.rest_0_), channel_id=1, source_target_pairs={{0,3},{1,0},{2,1},{3,2},{4,7},{5,4},{6,5},{7,6},{8,11},{9,8},{10,9... | collective-permute-start | bytes 12296 | tf_op jit(solution)/shard_map/ppermute | solution.py:493
  18.9 0.0 collective-permute-start.1
  18.9 0.7 collective-permute-start
  19.6 6.6 %split_roots.1 = (bf16[1024,1024]{1,0:T(8,128)(2,1)}, bf16[1024,1024]{1,0:T(8,128)(2,1)}, bf16[1024,1024]{1,0:T(8,128)(2,1)}, bf16[1024,1024]{1,0:T(8,128)(2,1)}) custom-call(f32[1024,1024]{1,0:T(8,128)} %bitcast.5, f32[1024,1024]{1,0:T(8,128)} %bitcast.6), custom_call_target="tpu_custom_call" | custom-call | flops 4194304 | bytes 16777216 | tf_op jit(solution)/shard_map/split_roots/pallas_call | solution.py:196
  26.2 0.0 collective-permute-done.2.rest_3_
  26.2 0.0 copy-start.1
  26.2 0.0 collective-permute-done.1.rest_2_
  26.2 0.0 collective-permute-done.rest_1_
  26.2 0.5 copy-done.1
  26.8 0.0 copy-done.2
  26.8 0.0 copy-done.3
  26.8 2.4 %pack_768.1 = bf16[32,144,128]{2,1,0:T(8,128)(2,1)} custom-call(s32[1,32]{1,0:T(1,128)} %slots_ref.3, bf16[64,16384]{1,0:T(8,128)(2,1)} %q_hbm.5, bf16[64,128]{1,0:T(8,128)(2,1)} %s_hbm.5, f32[8,128]{1,0:T(8,128)} %square_sum.1.rest_0_, f32[8,128]{1,0:T(8,128)} %copy-done.3, f32[8,128]{1,0:T(8,128)} %copy-done.2, f32[8,128]{1,0:T(8,128)} %copy-done.1), custom_call_target="tpu_custom_call" | custom-call | bytes 3276800 | tf_op jit(solution)/shard_map/pack_768/pallas_call | solution.py:121
  29.2 23.9 %all-to-all-done.1.a_hbm = bf16[32,400,128]{2,1,0:T(8,128)(2,1)} async-done(((bf16[32,400,128]{2,1,0:T(8,128)(2,1)}), bf16[32,400,128]{2,1,0:T(8,128)(2,1)}, u32[]{:S(2)}, u32[]{:S(2)}) %all-to-all-start.1) | async-done | bytes 3276832 | tf_op jit(solution)/shard_map/all_to_all | solution.py:487
  53.1 5.7 %all-to-all-start = ((bf16[32,144,128]{2,1,0:T(8,128)(2,1)}), bf16[32,144,128]{2,1,0:T(8,128)(2,1)}, u32[]{:S(2)}, u32[]{:S(2)}) async-start(bf16[32,144,128]{2,1,0:T(8,128)(2,1)} %pack_768.1), calls=%async_computation | async-start | bytes 2359296 | tf_op jit(solution)/shard_map/all_to_all | solution.py:487
  58.8 15.5 %products.1 = (f32[1024,1024]{1,0:T(8,128)}, f32[1024,768]{1,0:T(8,128)}) custom-call(s32[1,32]{1,0:T(1,128)} %slots_ref.3, bf16[32,400,128]{2,1,0:T(8,128)(2,1)} %all-to-all-done.1.a_hbm, bf16[1024,1024]{1,0:T(8,128)(2,1)} %get-tuple-element.26.l1_hbm, bf16[1024,1024]{1,0:T(8,128)(2,1)} %get-tuple-element.27.l2_hbm, ...), custom_call_target="tpu_custom_call" | custom-call | flops 9663676416 | bytes 20971520 | tf_op jit(solution)/shard_map/products/pallas_call | solution.py:286
  74.3 2.9 %all-to-all-done.a_hbm = bf16[32,144,128]{2,1,0:T(8,128)(2,1)} async-done(((bf16[32,144,128]{2,1,0:T(8,128)(2,1)}), bf16[32,144,128]{2,1,0:T(8,128)(2,1)}, u32[]{:S(2)}, u32[]{:S(2)}) %all-to-all-start) | async-done | bytes 1179680 | tf_op jit(solution)/shard_map/all_to_all | solution.py:487
  77.2 12.4 %graft.1 = (bf16[2048,1024]{1,0:T(8,128)(2,1)}, f32[1024,1024]{1,0:T(8,128)}) custom-call(s32[1,32]{1,0:T(1,128)} %slots_ref.3, bf16[32,144,128]{2,1,0:T(8,128)(2,1)} %all-to-all-done.a_hbm, bf16[1024,1024]{1,0:T(8,128)(2,1)} %get-tuple-element.26.l1_hbm, bf16[1024,1024]{1,0:T(8,128)(2,1)} %get-tuple-element.27.l2_hbm, ...), custom_call_target="tpu_custom_call" | custom-call | flops 3221225472 | bytes 25165824 | tf_op jit(solution)/shard_map/graft/pallas_call | solution.py:418
  89.6 0.0 copy-start
  89.6 55.1 %all_to_all.15.r_ref = bf16[32,64,1024]{2,1,0:T(8,128)(2,1)S(1)} all-to-all(bf16[32,64,1024]{2,1,0:T(8,128)(2,1)} %bitcast.7), channel_id=1, replica_groups=mesh['fsdp'=32,'grp'=4] {'fsdp'}, dimensions={0} | all-to-all | bytes 8388608 | tf_op jit(solution)/shard_map/all_to_all | solution.py:487
  144.8 0.0 copy-done
  144.8 2.0 %place.1 = bf16[64,16384]{1,0:T(8,128)(2,1)} custom-call(s32[1,32]{1,0:T(1,128)S(1)} %copy-done, bf16[32,64,1024]{2,1,0:T(8,128)(2,1)S(1)} %all_to_all.15.r_ref), custom_call_target="tpu_custom_call" | custom-call | bytes 4194304 | tf_op jit(solution)/shard_map/place/pallas_call | solution.py:466
  (2 shorter events, 0.0 us)
Async XLA Ops:
  3.3 49.8 %all-to-all-start.1 = ((bf16[32,400,128]{2,1,0:T(8,128)(2,1)}), bf16[32,400,128]{2,1,0:T(8,128)(2,1)}, u32[]{:S(2)}, u32[]{:S(2)}) async-start(bf16[32,400,128]{2,1,0:T(8,128)(2,1)} %pack_0.1), calls=%async_computation.1 | async-start | bytes 6553600 | tf_op jit(solution)/shard_map/all_to_all | solution.py:487
  15.1 11.1 %collective-permute-start.2 = (f32[8,128]{1,0:T(8,128)}, f32[8,128]{1,0:T(8,128)S(1)}, u32[]{:S(2)}, u32[]{:S(2)}) collective-permute-start(f32[8,128]{1,0:T(8,128)} %square_sum.1.rest_0_), channel_id=1, source_target_pairs={{0,3},{1,0},{2,1},{3,2},{4,7},{5,4},{6,5},{7,6},{8,11},{9,8},{10,9... | collective-permute-start | bytes 12296 | tf_op jit(solution)/shard_map/ppermute | solution.py:493
  18.9 7.3 %collective-permute-start.1 = (f32[8,128]{1,0:T(8,128)}, f32[8,128]{1,0:T(8,128)S(1)}, u32[]{:S(2)}, u32[]{:S(2)}) collective-permute-start(f32[8,128]{1,0:T(8,128)} %square_sum.1.rest_0_), channel_id=1, source_target_pairs={{0,2},{1,3},{2,0},{3,1},{4,6},{5,7},{6,4},{7,5},{8,10},{9,11},{10,... | collective-permute-start | bytes 12296 | tf_op jit(solution)/shard_map/ppermute | solution.py:493
  18.9 7.3 %collective-permute-start = (f32[8,128]{1,0:T(8,128)}, f32[8,128]{1,0:T(8,128)S(1)}, u32[]{:S(2)}, u32[]{:S(2)}) collective-permute-start(f32[8,128]{1,0:T(8,128)} %square_sum.1.rest_0_), channel_id=1, source_target_pairs={{0,1},{1,2},{2,3},{3,0},{4,5},{5,6},{6,7},{7,4},{8,9},{9,10},{10,1... | collective-permute-start | bytes 12296 | tf_op jit(solution)/shard_map/ppermute | solution.py:493
  26.2 0.6 copy-start.1
  26.2 0.6 copy-start.2
  26.2 0.6 copy-start.3
  53.1 24.1 %all-to-all-start = ((bf16[32,144,128]{2,1,0:T(8,128)(2,1)}), bf16[32,144,128]{2,1,0:T(8,128)(2,1)}, u32[]{:S(2)}, u32[]{:S(2)}) async-start(bf16[32,144,128]{2,1,0:T(8,128)(2,1)} %pack_768.1), calls=%async_computation | async-start | bytes 2359296 | tf_op jit(solution)/shard_map/all_to_all | solution.py:487
  89.6 55.2 %copy-start = (s32[1,32]{1,0:T(1,128)S(1)}, s32[1,32]{1,0:T(1,128)}, u32[]{:S(2)}) copy-start(s32[1,32]{1,0:T(1,128)} %slots_ref.3) | copy-start | bytes 388

commit v10 on v7

--- a/solution.py
+++ b/solution.py
@@ -85,6 +85,7 @@
         def _(k):
             q_read(k).start()
 
+        bands = range(owners // columns) if e_hbm else [lax.div(lax.axis_index("fsdp") * rows, width)]
         for read in reads:
             read.wait()
         invert(slots_ref, inverse)
@@ -108,12 +109,12 @@
             q_read(k).wait()
             for j in range(here):
                 out_ref[k, j * rows : (j + 1) * rows, :] = q_ref[k, :, j * LANES : (j + 1) * LANES]
-            for band in range(owners // columns):
+            for band in bands:
                 write(k, band).start()
 
         @pl.loop(0, columns)
         def _(k):
-            for band in range(owners // columns):
+            for band in bands:
                 write(k, band).wait()
 
     operands = [slots, q_values, scales, *sums_of]

time: 147 us -> 147 us (level)
  no operation moved by 1% of the time
where the time goes in v10:
time: 147 us; the launch traced here: 146 us
  blocking collectives  55.2 us (38%)
  Pallas kernels  44.1 us (30%)
  waiting for transfers between devices  26.7 us (18%)
  starting transfers between devices  18.9 us (13%)
    all_to_all x1, blocking collectives, exchange(): lax.all_to_all(value, 'fsdp', split_axis=0, concat_axis=0, tiled=True)  55.2 us
    all_to_all x2, waiting for transfers between devices, exchange(): lax.all_to_all(value, 'fsdp', split_axis=0, concat_axis=0, tiled=True)  26.7 us
    pallas_call x1, Pallas kernels, products(): pl.pallas_call(body, out_shape=[jax.ShapeDtypeStruct(square, F32), jax.Sh...  15.5 us
    all_to_all x2, starting transfers between devices, exchange(): lax.all_to_all(value, 'fsdp', split_axis=0, concat_axis=0, tiled=True)  14.4 us
    pallas_call x1, Pallas kernels, graft(): pl.pallas_call(body, out_shape=[jax.ShapeDtypeStruct((owners * rows, size...  11.8 us
    pallas_call x1, Pallas kernels, split_roots(): pl.pallas_call(body, out_shape=[jax.ShapeDtypeStruct((size, size), BF16)]...  6.59 us
    pallas_call x2, Pallas kernels, pack(): pl.pallas_call(body, out_shape=jax.ShapeDtypeStruct((owners, tall, LANES)...  4.99 us
    ppermute x3, starting transfers between devices, on_device(): lax.ppermute(own, 'grp', [(i, (i + k) % planes) for i in range(planes)])  4.53 us
  transfers between devices with their start and end apart: 5, of which 2 were waited for; matrix products, arithmetic and copies ran while one was open for 0% of the time, Pallas kernels for 19%

profile of v10, /device:TPU:1, one launch (start us, length us, event | category | flops | bytes accessed | tf_op | source)
XLA Modules:
  0.0 146.2 jit_solution(12087829842585947413)
XLA Ops:
  0.6 2.6 %pack_0.1 = bf16[32,400,128]{2,1,0:T(8,128)(2,1)} custom-call(s32[1,32]{1,0:T(1,128)} %slots_ref.3, bf16[64,16384]{1,0:T(8,128)(2,1)} %q_hbm.5, bf16[64,128]{1,0:T(8,128)(2,1)} %s_hbm.5), custom_call_target="tpu_custom_call" | custom-call | bytes 5373952 | tf_op jit(solution)/shard_map/pack_0/pallas_call | solution.py:121
  3.3 8.6 %all-to-all-start.1 = ((bf16[32,400,128]{2,1,0:T(8,128)(2,1)}), bf16[32,400,128]{2,1,0:T(8,128)(2,1)}, u32[]{:S(2)}, u32[]{:S(2)}) async-start(bf16[32,400,128]{2,1,0:T(8,128)(2,1)} %pack_0.1), calls=%async_computation.1 | async-start | bytes 6553600 | tf_op jit(solution)/shard_map/all_to_all | solution.py:487
  11.9 3.1 %square_sum.1.rest_0_ = f32[8,128]{1,0:T(8,128)} custom-call(bf16[64,16384]{1,0:T(8,128)(2,1)} %q_hbm.5, bf16[64,128]{1,0:T(8,128)(2,1)} %s_hbm.5), custom_call_target="tpu_custom_call" | custom-call | flops 3145728 | bytes 2097152 | tf_op jit(solution)/shard_map/square_sum/pallas_call | solution.py:160
  15.1 3.8 %collective-permute-start.2 = (f32[8,128]{1,0:T(8,128)}, f32[8,128]{1,0:T(8,128)S(1)}, u32[]{:S(2)}, u32[]{:S(2)}) collective-permute-start(f32[8,128]{1,0:T(8,128)} %square_sum.1.rest_0_), channel_id=1, source_target_pairs={{0,3},{1,0},{2,1},{3,2},{4,7},{5,4},{6,5},{7,6},{8,11},{9,8},{10,9... | collective-permute-start | bytes 12296 | tf_op jit(solution)/shard_map/ppermute | solution.py:493
  18.9 0.0 collective-permute-start.1
  18.9 0.7 collective-permute-start
  19.6 6.6 %split_roots.1 = (bf16[1024,1024]{1,0:T(8,128)(2,1)}, bf16[1024,1024]{1,0:T(8,128)(2,1)}, bf16[1024,1024]{1,0:T(8,128)(2,1)}, bf16[1024,1024]{1,0:T(8,128)(2,1)}) custom-call(f32[1024,1024]{1,0:T(8,128)} %bitcast.5, f32[1024,1024]{1,0:T(8,128)} %bitcast.6), custom_call_target="tpu_custom_call" | custom-call | flops 4194304 | bytes 16777216 | tf_op jit(solution)/shard_map/split_roots/pallas_call | solution.py:196
  26.2 0.0 collective-permute-done.2.rest_3_
  26.2 0.0 collective-permute-done.1.rest_2_
  26.2 0.0 collective-permute-done.rest_1_
  26.2 0.0 copy-start.3
  26.2 0.5 copy-done.1
  26.8 0.0 copy-done.2
  26.8 0.0 copy-done.3
  26.8 2.4 %pack_768.1 = bf16[32,144,128]{2,1,0:T(8,128)(2,1)} custom-call(s32[1,32]{1,0:T(1,128)} %slots_ref.3, bf16[64,16384]{1,0:T(8,128)(2,1)} %q_hbm.5, bf16[64,128]{1,0:T(8,128)(2,1)} %s_hbm.5, f32[8,128]{1,0:T(8,128)} %square_sum.1.rest_0_, f32[8,128]{1,0:T(8,128)} %copy-done.3, f32[8,128]{1,0:T(8,128)} %copy-done.2, f32[8,128]{1,0:T(8,128)} %copy-done.1), custom_call_target="tpu_custom_call" | custom-call | bytes 3276800 | tf_op jit(solution)/shard_map/pack_768/pallas_call | solution.py:121
  29.2 23.9 %all-to-all-done.1.a_hbm = bf16[32,400,128]{2,1,0:T(8,128)(2,1)} async-done(((bf16[32,400,128]{2,1,0:T(8,128)(2,1)}), bf16[32,400,128]{2,1,0:T(8,128)(2,1)}, u32[]{:S(2)}, u32[]{:S(2)}) %all-to-all-start.1) | async-done | bytes 3276832 | tf_op jit(solution)/shard_map/all_to_all | solution.py:487
  53.1 5.7 %all-to-all-start = ((bf16[32,144,128]{2,1,0:T(8,128)(2,1)}), bf16[32,144,128]{2,1,0:T(8,128)(2,1)}, u32[]{:S(2)}, u32[]{:S(2)}) async-start(bf16[32,144,128]{2,1,0:T(8,128)(2,1)} %pack_768.1), calls=%async_computation | async-start | bytes 2359296 | tf_op jit(solution)/shard_map/all_to_all | solution.py:487
  58.8 15.5 %products.1 = (f32[1024,1024]{1,0:T(8,128)}, f32[1024,768]{1,0:T(8,128)}) custom-call(s32[1,32]{1,0:T(1,128)} %slots_ref.3, bf16[32,400,128]{2,1,0:T(8,128)(2,1)} %all-to-all-done.1.a_hbm, bf16[1024,1024]{1,0:T(8,128)(2,1)} %get-tuple-element.26.l1_hbm, bf16[1024,1024]{1,0:T(8,128)(2,1)} %get-tuple-element.27.l2_hbm, ...), custom_call_target="tpu_custom_call" | custom-call | flops 9663676416 | bytes 20971520 | tf_op jit(solution)/shard_map/products/pallas_call | solution.py:286
  74.3 2.9 %all-to-all-done.a_hbm = bf16[32,144,128]{2,1,0:T(8,128)(2,1)} async-done(((bf16[32,144,128]{2,1,0:T(8,128)(2,1)}), bf16[32,144,128]{2,1,0:T(8,128)(2,1)}, u32[]{:S(2)}, u32[]{:S(2)}) %all-to-all-start) | async-done | bytes 1179680 | tf_op jit(solution)/shard_map/all_to_all | solution.py:487
  77.2 11.8 %graft.1 = (bf16[2048,1024]{1,0:T(8,128)(2,1)}, f32[1024,1024]{1,0:T(8,128)}) custom-call(s32[1,32]{1,0:T(1,128)} %slots_ref.3, bf16[32,144,128]{2,1,0:T(8,128)(2,1)} %all-to-all-done.a_hbm, bf16[1024,1024]{1,0:T(8,128)(2,1)} %get-tuple-element.26.l1_hbm, bf16[1024,1024]{1,0:T(8,128)(2,1)} %get-tuple-element.27.l2_hbm, ...), custom_call_target="tpu_custom_call" | custom-call | flops 3221225472 | bytes 25165824 | tf_op jit(solution)/shard_map/graft/pallas_call | solution.py:418
  89.0 0.0 copy-start
  89.0 55.2 %all_to_all.15.r_ref = bf16[32,64,1024]{2,1,0:T(8,128)(2,1)S(1)} all-to-all(bf16[32,64,1024]{2,1,0:T(8,128)(2,1)} %bitcast.7), channel_id=1, replica_groups=mesh['fsdp'=32,'grp'=4] {'fsdp'}, dimensions={0} | all-to-all | bytes 8388608 | tf_op jit(solution)/shard_map/all_to_all | solution.py:487
  144.2 0.0 copy-done
  144.2 2.0 %place.1 = bf16[64,16384]{1,0:T(8,128)(2,1)} custom-call(s32[1,32]{1,0:T(1,128)S(1)} %copy-done, bf16[32,64,1024]{2,1,0:T(8,128)(2,1)S(1)} %all_to_all.15.r_ref), custom_call_target="tpu_custom_call" | custom-call | bytes 4194304 | tf_op jit(solution)/shard_map/place/pallas_call | solution.py:466
  (2 shorter events, 0.0 us)
Async XLA Ops:
  3.3 49.8 %all-to-all-start.1 = ((bf16[32,400,128]{2,1,0:T(8,128)(2,1)}), bf16[32,400,128]{2,1,0:T(8,128)(2,1)}, u32[]{:S(2)}, u32[]{:S(2)}) async-start(bf16[32,400,128]{2,1,0:T(8,128)(2,1)} %pack_0.1), calls=%async_computation.1 | async-start | bytes 6553600 | tf_op jit(solution)/shard_map/all_to_all | solution.py:487
  15.1 11.1 %collective-permute-start.2 = (f32[8,128]{1,0:T(8,128)}, f32[8,128]{1,0:T(8,128)S(1)}, u32[]{:S(2)}, u32[]{:S(2)}) collective-permute-start(f32[8,128]{1,0:T(8,128)} %square_sum.1.rest_0_), channel_id=1, source_target_pairs={{0,3},{1,0},{2,1},{3,2},{4,7},{5,4},{6,5},{7,6},{8,11},{9,8},{10,9... | collective-permute-start | bytes 12296 | tf_op jit(solution)/shard_map/ppermute | solution.py:493
  18.9 7.3 %collective-permute-start.1 = (f32[8,128]{1,0:T(8,128)}, f32[8,128]{1,0:T(8,128)S(1)}, u32[]{:S(2)}, u32[]{:S(2)}) collective-permute-start(f32[8,128]{1,0:T(8,128)} %square_sum.1.rest_0_), channel_id=1, source_target_pairs={{0,2},{1,3},{2,0},{3,1},{4,6},{5,7},{6,4},{7,5},{8,10},{9,11},{10,... | collective-permute-start | bytes 12296 | tf_op jit(solution)/shard_map/ppermute | solution.py:493
  18.9 7.3 %collective-permute-start = (f32[8,128]{1,0:T(8,128)}, f32[8,128]{1,0:T(8,128)S(1)}, u32[]{:S(2)}, u32[]{:S(2)}) collective-permute-start(f32[8,128]{1,0:T(8,128)} %square_sum.1.rest_0_), channel_id=1, source_target_pairs={{0,1},{1,2},{2,3},{3,0},{4,5},{5,6},{6,7},{7,4},{8,9},{9,10},{10,1... | collective-permute-start | bytes 12296 | tf_op jit(solution)/shard_map/ppermute | solution.py:493
  26.2 0.6 copy-start.1
  26.2 0.6 copy-start.2
  26.2 0.6 copy-start.3
  53.1 24.1 %all-to-all-start = ((bf16[32,144,128]{2,1,0:T(8,128)(2,1)}), bf16[32,144,128]{2,1,0:T(8,128)(2,1)}, u32[]{:S(2)}, u32[]{:S(2)}) async-start(bf16[32,144,128]{2,1,0:T(8,128)(2,1)} %pack_768.1), calls=%async_computation | async-start | bytes 2359296 | tf_op jit(solution)/shard_map/all_to_all | solution.py:487
  89.0 55.2 %copy-start = (s32[1,32]{1,0:T(1,128)S(1)}, s32[1,32]{1,0:T(1,128)}, u32[]{:S(2)}) copy-start(s32[1,32]{1,0:T(1,128)} %slots_ref.3) | copy-start | bytes 388
